TPU v7x, 32 devices: a whole 2x2x4 slice. The times are simulated.
32 devices in a mesh: dp: 4 (over y, x), seq: 8 (over z, core).
Axes of the slice: x: 2, y: 2, z: 4, core: 2. Of those that a mesh axis runs over, the one named last changes fastest.
Arguments:
- tokens: bfloat16 [16, 1024, 1536], P('dp', 'seq'), may hold values from -6 to 6
- conv_state: bfloat16 [16, 3, 3072], P('dp'), may hold values from -6 to 6
- entry_state: float32 [16, 16, 3072], P('dp'), may hold values from -4 to 4
- norm_gain: float32 [1536], replicated, may hold values from 0.5 to 1.5
- in_proj: bfloat16 [1536, 6144], replicated, may hold values from -0.15625 to 0.15625
- conv_weight: float32 [4, 3072], replicated, may hold values from -3 to 3
- conv_bias: float32 [3072], replicated, may hold values from -2 to 2
- x_proj: bfloat16 [3072, 128], replicated, may hold values from -0.109375 to 0.109375
- dt_proj: bfloat16 [96, 3072], replicated, may hold values from -0.625 to 0.625
- dt_bias: float32 [3072], replicated, may hold values from -7 to -2.3
- a_log: float32 [16, 3072], replicated, may hold values from -5.8 to 1.1
- d_skip: float32 [3072], replicated, may hold values from 0.5 to 1.5
- out_proj: bfloat16 [3072, 1536], replicated, may hold values from -0.109375 to 0.109375
- cotangent: bfloat16 [16, 1024, 1536], P('dp', 'seq'), may hold values from -6 to 6
Outputs:
- output: float32 [16, 1024, 1536], P('dp', 'seq')
- d_tokens: float32 [16, 1024, 1536], P('dp', 'seq')
- d_conv_state: float32 [16, 3, 3072], P('dp')
- d_entry_state: float32 [16, 16, 3072], P('dp')
- d_norm_gain: float32 [1536], P('seq')
- d_in_proj: float32 [1536, 6144], P(None, 'seq')
- d_conv_weight: float32 [4, 3072], P(None, 'seq')
- d_conv_bias: float32 [3072], P('seq')
- d_x_proj: float32 [3072, 128], P('seq')
- d_dt_proj: float32 [96, 3072], P(None, 'seq')
- d_dt_bias: float32 [3072], P('seq')
- d_a_log: float32 [16, 3072], P(None, 'seq')
- d_d_skip: float32 [3072], P('seq')
- d_out_proj: float32 [3072, 1536], P('seq')
All inputs are finite; a program needn't handle non-finite values.
Results may differ from a plain program's by a relative error of at most 0.0095.
Values may be sent and summed in bfloat16 or wider, within the bound.
A program may use at most 320 MiB of HBM per device.

v0:
```python
import jax
import jax.numpy as jnp
from jax import lax
from jax.sharding import PartitionSpec as P

EPS = 1e-05


def passed_along(block, axis, distance):
    devices = range(lax.axis_size(axis))
    route = [(i - distance, i) for i in devices if i - distance in devices]
    return lax.ppermute(block, axis, route)


def prefix(value, axis, join, neutral, backward):
    count, mine = (lax.axis_size(axis), lax.axis_index(axis))
    pieces = jax.tree.map(lambda part: lax.all_gather(part, axis), value)
    if backward:
        pieces = jax.tree.map(lambda part: part[::-1], pieces)
        mine = count - 1 - mine
    total = jax.tree.map(
        lambda part, zero: jnp.full_like(part, 0) + jnp.asarray(zero, part.dtype), value, neutral
    )

    def hop(position, total):
        longer = join(total, jax.tree.map(lambda part: part[position], pieces))
        return jax.tree.map(lambda new, old: jnp.where(position < mine, new, old), longer, total)

    return lax.fori_loop(0, count - 1, hop, total)


def silu(value):
    return value * jax.nn.sigmoid(value)


def silu_slope(value):
    sigmoid = jax.nn.sigmoid(value)
    return sigmoid * (1.0 + value * (1.0 - sigmoid))


def block_span():
    return 16


def project(left, right):
    return lax.dot_general(
        left, right, (((2,), (0,)), ((), ())), preferred_element_type=jnp.float32
    )


def project_back(left, right):
    return lax.dot_general(
        left, right, (((2,), (1,)), ((), ())), preferred_element_type=jnp.float32
    )


def weight_grad(left, right):
    return lax.dot_general(
        left, right, (((0, 1), (0, 1)), ((), ())), preferred_element_type=jnp.float32
    )


def scan_outputs(delta, drive, b_in, c_in, a_mat, start):
    seg_count, length, inner = delta.shape
    span = block_span()
    blocks = length // span

    def one_block(position, carry):
        current, produced, boundary = carry
        boundary = lax.dynamic_update_index_in_dim(boundary, current, position, 0)
        anchor = position * span
        d_part = lax.dynamic_slice_in_dim(delta, anchor, span, 1)
        v_part = lax.dynamic_slice_in_dim(drive, anchor, span, 1)
        b_part = lax.dynamic_slice_in_dim(b_in, anchor, span, 1)
        c_part = lax.dynamic_slice_in_dim(c_in, anchor, span, 1)
        emitted = []
        for moment in range(span):
            current = (
                jnp.exp(d_part[:, moment, None, :] * a_mat) * current
                + v_part[:, moment, None, :] * b_part[:, moment, :, None]
            )
            emitted.append(jnp.sum(current * c_part[:, moment, :, None], axis=1))
        produced = lax.dynamic_update_slice_in_dim(produced, jnp.stack(emitted, axis=1), anchor, 1)
        return (current, produced, boundary)

    produced = jnp.zeros((seg_count, length, inner), jnp.float32)
    boundary = jnp.zeros((blocks,) + start.shape, jnp.float32)
    final, produced, boundary = lax.fori_loop(0, blocks, one_block, (start, produced, boundary))
    return (produced, boundary, final)


def start_correction(delta, c_in, a_mat, start, produced, boundary):
    length = delta.shape[1]
    span = block_span()
    blocks = length // span

    def one_block(position, carry):
        running, produced, boundary = carry
        held = lax.dynamic_index_in_dim(boundary, position, 0, keepdims=False)
        boundary = lax.dynamic_update_index_in_dim(boundary, held + running, position, 0)
        anchor = position * span
        d_part = lax.dynamic_slice_in_dim(delta, anchor, span, 1)
        c_part = lax.dynamic_slice_in_dim(c_in, anchor, span, 1)
        emitted = []
        for moment in range(span):
            running = jnp.exp(d_part[:, moment, None, :] * a_mat) * running
            emitted.append(jnp.sum(running * c_part[:, moment, :, None], axis=1))
        earlier = lax.dynamic_slice_in_dim(produced, anchor, span, 1)
        produced = lax.dynamic_update_slice_in_dim(
            produced, earlier + jnp.stack(emitted, axis=1), anchor, 1
        )
        return (running, produced, boundary)

    _, produced, boundary = lax.fori_loop(0, blocks, one_block, (start, produced, boundary))
    return (produced, boundary)


def entry_adjoint(delta, d_scanned, c_in, a_mat, zeros_state):
    span = block_span()
    blocks = delta.shape[1] // span

    def one_block(counter, adjoint):
        anchor = (blocks - 1 - counter) * span
        d_part = lax.dynamic_slice_in_dim(delta, anchor, span, 1)
        y_part = lax.dynamic_slice_in_dim(d_scanned, anchor, span, 1)
        c_part = lax.dynamic_slice_in_dim(c_in, anchor, span, 1)
        for moment in reversed(range(span)):
            adjoint = adjoint + y_part[:, moment, None, :] * c_part[:, moment, :, None]
            adjoint = jnp.exp(d_part[:, moment, None, :] * a_mat) * adjoint
        return adjoint

    return lax.fori_loop(0, blocks, one_block, zeros_state)


def scan_backward(delta, drive, b_in, c_in, d_scanned, a_mat, boundary, adjoint_end):
    seg_count, length, inner = delta.shape
    states = a_mat.shape[0]
    span = block_span()
    blocks = length // span

    def one_block(counter, carry):
        adjoint, d_amat, d_delta_all, d_drive_all, d_b_all, d_c_all = carry
        position = blocks - 1 - counter
        anchor = position * span
        current = lax.dynamic_index_in_dim(boundary, position, 0, keepdims=False)
        d_part = lax.dynamic_slice_in_dim(delta, anchor, span, 1)
        v_part = lax.dynamic_slice_in_dim(drive, anchor, span, 1)
        b_part = lax.dynamic_slice_in_dim(b_in, anchor, span, 1)
        c_part = lax.dynamic_slice_in_dim(c_in, anchor, span, 1)
        y_part = lax.dynamic_slice_in_dim(d_scanned, anchor, span, 1)
        history = [current]
        decays = []
        for moment in range(span):
            decay = jnp.exp(d_part[:, moment, None, :] * a_mat)
            current = decay * current + v_part[:, moment, None, :] * b_part[:, moment, :, None]
            decays.append(decay)
            history.append(current)
        delta_list = [None] * span
        drive_list = [None] * span
        b_list = [None] * span
        c_list = [None] * span
        for moment in reversed(range(span)):
            upstream = y_part[:, moment, None, :]
            c_list[moment] = jnp.sum(upstream * history[moment + 1], axis=2)
            adjoint = adjoint + upstream * c_part[:, moment, :, None]
            drive_list[moment] = jnp.sum(adjoint * b_part[:, moment, :, None], axis=1)
            b_list[moment] = jnp.sum(adjoint * v_part[:, moment, None, :], axis=2)
            through = adjoint * history[moment] * decays[moment]
            delta_list[moment] = jnp.sum(through * a_mat, axis=1)
            d_amat = d_amat + jnp.sum(through * d_part[:, moment, None, :], axis=0)
            adjoint = decays[moment] * adjoint
        d_delta_all = lax.dynamic_update_slice_in_dim(
            d_delta_all, jnp.stack(delta_list, axis=1), anchor, 1
        )
        d_drive_all = lax.dynamic_update_slice_in_dim(
            d_drive_all, jnp.stack(drive_list, axis=1), anchor, 1
        )
        d_b_all = lax.dynamic_update_slice_in_dim(d_b_all, jnp.stack(b_list, axis=1), anchor, 1)
        d_c_all = lax.dynamic_update_slice_in_dim(d_c_all, jnp.stack(c_list, axis=1), anchor, 1)
        return (adjoint, d_amat, d_delta_all, d_drive_all, d_b_all, d_c_all)

    start = (
        adjoint_end,
        jnp.zeros((states, inner), jnp.float32),
        jnp.zeros((seg_count, length, inner), jnp.float32),
        jnp.zeros((seg_count, length, inner), jnp.float32),
        jnp.zeros((seg_count, length, states), jnp.float32),
        jnp.zeros((seg_count, length, states), jnp.float32),
    )
    result = lax.fori_loop(0, blocks, one_block, start)
    return (result[2], result[3], result[4], result[5], result[1])


def carry_join(earlier, later):
    return (earlier[0] * later[0], later[0] * earlier[1] + later[1])


def back_join(earlier, later):
    return (later[0] * earlier[0], later[1] + later[0] * earlier[1])


def body(
    tokens,
    conv_state,
    entry_state,
    norm_gain,
    in_proj,
    conv_weight,
    conv_bias,
    x_proj,
    dt_proj,
    dt_bias,
    a_log,
    d_skip,
    out_proj,
    cotangent,
):
    inner = in_proj.shape[1] // 2
    rank = dt_proj.shape[0]
    taps = conv_weight.shape[0]
    halo_rows = taps - 1
    length = tokens.shape[1]
    states = a_log.shape[0]
    is_first = lax.axis_index("seq") == 0
    token_float = tokens.astype(jnp.float32)
    inverse = lax.rsqrt(jnp.mean(token_float * token_float, axis=-1, keepdims=True) + EPS)
    normed = (token_float * inverse * norm_gain).astype(jnp.bfloat16)
    projected = project(normed, in_proj)
    conv_in = projected[..., :inner].astype(jnp.bfloat16)
    gate_in = projected[..., inner:]
    received = passed_along(conv_in[:, length - halo_rows :, :], "seq", 1)
    before = jnp.where(is_first, conv_state, received)
    padded = jnp.concatenate([before, conv_in], axis=1).astype(jnp.float32)
    conv_out = conv_bias + jnp.zeros(conv_in.shape, jnp.float32)
    for tap in range(taps):
        conv_out = conv_out + conv_weight[tap] * padded[:, tap : tap + length]
    activated = silu(conv_out).astype(jnp.bfloat16)
    act_float = activated.astype(jnp.float32)
    coeffs = project(activated, x_proj)
    dt_low = coeffs[..., :rank].astype(jnp.bfloat16)
    b_in = coeffs[..., rank : rank + states]
    c_in = coeffs[..., rank + states :]
    pre_delta = project(dt_low, dt_proj) + dt_bias
    delta = jax.nn.softplus(pre_delta)
    a_mat = -jnp.exp(a_log)
    drive = delta * act_float
    zeros_state = jnp.zeros_like(entry_state)
    local_part, local_bounds, local_end = scan_outputs(delta, drive, b_in, c_in, a_mat, zeros_state)
    decay_all = jnp.exp(jnp.sum(delta, axis=1)[:, None, :] * a_mat)
    pre_decay, pre_state = prefix(
        (decay_all, local_end), "seq", carry_join, (jnp.ones_like(decay_all), zeros_state), False
    )
    start_state = pre_state + pre_decay * entry_state
    scanned_part, boundary = start_correction(
        delta, c_in, a_mat, start_state, local_part, local_bounds
    )
    scanned = scanned_part + d_skip * act_float
    gate_act = silu(gate_in)
    gated = (scanned * gate_act).astype(jnp.bfloat16)
    output = token_float + project(gated, out_proj)
    cot_float = cotangent.astype(jnp.float32)
    d_out_proj = weight_grad(gated, cotangent)
    d_gated = project_back(cotangent, out_proj)
    d_scanned = d_gated * gate_act
    d_gate = d_gated * scanned * silu_slope(gate_in)
    d_d_skip = jnp.sum(d_scanned * act_float, axis=(0, 1))
    entry_mu = entry_adjoint(delta, d_scanned, c_in, a_mat, zeros_state)
    _, adjoint_end = prefix(
        (decay_all, entry_mu), "seq", back_join, (jnp.ones_like(decay_all), zeros_state), True
    )
    d_delta_scan, d_drive, d_b, d_c, d_amat = scan_backward(
        delta, drive, b_in, c_in, d_scanned, a_mat, boundary, adjoint_end
    )
    d_act = d_skip * d_scanned + d_drive * delta
    d_delta = d_delta_scan + d_drive * act_float
    d_pre = d_delta * jax.nn.sigmoid(pre_delta)
    d_dt_bias = jnp.sum(d_pre, axis=(0, 1))
    d_pre_low = d_pre.astype(jnp.bfloat16)
    d_dt_proj = weight_grad(dt_low, d_pre_low)
    d_dt_low = project_back(d_pre_low, dt_proj)
    d_coeffs = jnp.concatenate([d_dt_low, d_b, d_c], axis=-1).astype(jnp.bfloat16)
    d_x_proj = weight_grad(activated, d_coeffs)
    d_act = d_act + project_back(d_coeffs, x_proj)
    d_conv_out = d_act * silu_slope(conv_out)
    d_conv_bias = jnp.sum(d_conv_out, axis=(0, 1))
    d_conv_weight = jnp.stack(
        [jnp.sum(d_conv_out * padded[:, tap : tap + length], axis=(0, 1)) for tap in range(taps)]
    )
    d_padded = jnp.zeros(padded.shape, jnp.float32)
    for tap in range(taps):
        d_padded = d_padded + jnp.pad(
            d_conv_out * conv_weight[tap], ((0, 0), (tap, halo_rows - tap), (0, 0))
        )
    halo_grad = d_padded[:, :halo_rows]
    returned = passed_along(halo_grad, "seq", -1)
    d_conv_in = d_padded[:, halo_rows:] + jnp.pad(
        returned, ((0, 0), (length - halo_rows, 0), (0, 0))
    )
    d_entry, d_conv_state = lax.psum(
        (pre_decay * entry_mu, jnp.where(is_first, halo_grad, 0.0)), "seq"
    )
    d_projected = jnp.concatenate([d_conv_in, d_gate], axis=-1).astype(jnp.bfloat16)
    d_in_proj = weight_grad(normed, d_projected)
    d_normed = project_back(d_projected, in_proj)
    scaled = d_normed * norm_gain
    d_norm_gain = jnp.sum(d_normed * token_float * inverse, axis=(0, 1))
    cubed = inverse * inverse * inverse
    d_tokens = (
        cot_float
        + inverse * scaled
        - token_float * cubed * jnp.mean(scaled * token_float, axis=-1, keepdims=True)
    )
    d_a_log = d_amat * a_mat
    summed = (
        lax.psum_scatter(d_norm_gain, "seq", scatter_dimension=0, tiled=True),
        lax.psum_scatter(d_in_proj, "seq", scatter_dimension=1, tiled=True),
        lax.psum_scatter(d_conv_weight, "seq", scatter_dimension=1, tiled=True),
        lax.psum_scatter(d_conv_bias, "seq", scatter_dimension=0, tiled=True),
        lax.psum_scatter(d_x_proj, "seq", scatter_dimension=0, tiled=True),
        lax.psum_scatter(d_dt_proj, "seq", scatter_dimension=1, tiled=True),
        lax.psum_scatter(d_dt_bias, "seq", scatter_dimension=0, tiled=True),
        lax.psum_scatter(d_a_log, "seq", scatter_dimension=1, tiled=True),
        lax.psum_scatter(d_d_skip, "seq", scatter_dimension=0, tiled=True),
        lax.psum_scatter(d_out_proj, "seq", scatter_dimension=0, tiled=True),
    )
    totals = lax.psum(
        (
            summed[0],
            summed[1],
            summed[2],
            summed[3],
            summed[4],
            summed[5],
            summed[6],
            summed[7],
            summed[8],
            summed[9],
        ),
        "dp",
    )
    return (
        output,
        d_tokens,
        d_conv_state,
        d_entry,
        totals[0],
        totals[1],
        totals[2],
        totals[3],
        totals[4],
        totals[5],
        totals[6],
        totals[7],
        totals[8],
        totals[9],
    )


def solution(mesh):
    placed = (
        P("dp", "seq", None),
        P("dp", None, None),
        P("dp", None, None),
        P(),
        P(),
        P(),
        P(),
        P(),
        P(),
        P(),
        P(),
        P(),
        P(),
        P("dp", "seq", None),
    )
    return jax.shard_map(
        body,
        mesh=mesh,
        in_specs=placed,
        out_specs=(
            P("dp", "seq", None),
            P("dp", "seq", None),
            P("dp", None, None),
            P("dp", None, None),
            P("seq"),
            P(None, "seq"),
            P(None, "seq"),
            P("seq"),
            P("seq", None),
            P(None, "seq"),
            P("seq"),
            P(None, "seq"),
            P("seq"),
            P("seq", None),
        ),
        check_vma=False,
    )
```

profile of v0, /device:TPU:1, one launch (start us, length us, event | category | flops | bytes accessed | tf_op | source)
XLA Modules:
  0.0 2349.9 jit_solution(12625316169265462403)
XLA Ops:
  9.7 17.1 fusion.192
  39.7 25.2 %fusion.152 = (f32[3072]{0:T(1024)}, f32[4,128,3072]{2,1,0:T(8,128)}, bf16[4,128,3072]{2,1,0:T(8,128)(2,1)S(1)}, f32[4,128,3072]{2,1,0:T(8,128)}, f32[4,128,3072]{2,1,0:T(8,128)}) fusion(f32[4,128,6144]{2,1,0:T(8,128)} %get-tuple-element.1768, f32[4,131,3072]{2,1,0:T(8,128)} %maximum_convert_fusion, f32[3072]{0:T(1024)S(1)} %bitcast.733, ...), kind=kOutput, calls=%fused_computation.643 | convolution fusion | flops 4864865280 | bytes 64561152 | tf_op jit(solution)/shard_map/dot_general | solution.py:52
  68.7 6.4 convert_multiply_fusion.3
  75.2 6.6 copy.54
  81.8 6.7 copy.55
  93.5 118.0 %while.106 = (s32[]{:T(128)}, f32[4,16,3072]{2,1,0:T(8,128)S(1)}, f32[4,128,3072]{2,1,0:T(8,128)}, f32[8,4,16,3072]{3,2,1,0:T(8,128)}, f32[4,128,3072]{2,0,1:T(4...) while((s32[]{:T(128)}, f32[4,16,3072]{2,1,0:T(8,128)S(1)}, ...), condition=%wide.region_19.20_spmd.clone, body=%wide.region_2.19_spmd.clone.sunk | while | flops 28704788 | bytes 21065828 | solution.py:88
  217.1 9.4 copy.61
  226.5 78.7 %while.108 = (s32[]{:T(128)}, f32[4,16,3072]{2,1,0:T(8,128)}, f32[4,128,3072]{2,0,1:T(4,128)}, f32[16,3072]{1,0:T(8,128)S(1)}, f32[4,128,3072]{2,0,1:T(4,128)}, ...) while((s32[]{:T(128)}, f32[4,16,3072]{2,1,0:T(8,128)}, ...), condition=%wide.region_41.42_spmd.clone, body=%wide.region_40.41_spmd.clone.sunk | while | flops 12779543 | bytes 6500957 | solution.py:132
  240.2 5.7 add_multiply_fusion.2
  250.1 5.7 add_multiply_fusion.2
  259.9 5.8 add_multiply_fusion.2
  305.7 38.7 %all-gather.6.cloned.1.call-done = f32[8,4,16,3072]{3,2,1,0:T(8,128)} async-done(((f32[1,4,16,3072]{3,2,1,0:T(8,128)}), f32[8,4,16,3072]{3,2,1,0:T(8,128)}) %all-gather.6.cloned.1.call-update) | async-done | bytes 6291472 | tf_op jit(solution)/shard_map/all_gather | solution.py:17
  344.5 14.2 while.107
  362.2 183.5 %while.105 = (s32[]{:T(128)}, f32[4,16,3072]{2,1,0:T(8,128)S(1)}, f32[4,128,3072]{2,1,0:T(8,128)}, f32[8,4,16,3072]{3,2,1,0:T(8,128)}, f32[4,128,3072]{2,0,1:T(4...) while((s32[]{:T(128)}, f32[4,16,3072]{2,1,0:T(8,128)S(1)}, ...), condition=%wide.region_39.40_spmd, body=%wide.region_22.39_spmd.sunk | while | flops 18284564 | bytes 17806416 | solution.py:114
  545.7 6.2 rev.6
  551.9 6.2 rev.7
  558.1 14.6 while.109
  580.8 822.2 %while.110 = (s32[]{:T(128)}, f32[4,16,3072]{2,1,0:T(8,128)S(1)}, f32[16,3072]{1,0:T(8,128)}, f32[4,128,3072]{2,1,0:T(8,128)}, f32[4,128,3072]{2,1,0:T(8,128)}, ...) while((s32[]{:T(128)}, f32[4,16,3072]{2,1,0:T(8,128)S(1)}, ...), condition=%wide.region_125.126_spmd.clone, body=%wide.region_44.125_spmd.clone.sunk | while | flops 75151384 | bytes 60983624 | solution.py:190
  1403.1 17.8 fusion.187
  1431.6 11.3 convolution_bitcast_fusion.1
  1443.7 27.9 %multiply_reduce_fusion.115 = (f32[3072]{0:T(1024)S(1)}, f32[3072]{0:T(1024)S(1)}, f32[3072]{0:T(1024)S(1)}, f32[3072]{0:T(1024)S(1)}, f32[3072]{0:T(1024)S(1)},...) fusion(f32[4,131,3072]{2,1,0:T(8,128)} %maximum_convert_fusion, ...), kind=kOutput, calls=%fused_computation.652 | convolution fusion | flops 442352640 | bytes 76537856 | tf_op jit(solution)/shard_map/dot_general | solution.py:52
  1476.7 6.3 pad_add_fusion
  1486.1 19.2 convolution_bitcast_fusion
  1508.6 168.9 %reduce-scatter.17.cloned.1.call-done = f32[384,1536]{1,0:T(8,128)} async-done(((f32[3072,1536]{1,0:T(8,128)}), f32[384,1536]{1,0:T(8,128)}) %reduce-scatter.17.cloned.1.call-update) | async-done | bytes 2359312 | tf_op jit(solution)/shard_map/reduce_scatter | solution.py:324
  1677.5 365.7 %reduce-scatter.9.cloned.1.call-done = f32[1536,768]{1,0:T(8,128)} async-done(((f32[1536,6144]{1,0:T(8,128)}), f32[1536,768]{1,0:T(8,128)}) %reduce-scatter.9.cloned.1.call-update) | async-done | bytes 4718608 | tf_op jit(solution)/shard_map/reduce_scatter | solution.py:316
  2045.1 10.7 convert_add_fusion
  2055.9 21.7 reduce-scatter.19.cloned.1.call-done
  2078.6 17.2 fusion.164
  2095.8 26.7 %all-reduce.9 = (f32[1536]{0:T(1024)S(1)}, f32[3072]{0:T(1024)S(1)}, f32[3072]{0:T(1024)S(1)}, f32[3072]{0:T(1024)S(1)}) all-reduce(f32[1536]{0:T(1024)S(1)} %get-tuple-element.1330, f32[3072]{0:T(1024)S(1)} %get-tuple-element.1329, f32[3072]{0:T(1024)S(1)} %get-tuple-element.1465, ...), channel_id=4, replica_groups=mesh['dp'=4,'seq'=8] {'seq'}, use_global_device_ids=true, to_apply=%region_130.131.clone | all-reduce | flops 10752 | bytes 86016
  2127.7 13.6 all-reduce.11
  2141.3 28.6 %all-reduce.16.cloned.1.call-done = (f32[4,3,3072]{2,1,0:T(4,128)}, f32[4,16,3072]{2,1,0:T(8,128)}) async-done(((f32[4,3,3072]{2,1,0:T(4,128)}, f32[4,16,3072]{2,1,0:T(8,128)}), (f32[4,3,3072]{2,1,0:T(4,128)}, f32[4,16,3072]{2,1,0:T(8,128)})) %all-reduce.16.cloned.1.call-update) | async-done | bytes 933904 | tf_op jit(solution)/shard_map/psum | solution.py:299
  2171.6 161.8 %all-reduce.18.cloned.1.call-done = (f32[1536,768]{1,0:T(8,128)}, f32[384,128]{1,0:T(8,128)}, f32[96,384]{1,0:T(8,128)}, f32[384,1536]{1,0:T(8,128)}) async-done(((f32[1536,768]{1,0:T(8,128)}, f32[384,128]{1,0:T(8,128)}, f32[96,384]{1,0:T(8,128)}, f32[384,1536]{1,0:T(8,128)}), (f32[1536,768]{1,0:T(8,128)}, f32[384,128]{1,0:T(8,128)}, f32[96,384]{1,0:T(8,128)}, ...) | async-done | bytes 7421968 | tf_op jit(solution)/shard_map/psum | solution.py:326
  (2280 shorter events, 1286.3 us)
Async XLA Ops:
  7.2 57.7 %copy-start = (bf16[3072,128]{1,0:T(8,128)(2,1)S(1)}, bf16[3072,128]{1,0:T(8,128)(2,1)}, u32[]{:S(2)}) copy-start(bf16[3072,128]{1,0:T(8,128)(2,1)} %param.33) | copy-start | bytes 2359300
  7.2 298.5 %all-gather.8.cloned.1.call-start = ((), (), s32[]{:S(2)}) async-start(), calls=%async_computation.12 | async-start | bytes 7077888 | tf_op jit(solution)/shard_map/all_gather | solution.py:17
  26.9 7.0 collective-permute-start
  212.5 132.0 %all-gather.6.cloned.1.call-start = ((), (), s32[]{:S(2)}) async-start(), calls=%async_computation.6 | async-start | bytes 7077888 | tf_op jit(solution)/shard_map/all_gather | solution.py:17
  216.8 329.0 %all-gather.10.cloned.1.call-start = ((), (), s32[]{:S(2)}) async-start(), calls=%async_computation.13 | async-start | bytes 7077888 | tf_op jit(solution)/shard_map/all_gather | solution.py:17
  305.2 1203.4 %reduce-scatter.13.cloned.1.call-start = ((), (), s32[]{:S(2)}) async-start(), calls=%async_computation.9 | async-start | bytes 1327104 | tf_op jit(solution)/shard_map/reduce_scatter | solution.py:320
  614.5 50.0 %copy-start.10 = (f32[16,3072]{1,0:T(8,128)S(1)}, f32[16,3072]{1,0:T(8,128)}, u32[]{:S(2)}) copy-start(f32[16,3072]{1,0:T(8,128)} %get-tuple-element.2723) | copy-start | bytes 589828 | tf_op jit(solution)/shard_map/while
  621.0 60.7 %copy-start.17 = (f32[4,3072]{1,0:T(4,128)S(1)}, f32[4,3072]{1,0:T(4,128)}, u32[]{:S(2)}) copy-start(f32[4,3072]{1,0:T(4,128)} %get-tuple-element.2610) | copy-start | bytes 147460 | tf_op jit(solution)/shard_map/while
  717.2 50.0 %copy-start.10 = (f32[16,3072]{1,0:T(8,128)S(1)}, f32[16,3072]{1,0:T(8,128)}, u32[]{:S(2)}) copy-start(f32[16,3072]{1,0:T(8,128)} %get-tuple-element.2723) | copy-start | bytes 589828 | tf_op jit(solution)/shard_map/while
  723.7 60.7 %copy-start.17 = (f32[4,3072]{1,0:T(4,128)S(1)}, f32[4,3072]{1,0:T(4,128)}, u32[]{:S(2)}) copy-start(f32[4,3072]{1,0:T(4,128)} %get-tuple-element.2610) | copy-start | bytes 147460 | tf_op jit(solution)/shard_map/while
  820.0 49.9 %copy-start.10 = (f32[16,3072]{1,0:T(8,128)S(1)}, f32[16,3072]{1,0:T(8,128)}, u32[]{:S(2)}) copy-start(f32[16,3072]{1,0:T(8,128)} %get-tuple-element.2723) | copy-start | bytes 589828 | tf_op jit(solution)/shard_map/while
  826.5 60.7 %copy-start.17 = (f32[4,3072]{1,0:T(4,128)S(1)}, f32[4,3072]{1,0:T(4,128)}, u32[]{:S(2)}) copy-start(f32[4,3072]{1,0:T(4,128)} %get-tuple-element.2610) | copy-start | bytes 147460 | tf_op jit(solution)/shard_map/while
  922.7 49.9 %copy-start.10 = (f32[16,3072]{1,0:T(8,128)S(1)}, f32[16,3072]{1,0:T(8,128)}, u32[]{:S(2)}) copy-start(f32[16,3072]{1,0:T(8,128)} %get-tuple-element.2723) | copy-start | bytes 589828 | tf_op jit(solution)/shard_map/while
  929.2 60.7 %copy-start.17 = (f32[4,3072]{1,0:T(4,128)S(1)}, f32[4,3072]{1,0:T(4,128)}, u32[]{:S(2)}) copy-start(f32[4,3072]{1,0:T(4,128)} %get-tuple-element.2610) | copy-start | bytes 147460 | tf_op jit(solution)/shard_map/while
  1025.5 49.9 %copy-start.10 = (f32[16,3072]{1,0:T(8,128)S(1)}, f32[16,3072]{1,0:T(8,128)}, u32[]{:S(2)}) copy-start(f32[16,3072]{1,0:T(8,128)} %get-tuple-element.2723) | copy-start | bytes 589828 | tf_op jit(solution)/shard_map/while
  1032.0 60.7 %copy-start.17 = (f32[4,3072]{1,0:T(4,128)S(1)}, f32[4,3072]{1,0:T(4,128)}, u32[]{:S(2)}) copy-start(f32[4,3072]{1,0:T(4,128)} %get-tuple-element.2610) | copy-start | bytes 147460 | tf_op jit(solution)/shard_map/while
  1128.3 49.9 %copy-start.10 = (f32[16,3072]{1,0:T(8,128)S(1)}, f32[16,3072]{1,0:T(8,128)}, u32[]{:S(2)}) copy-start(f32[16,3072]{1,0:T(8,128)} %get-tuple-element.2723) | copy-start | bytes 589828 | tf_op jit(solution)/shard_map/while
  1134.7 60.7 %copy-start.17 = (f32[4,3072]{1,0:T(4,128)S(1)}, f32[4,3072]{1,0:T(4,128)}, u32[]{:S(2)}) copy-start(f32[4,3072]{1,0:T(4,128)} %get-tuple-element.2610) | copy-start | bytes 147460 | tf_op jit(solution)/shard_map/while
  1231.1 50.0 %copy-start.10 = (f32[16,3072]{1,0:T(8,128)S(1)}, f32[16,3072]{1,0:T(8,128)}, u32[]{:S(2)}) copy-start(f32[16,3072]{1,0:T(8,128)} %get-tuple-element.2723) | copy-start | bytes 589828 | tf_op jit(solution)/shard_map/while
  1237.5 60.7 %copy-start.17 = (f32[4,3072]{1,0:T(4,128)S(1)}, f32[4,3072]{1,0:T(4,128)}, u32[]{:S(2)}) copy-start(f32[4,3072]{1,0:T(4,128)} %get-tuple-element.2610) | copy-start | bytes 147460 | tf_op jit(solution)/shard_map/while
  1333.8 49.4 %copy-start.10 = (f32[16,3072]{1,0:T(8,128)S(1)}, f32[16,3072]{1,0:T(8,128)}, u32[]{:S(2)}) copy-start(f32[16,3072]{1,0:T(8,128)} %get-tuple-element.2723) | copy-start | bytes 589828 | tf_op jit(solution)/shard_map/while
  1340.3 60.2 %copy-start.17 = (f32[4,3072]{1,0:T(4,128)S(1)}, f32[4,3072]{1,0:T(4,128)}, u32[]{:S(2)}) copy-start(f32[4,3072]{1,0:T(4,128)} %get-tuple-element.2610) | copy-start | bytes 147460 | tf_op jit(solution)/shard_map/while
  1424.2 84.4 %reduce-scatter.11.cloned.1.call-start = ((), (), s32[]{:S(2)}) async-start(), calls=%async_computation.8 | async-start | bytes 1769472 | tf_op jit(solution)/shard_map/reduce_scatter | solution.py:319
  1431.5 246.0 %reduce-scatter.17.cloned.1.call-start = ((), (), s32[]{:S(2)}) async-start(), calls=%async_computation.11 | async-start | bytes 21233664 | tf_op jit(solution)/shard_map/reduce_scatter | solution.py:324
  1443.0 600.2 %reduce-scatter.9.cloned.1.call-start = ((), (), s32[]{:S(2)}) async-start(), calls=%async_computation.7 | async-start | bytes 42467328 | tf_op jit(solution)/shard_map/reduce_scatter | solution.py:316
  1473.9 9.6 collective-permute-start.1
  1505.3 537.9 %copy-start.102 = (u32[32]{0:T(128)S(1)}, u32[32]{0:T(128)}, u32[]{:S(2)}) copy-start(u32[32]{0:T(128)} %constant.279) | copy-start | bytes 388
  1505.3 572.2 %reduce-scatter.19.cloned.1.call-start = ((), (), s32[]{:S(2)}) async-start(), calls=%async_computation.14 | async-start | bytes 1769472
  1507.1 620.6 %reduce-scatter.15.cloned.1.call-start = ((), (), s32[]{:S(2)}) async-start(), calls=%async_computation.10 | async-start | bytes 221184 | tf_op jit(solution)/shard_map/reduce_scatter | solution.py:322
  1507.9 662.0 %all-reduce.16.cloned.1.call-start = ((), (), s32[]{:S(2)}) async-start(), calls=%async_computation.15 | async-start | bytes 1966080 | tf_op jit(solution)/shard_map/psum | solution.py:299
  1508.5 824.9 %all-reduce.18.cloned.1.call-start = ((), (), s32[]{:S(2)}) async-start(), calls=%async_computation.16 | async-start | bytes 14843904 | tf_op jit(solution)/shard_map/psum | solution.py:326
  2078.6 44.2 %copy-start.100 = (f32[4,128]{1,0:T(4,128)S(1)}, f32[4,128]{1,0:T(4,128)}, u32[]{:S(2)}) copy-start(f32[4,128]{1,0:T(4,128)} %get-tuple-element.1765) | copy-start | bytes 6148
  (511 other events, 6490.3 us)
Sparse Core Ops, SparseCore 0:
  212.6 66.1 all-gather.7
  281.0 63.3 all-gather.5
  346.7 63.3 all-gather.9
  1424.3 27.7 reduce-scatter.12
  1454.9 32.4 reduce-scatter.10
  1489.6 187.8 reduce-scatter.16
  1679.9 363.2 reduce-scatter.8
  2046.2 31.3 reduce-scatter.18
  2080.5 28.1 reduce-scatter.14
  2111.6 58.3 all-reduce.15
  2174.2 159.1 all-reduce.17
where the time goes:
time: 2380 us; the launch traced here: 2350 us
  local copies, waits for them, and re-layouts  814 us (34%)
  waiting for transfers between devices  787 us (33%)
  other arithmetic  533 us (22%)
  matrix products  141 us (6%)
  blocking collectives  40.3 us (2%)
    reduce_scatter x1, waiting for transfers between devices, body(): lax.psum_scatter(d_in_proj, 'seq', scatter_dimension=1, tiled=True)  366 us
    another operation x136, local copies, waits for them, and re-layouts, one_block(): jnp.stack(delta_list, axis=1)  209 us
    reduce_scatter x1, waiting for transfers between devices, body(): lax.psum_scatter(d_out_proj, 'seq', scatter_dimension=0, tiled=True)  169 us
    reduce_sum x40, other arithmetic, one_block(): delta_list[moment] = jnp.sum(through * a_mat, axis=1)  165 us
    psum x1, waiting for transfers between devices, body(): lax.psum((summed[0], summed[1], summed[2], summed[3], summed[4], summed[5...  162 us
    while x1208, local copies, waits for them, and re-layouts  117 us
    another operation x136, local copies, waits for them, and re-layouts, one_block(): jnp.stack(drive_list, axis=1)  117 us
    another operation x272, local copies, waits for them, and re-layouts, one_block(): jnp.stack(emitted, axis=1)  101 us
  transfers between devices with their start and end apart: 13, of which 7 were waited for; matrix products, arithmetic and copies ran while one was open for 17% of the time, Pallas kernels for 0%

commit v1 on v0

v1 whole, which is shorter than its diff:
```python
import functools
import math

import jax
import jax.numpy as jnp
from jax import lax
from jax.experimental import pallas as pl
from jax.experimental.pallas import tpu as pltpu
from jax.sharding import PartitionSpec as P

EPS = 1e-05
LANES = 128
CHUNK = 16
LOG2E = math.log2(math.e)
LN2 = math.log(2.0)
BF16 = jnp.bfloat16
F32 = jnp.float32
VMEM_BYTES = 56 * 2**20


def silu_parts(value):
    sigmoid = jax.nn.sigmoid(value)
    return value * sigmoid, sigmoid * (1.0 + value * (1.0 - sigmoid))


def matmul(left, right):
    return lax.dot_general(left, right, (((1,), (0,)), ((), ())), preferred_element_type=F32)


def matmul_nt(left, right):
    return lax.dot_general(left, right, (((1,), (1,)), ((), ())), preferred_element_type=F32)


def matmul_tn(left, right):
    return lax.dot_general(left, right, (((0,), (0,)), ((), ())), preferred_element_type=F32)


def partner_route(axis, step):
    count = lax.axis_size(axis)
    if count & (count - 1) == 0:
        return [(i, i ^ step) for i in range(count)]
    return [(i, (i + step) % count) for i in range(count)]


def partners(axis, step):
    count, mine = lax.axis_size(axis), lax.axis_index(axis)
    if count & (count - 1) == 0:
        return mine ^ step, mine ^ step
    return (mine + step) % count, (mine + count - step) % count


def swap_columns(block, axis):
    count = lax.axis_size(axis)
    rows, width = block.shape[0], block.shape[1] // count
    gathered = jnp.zeros((count * rows, width), block.dtype)
    for step in range(count):
        target, source = partners(axis, step)
        piece = lax.dynamic_slice_in_dim(block, target * width, width, 1)
        if step:
            piece = lax.ppermute(piece, axis, partner_route(axis, step))
        gathered = lax.dynamic_update_slice_in_dim(gathered, piece, source * rows, 0)
    return gathered


def sum_scatter_rows(block, axis):
    count = lax.axis_size(axis)
    rows = block.shape[0] // count
    low = block.astype(BF16)
    total = None
    for step in range(count):
        target, _ = partners(axis, step)
        if step == 0:
            total = lax.dynamic_slice_in_dim(block, target * rows, rows, 0)
        else:
            piece = lax.dynamic_slice_in_dim(low, target * rows, rows, 0)
            total = total + lax.ppermute(piece, axis, partner_route(axis, step)).astype(F32)
    return total


def gather_rows(block, axis):
    count = lax.axis_size(axis)
    rows = block.shape[0]
    gathered = jnp.zeros((count * rows,) + block.shape[1:], block.dtype)
    for step in range(count):
        _, source = partners(axis, step)
        piece = lax.ppermute(block, axis, partner_route(axis, step)) if step else block
        gathered = lax.dynamic_update_slice_in_dim(gathered, piece, source * rows, 0)
    return gathered


def shifted(block, axis, distance):
    devices = range(lax.axis_size(axis))
    route = [(i - distance, i) for i in devices if i - distance in devices]
    return lax.ppermute(block, axis, route)


def from_first(block, axis):
    count, mine = lax.axis_size(axis), lax.axis_index(axis)
    reach = 1
    while reach < count:
        route = [(i, i + reach) for i in range(min(reach, count - reach))]
        arrived = lax.ppermute(block, axis, route)
        block = jnp.where(mine < reach, block, arrived)
        reach *= 2
    return block


def carried(state, total, first, a_mat, axis, sign):
    count, mine = lax.axis_size(axis), lax.axis_index(axis)
    edge = mine == (0 if sign > 0 else count - 1)
    held, span = shifted(state, axis, sign), shifted(total, axis, sign)
    held = jnp.where(edge, first, held)
    reach = 1
    while reach < count:
        far = shifted(held, axis, sign * reach)
        far_span = shifted(span, axis, sign * reach)
        held = held + jnp.exp(span * a_mat) * far
        span = span + far_span
        reach *= 2
    return held


def spread_row(ref, rows, at, tile, states):
    row = ref.at[0, rows][at : at + 1, tile * LANES : (tile + 1) * LANES]
    return jnp.broadcast_to(row, (states, LANES))


def column(tile):
    return slice(tile * LANES, (tile + 1) * LANES)


def ends_kernel(d_ref, act_ref, y_ref, b_ref, c_ref, a_ref, end_ref, mu_ref, drive):
    states = a_ref.shape[0]
    length, width = d_ref.shape[1:]
    tiles = width // LANES
    rate = [a_ref[:, column(j)] * LOG2E for j in range(tiles)]
    drive[0] = d_ref[0] * act_ref[0].astype(F32)

    def chunk(i, carry):
        h, p, mu = (list(part) for part in carry)
        rows = pl.ds(pl.multiple_of(i * CHUNK, CHUNK), CHUNK)
        for r in range(CHUNK):
            b, c = b_ref[0, i * CHUNK + r], c_ref[0, i * CHUNK + r]
            for j in range(tiles):
                decay = jnp.exp2(spread_row(d_ref, rows, r, j, states) * rate[j])
                h[j] = h[j] * decay + spread_row(drive, rows, r, j, states) * b
                p[j] = p[j] * decay
                mu[j] = mu[j] + p[j] * (spread_row(y_ref, rows, r, j, states) * c)
        return tuple(h), tuple(p), tuple(mu)

    zeros = tuple(jnp.zeros((states, LANES), F32) for _ in range(tiles))
    ones = tuple(jnp.ones((states, LANES), F32) for _ in range(tiles))
    h, _, mu = lax.fori_loop(0, length // CHUNK, chunk, (zeros, ones, zeros))
    for j in range(tiles):
        end_ref[0, :, column(j)] = h[j]
        mu_ref[0, :, column(j)] = mu[j]


def widest(inner, most):
    width = most
    while inner % width:
        width -= LANES
    return width


def block_ends(delta, act, d_scanned, b_wide, c_wide, a_mat):
    segs, length, inner = delta.shape
    states = a_mat.shape[0]
    width = widest(inner, 512)
    tokens = pl.BlockSpec((1, length, width), lambda s, e: (s, 0, e))
    wide = pl.BlockSpec((1, length, states, LANES), lambda s, e: (s, 0, 0, 0))
    state = pl.BlockSpec((1, states, width), lambda s, e: (s, 0, e))
    shape = jax.ShapeDtypeStruct((segs, states, inner), F32)
    return pl.pallas_call(
        ends_kernel,
        grid=(segs, inner // width),
        in_specs=[tokens, tokens, tokens, wide, wide, pl.BlockSpec((states, width), lambda s, e: (0, e))],
        out_specs=[state, state],
        out_shape=[shape, shape],
        scratch_shapes=[pltpu.VMEM((1, length, width), F32)],
        compiler_params=pltpu.CompilerParams(vmem_limit_bytes=VMEM_BYTES),
        cost_estimate=pl.CostEstimate(
            flops=9 * delta.size * states, bytes_accessed=12 * delta.size, transcendentals=delta.size * states
        ),
        name="block_ends",
    )(delta, act, d_scanned, b_wide, c_wide, a_mat)


def scan_kernel(
    d_ref, act_ref, dy_ref, b_ref, c_ref, c_diag, b_diag, ones_ref, a_ref, start_ref, end_ref,
    y_ref, dv_ref, dd_ref, db_ref, dc_ref, da_ref,
    history, drive, low_a, low_b, through_a, through_b,
):
    states = a_ref.shape[0]
    length, width = d_ref.shape[1:]
    tiles, chunks = width // LANES, length // CHUNK
    span = min(width, 256)
    parts = width // span
    rate = [a_ref[:, column(j)] * LOG2E for j in range(tiles)]
    history[0:states, :] = start_ref[0]
    drive[0] = d_ref[0] * act_ref[0].astype(F32)

    def rows_of(i):
        return pl.ds(pl.multiple_of(i * CHUNK, CHUNK), CHUNK)

    def kept(i, r):
        return pl.ds(pl.multiple_of((i * CHUNK + r) * states, states), states)

    def sum_y(i, low, part):
        at = slice(part * span, (part + 1) * span)
        y_ref[0, rows_of(i), at] = jnp.dot(c_diag[0, i], low[:, at], preferred_element_type=F32)

    def forward(i, h, low, before, low_before):
        rows = rows_of(i)
        waiting = list(range(parts))
        for r in range(CHUNK):
            b = b_ref[0, i * CHUNK + r]
            for j in range(tiles):
                decay = jnp.exp2(spread_row(d_ref, rows, r, j, states) * rate[j])
                h[j] = h[j] * decay + spread_row(drive, rows, r, j, states) * b
                history[kept(i, r + 1), column(j)] = h[j]
                low[r * states : (r + 1) * states, column(j)] = h[j].astype(BF16)
            if waiting and r % (CHUNK // parts) == 1:
                sum_y(before, low_before, waiting.pop(0))
        return h

    def forward_pair(pair, carry):
        h = forward(2 * pair, list(carry), low_a, jnp.maximum(2 * pair - 1, 0), low_b)
        return tuple(forward(2 * pair + 1, h, low_b, 2 * pair, low_a))

    lax.fori_loop(0, chunks // 2, forward_pair, tuple(start_ref[0, :, column(j)] for j in range(tiles)))
    for part in range(parts):
        sum_y(chunks - 1, low_b, part)

    @pl.when(pl.program_id(1) == 0)
    def _():
        db_ref[...] = jnp.zeros_like(db_ref)
        dc_ref[...] = jnp.zeros_like(dc_ref)

    def sum_back(i, low, through, part, which):
        at = slice(part * span, (part + 1) * span)
        if which == 0:
            dv_ref[0, rows_of(i), at] = jnp.dot(b_diag[0, i], low[:, at], preferred_element_type=F32)
        else:
            dd_ref[0, rows_of(i), at] = jnp.dot(ones_ref[...], through[:, at], preferred_element_type=F32)

    def backward(i, lam, da, low, through, before, low_before, through_before):
        rows = rows_of(i)
        waiting = [(part, which) for part in range(parts) for which in (0, 1)]
        for r in reversed(range(CHUNK)):
            c = c_ref[0, i * CHUNK + r]
            db = dc = None
            for j in range(tiles):
                step = spread_row(d_ref, rows, r, j, states)
                up = spread_row(dy_ref, rows, r, j, states)
                adjoint = lam[j] + up * c
                db_j = adjoint * spread_row(drive, rows, r, j, states)
                dc_j = up * history[kept(i, r + 1), column(j)]
                db, dc = (db_j, dc_j) if db is None else (db + db_j, dc + dc_j)
                low[r * states : (r + 1) * states, column(j)] = adjoint.astype(BF16)
                lam[j] = adjoint * jnp.exp2(step * rate[j])
                flow = lam[j] * history[kept(i, r), column(j)]
                through[r * states : (r + 1) * states, column(j)] = (flow * rate[j]).astype(BF16)
                da[j] = da[j] + flow * step
            db_ref[0, i * CHUNK + r] += db
            dc_ref[0, i * CHUNK + r] += dc
            if waiting and (CHUNK - 1 - r) % max(1, CHUNK // (2 * parts)) == 1:
                sum_back(before, low_before, through_before, *waiting.pop(0))
        for item in waiting:
            sum_back(before, low_before, through_before, *item)
        return lam, da

    def backward_pair(pair, carry):
        lam, da = (list(part) for part in carry)
        i = chunks - 1 - 2 * pair
        lam, da = backward(i, lam, da, low_a, through_a, jnp.minimum(i + 1, chunks - 1), low_b, through_b)
        lam, da = backward(i - 1, lam, da, low_b, through_b, i, low_a, through_a)
        return tuple(lam), tuple(da)

    zeros = tuple(jnp.zeros((states, LANES), F32) for _ in range(tiles))
    _, da = lax.fori_loop(
        0, chunks // 2, backward_pair, (tuple(end_ref[0, :, column(j)] for j in range(tiles)), zeros)
    )
    for part in range(parts):
        sum_back(0, low_b, through_b, part, 0)
        sum_back(0, low_b, through_b, part, 1)
    for j in range(tiles):
        da_ref[0, :, column(j)] = da[j]


def scan_both(delta, act, d_scanned, b_wide, c_wide, c_diag, b_diag, ones_diag, a_mat, start, end):
    segs, length, inner = delta.shape
    states = a_mat.shape[0]
    width = widest(inner, 1024)
    tokens = pl.BlockSpec((1, length, width), lambda s, e: (s, 0, e))
    wide = pl.BlockSpec((1, length, states, LANES), lambda s, e: (s, 0, 0, 0))
    diag = pl.BlockSpec((1,) + c_diag.shape[1:], lambda s, e: (s, 0, 0, 0))
    state = pl.BlockSpec((1, states, width), lambda s, e: (s, 0, e))
    by_token = jax.ShapeDtypeStruct((segs, length, inner), F32)
    by_lane = jax.ShapeDtypeStruct((segs, length, states, LANES), F32)
    low = pltpu.VMEM((CHUNK * states, width), BF16)
    return pl.pallas_call(
        scan_kernel,
        grid=(segs, inner // width),
        in_specs=[
            tokens, tokens, tokens, wide, wide, diag, diag,
            pl.BlockSpec(ones_diag.shape, lambda s, e: (0, 0)),
            pl.BlockSpec((states, width), lambda s, e: (0, e)),
            state, state,
        ],
        out_specs=[tokens, tokens, tokens, wide, wide, state],
        out_shape=[by_token, by_token, by_token, by_lane, by_lane, jax.ShapeDtypeStruct((segs, states, inner), F32)],
        scratch_shapes=[
            pltpu.VMEM(((length + 1) * states, width), F32),
            pltpu.VMEM((1, length, width), F32),
            low, low, low, low,
        ],
        compiler_params=pltpu.CompilerParams(vmem_limit_bytes=VMEM_BYTES),
        cost_estimate=pl.CostEstimate(
            flops=20 * delta.size * states, bytes_accessed=30 * delta.size, transcendentals=2 * delta.size * states
        ),
        name="scan_both",
    )(delta, act, d_scanned, b_wide, c_wide, c_diag, b_diag, ones_diag, a_mat, start, end)


def diagonal_blocks(value):
    segs, length, states = value.shape
    spread = value.reshape(segs, length // CHUNK, CHUNK, 1, states)
    spread = spread * jnp.eye(CHUNK, dtype=value.dtype)[:, :, None]
    return spread.reshape(segs, length // CHUNK, CHUNK, CHUNK * states).astype(BF16)


def body(
    tokens, conv_state, entry_state, norm_gain, in_proj, conv_weight, conv_bias, x_proj,
    dt_proj, dt_bias, a_log, d_skip, out_proj, cotangent,
):
    segs, length, width = tokens.shape
    inner = in_proj.shape[1] // 2
    rank, states, taps = dt_proj.shape[0], a_log.shape[0], conv_weight.shape[0]
    halo = taps - 1
    count = segs * length
    n_seq = lax.axis_size("seq")
    mine = lax.axis_index("seq")
    is_first = mine == 0

    def flat(value):
        return value.reshape((count,) + value.shape[2:])

    def split(value):
        return value.reshape((segs, length) + value.shape[1:])

    token_float = flat(tokens).astype(F32)
    inverse = lax.rsqrt(jnp.mean(token_float * token_float, axis=-1, keepdims=True) + EPS)
    normed = (token_float * inverse * norm_gain).astype(BF16)
    cot = flat(cotangent)
    normed_all = lax.all_gather(normed, "seq", axis=0, tiled=True)
    cot_all = lax.all_gather(cot, "seq", axis=0, tiled=True)
    conv_in = matmul(normed, in_proj[:, :inner]).astype(BF16)
    gate_in = matmul(normed, in_proj[:, inner:])
    d_gated = matmul_nt(cot, out_proj)
    conv_in = split(conv_in)
    before = jnp.where(is_first, conv_state, shifted(conv_in[:, length - halo :], "seq", 1))
    padded = jnp.concatenate([before, conv_in], axis=1).astype(F32)
    conv_out = conv_bias + sum(conv_weight[tap] * padded[:, tap : tap + length] for tap in range(taps))
    activated = (conv_out * jax.nn.sigmoid(conv_out)).astype(BF16)
    coeffs = matmul(flat(activated), x_proj)
    dt_low = coeffs[:, :rank].astype(BF16)
    b_in = split(coeffs[:, rank : rank + states])
    c_in = split(coeffs[:, rank + states :])
    pre_delta = matmul(dt_low, dt_proj) + dt_bias
    delta = split(jax.nn.softplus(pre_delta))
    a_mat = -jnp.exp(a_log)
    gate_act, gate_slope = silu_parts(gate_in)
    d_scanned = d_gated * gate_act

    b_wide = jnp.broadcast_to(b_in[..., None], b_in.shape + (LANES,))
    c_wide = jnp.broadcast_to(c_in[..., None], c_in.shape + (LANES,))
    ends, entry_mu = block_ends(delta, activated, split(d_scanned), b_wide, c_wide, a_mat)
    total = jnp.sum(delta, axis=1, keepdims=True)
    start = carried(ends, total, entry_state, a_mat, "seq", 1)
    end = carried(entry_mu, total, 0.0, a_mat, "seq", -1)
    d_entry = from_first(entry_mu + jnp.exp(total * a_mat) * end, "seq")
    ones_diag = diagonal_blocks(jnp.ones((1, CHUNK, states), F32))[0, 0]
    produced, d_drive, d_delta_scan, d_b, d_c, d_amat = scan_both(
        delta, activated, split(d_scanned), b_wide, c_wide,
        diagonal_blocks(c_in), diagonal_blocks(b_in), ones_diag, a_mat, start, end,
    )
    d_b = jnp.sum(flat(d_b), axis=-1)
    d_c = jnp.sum(flat(d_c), axis=-1)
    delta, act_float = flat(delta), flat(activated).astype(F32)
    produced, d_drive, d_delta_scan = flat(produced), flat(d_drive), flat(d_delta_scan)

    scanned = produced + d_skip * act_float
    gated = (scanned * gate_act).astype(BF16)
    d_gate = (d_gated * scanned * gate_slope).astype(BF16)
    out_columns = swap_columns(gated, "seq")
    gate_columns = swap_columns(d_gate, "seq")
    output = token_float + matmul(gated, out_proj)
    d_d_skip = jnp.sum(d_scanned * act_float, axis=0)

    d_act = d_skip * d_scanned + d_drive * delta
    d_delta = LN2 * d_delta_scan + d_drive * act_float
    d_pre = d_delta * jax.nn.sigmoid(pre_delta)
    d_dt_bias = jnp.sum(d_pre, axis=0)
    d_pre_low = d_pre.astype(BF16)
    d_dt_proj = matmul_tn(dt_low, d_pre_low)
    d_dt_low = matmul_nt(d_pre_low, dt_proj)
    d_coeffs = jnp.concatenate([d_dt_low, d_b, d_c], axis=-1).astype(BF16)
    d_x_proj = matmul_tn(d_coeffs, flat(activated))
    d_a_log = jnp.sum(d_amat, axis=0) * a_mat
    d_act = split(d_act + matmul_nt(d_coeffs, x_proj))
    conv_sigmoid = jax.nn.sigmoid(conv_out)
    d_conv_out = d_act * (conv_sigmoid * (1.0 + conv_out * (1.0 - conv_sigmoid)))
    d_conv_bias = jnp.sum(d_conv_out, axis=(0, 1))
    d_conv_weight = jnp.stack(
        [jnp.sum(d_conv_out * padded[:, tap : tap + length], axis=(0, 1)) for tap in range(taps)]
    )
    head = jnp.pad(d_conv_out[:, :halo], ((0, 0), (0, halo), (0, 0)))
    halo_grad = sum(
        conv_weight[tap] * jnp.pad(d_conv_out[:, : halo - tap], ((0, 0), (tap, 0), (0, 0))) for tap in range(halo)
    )
    del head
    returned = shifted(halo_grad, "seq", -1)
    tail = jnp.pad(d_conv_out, ((0, 0), (0, halo), (0, 0)))
    d_conv_in = sum(conv_weight[tap] * tail[:, halo - tap : halo - tap + length] for tap in range(taps))
    d_conv_in = d_conv_in + jnp.pad(returned, ((0, 0), (length - halo, 0), (0, 0)))
    d_conv_in = flat(d_conv_in).astype(BF16)
    d_conv_state = from_first(halo_grad, "seq")

    small = jnp.concatenate([d_x_proj, d_dt_proj, d_a_log, d_dt_bias[None], d_d_skip[None]], axis=0)
    edges = jnp.concatenate([d_conv_weight, d_conv_bias[None]], axis=0)

    def pad_rows(value):
        return jnp.pad(value, ((0, -value.shape[0] % (16 * lax.axis_size("dp"))), (0, 0))).astype(BF16)

    def summed_small(value):
        padded_rows = pad_rows(value)
        parts = swap_columns(padded_rows, "seq").reshape(n_seq, padded_rows.shape[0], -1)
        whole = sum_scatter_rows(jnp.sum(parts.astype(F32), axis=0), "dp")
        return gather_rows(whole.astype(BF16), "dp").astype(F32)

    small = summed_small(small)
    conv_columns = swap_columns(d_conv_in, "seq")
    edges = summed_small(edges)
    out_part = sum_scatter_rows(matmul_tn(out_columns, cot_all), "dp")
    d_out_proj = gather_rows(out_part.astype(BF16), "dp").astype(F32)

    gate_part = sum_scatter_rows(matmul_tn(normed_all, gate_columns), "dp").astype(BF16)
    conv_part = sum_scatter_rows(matmul_tn(normed_all, conv_columns), "dp").astype(BF16)
    half = n_seq // 2
    even = mine % 2 == 0
    straight = [(i, i // 2 + (0 if i % 2 == 0 else half)) for i in range(n_seq)]
    crossed = [(i, i // 2 + (half if i % 2 == 0 else 0)) for i in range(n_seq)]
    first = lax.ppermute(jnp.where(even, conv_part, gate_part), "seq", straight)
    second = lax.ppermute(jnp.where(even, gate_part, conv_part), "seq", crossed)
    low_half = mine < half
    d_in_part = jnp.concatenate(
        [jnp.where(low_half, first, second), jnp.where(low_half, second, first)], axis=1
    )
    d_in_proj = gather_rows(d_in_part, "dp").astype(F32)

    d_normed = matmul_nt(d_conv_in, in_proj[:, :inner]) + matmul_nt(d_gate, in_proj[:, inner:])
    d_norm_gain = jnp.sum(d_normed * token_float * inverse, axis=0)
    scaled = d_normed * norm_gain
    cubed = inverse * inverse * inverse
    d_tokens = (
        cot.astype(F32)
        + inverse * scaled
        - token_float * cubed * jnp.mean(scaled * token_float, axis=-1, keepdims=True)
    )
    gain_parts = swap_columns(d_norm_gain[None], "seq")
    d_norm_gain = jnp.sum(gather_rows(jnp.sum(gain_parts, axis=0, keepdims=True), "dp"), axis=0)

    return (
        split(output),
        split(d_tokens),
        d_conv_state,
        d_entry,
        d_norm_gain,
        d_in_proj,
        edges[:taps],
        edges[taps],
        small[: rank + 2 * states].T,
        small[rank + 2 * states : 2 * rank + 2 * states],
        small[2 * rank + 3 * states],
        small[2 * rank + 2 * states : 2 * rank + 3 * states],
        small[2 * rank + 3 * states + 1],
        d_out_proj,
    )


def solution(mesh):
    by_token, by_segment, whole = P("dp", "seq", None), P("dp", None, None), P()
    return jax.shard_map(
        body,
        mesh=mesh,
        in_specs=(by_token, by_segment, by_segment) + (whole,) * 10 + (by_token,),
        out_specs=(
            by_token, by_token, by_segment, by_segment, P("seq"), P(None, "seq"), P(None, "seq"), P("seq"),
            P("seq", None), P(None, "seq"), P("seq"), P(None, "seq"), P("seq"), P("seq", None),
        ),
        check_vma=False,
    )
```

time: 2380 us -> 998 us (0.42)
  local copies, waits for them, and re-layouts: 814 us -> 81.7 us
  waiting for transfers between devices: 787 us -> 296 us
  other arithmetic: 533 us -> 78.8 us
  starting transfers between devices: 8.57 us -> 234 us
  Pallas kernels: 0 us -> 160 us
  blocking collectives: 40.3 us -> 0 us
    reduce_scatter x5 -> x0, waiting for transfers between devices: 535 us -> none  [the longest x1 366 us: body(): lax.psum_scatter(d_in_proj, 'seq', scatter_dimension=1, tiled=True)]
    another operation x562 -> x8, local copies, waits for them, and re-layouts: 438 us -> 6.02 us  [the longest x136 209 us: one_block(): jnp.stack(delta_list, axis=1)]
    reduce_sum x138 -> x9, other arithmetic: 344 us -> 32.7 us  [the longest x1 18.3 us: body(): d_dt_bias = jnp.sum(d_pre, axis=0)]
    ppermute x2 -> x96, waiting for transfers between devices: 0.44 us -> 296 us  [the longest x42 142 us: swap_columns(): piece = lax.ppermute(piece, axis, partner_route(axis, step))]
    ppermute x2 -> x96, starting transfers between devices: 7.44 us -> 234 us  [the longest x42 85.3 us: swap_columns(): piece = lax.ppermute(piece, axis, partner_route(axis, step))]
    psum x2 -> x0, waiting for transfers between devices: 190 us -> none  [the longest x1 162 us: body(): lax.psum((summed[0], summed[1], summed[2], summed[3], summed[4], summed[5...]
    pallas_call x0 -> x2, Pallas kernels: none -> 160 us  [the longest x1 120 us: scan_both(): pl.pallas_call(scan_kernel, grid=(segs, inner // width), in_specs=[tokens...]
    mul x88 -> x6, local copies, waits for them, and re-layouts: 133 us -> 13.9 us  [diagonal_blocks(): spread = spread * jnp.eye(CHUNK, dtype=value.dtype)[:, :, None]]
  transfers between devices with their start and end apart: 13 -> 98, of which waited for: 7 -> 28; matrix products, arithmetic and copies ran while one was open for 17% -> 27% of each run, Pallas kernels for 0% -> 16%
where the time goes in v1:
time: 998 us; the launch traced here: 986 us
  waiting for transfers between devices  296 us (30%)
  starting transfers between devices  234 us (23%)
  Pallas kernels  160 us (16%)
  matrix products  119 us (12%)
  local copies, waits for them, and re-layouts  81.7 us (8%)
  other arithmetic  78.8 us (8%)
  between operations  16.5 us (2%)
    ppermute x42, waiting for transfers between devices, swap_columns(): piece = lax.ppermute(piece, axis, partner_route(axis, step))  142 us
    pallas_call x1, Pallas kernels, scan_both(): pl.pallas_call(scan_kernel, grid=(segs, inner // width), in_specs=[tokens...  120 us
    ppermute x16, waiting for transfers between devices, shifted(): return lax.ppermute(block, axis, route)  97.4 us
    ppermute x42, starting transfers between devices, swap_columns(): piece = lax.ppermute(piece, axis, partner_route(axis, step))  85.3 us
    ppermute x1, starting transfers between devices, body(): first = lax.ppermute(jnp.where(even, conv_part, gate_part), 'seq', straight)  49.5 us
    ppermute x16, starting transfers between devices, shifted(): return lax.ppermute(block, axis, route)  48.6 us
    dot_general x5, matrix products, matmul_nt(): lax.dot_general(left, right, (((1,), (1,)), ((), ())), preferred_element_...  42.2 us
    dot_general x5, matrix products, matmul(): lax.dot_general(left, right, (((1,), (0,)), ((), ())), preferred_element_...  40.3 us
  transfers between devices with their start and end apart: 98, of which 28 were waited for; matrix products, arithmetic and copies ran while one was open for 27% of the time, Pallas kernels for 16%

profile of v1, /device:TPU:1, one launch (start us, length us, event | category | flops | bytes accessed | tf_op | source)
XLA Modules:
  0.0 986.0 jit_solution(16038923943079317153)
XLA Ops:
  12.8 9.2 fusion.16
  27.6 10.6 %fusion.2 = f32[512,3072]{1,0:T(8,128)} fusion(bf16[512,1536]{1,0:T(8,128)(2,1)S(1)} %copy-done.12, bf16[1536,6144]{1,0:T(8,128)(2,1)} %param.18), kind=kOutput, calls=%fused_computation.6 | convolution fusion | flops 4831838208 | bytes 17301504 | tf_op jit(solution)/shard_map/dot_general | solution.py:27
  50.3 9.8 bitcast_reduce_fusion
  60.2 14.2 %fusion.11 = (bf16[3072]{0:T(1024)(128)(2,1)}, f32[512,3072]{1,0:T(8,128)}, f32[512,3072]{1,0:T(8,128)}) fusion(bf16[4,128,3072]{2,1,0:T(8,128)(2,1)} %copy-done.4, f32[512,3072]{1,0:T(8,128)} %fusion.2, bf16[512,1536]{1,0:T(8,128)(2,1)S(1)} %bitcast.145, bf16[3072,1536]{1,0:T(8,128)(2,1)} %param.26), kind=kOutput, calls=%fused_computation.15 | convolution fusion | flops 4844418048 | bytes 33036288 | tf_op jit(solution)/shard_map/dot_general | solution.py:31
  79.8 39.8 %block_ends.1 = (f32[4,16,3072]{2,1,0:T(8,128)}, f32[4,16,3072]{2,1,0:T(8,128)}) custom-call(f32[4,128,3072]{2,1,0:T(8,128)} %bitcast.140, bf16[4,128,3072]{2,1,0:T(8,128)(2,1)} %copy-done.4, f32[4,128,3072]{2,1,0:T(8,128)} %bitcast.142, f32[4,128,16,128]{3,2,1,0:T(8,128)} %broadcast_in_dim.77.b_ref, f32[4,128,16,128]{3,2,1,0:T(8,128)} %broadcast_in_dim.79.c_ref, ...), custom_call_target="tpu_custom_call" | custom-call | flops 226492416 | bytes 18874368 | tf_op jit(solution)/shard_map/block_ends/pallas_call | solution.py:174
  125.3 12.1 %collective-permute-done.8 = f32[4,16,3072]{2,1,0:T(8,128)S(1)} collective-permute-done((f32[4,16,3072]{2,1,0:T(8,128)}, f32[4,16,3072]{2,1,0:T(8,128)S(1)}, u32[]{:S(2)}, u32[]{:S(2)}) %collective-permute-start.8) | collective-permute-done | bytes 786464 | tf_op jit(solution)/shard_map/ppermute | solution.py:94
  199.8 79.6 %collective-permute-done.14 = f32[4,16,3072]{2,1,0:T(8,128)S(1)} collective-permute-done((f32[4,16,3072]{2,1,0:T(8,128)S(1)}, f32[4,16,3072]{2,1,0:T(8,128)S(1)}, u32[]{:S(2)}, u32[]{:S(2)}) %collective-permute-start.14) | collective-permute-done | bytes 786464 | tf_op jit(solution)/shard_map/ppermute | solution.py:94
  281.0 120.2 %scan_both.1 = (f32[4,128,3072]{2,1,0:T(8,128)}, f32[4,128,3072]{2,1,0:T(8,128)}, f32[4,128,3072]{2,1,0:T(8,128)}, f32[4,128,16,128]{3,2,1,0:T(8,128)}, f32[4,12...) custom-call(f32[4,128,3072]{2,1,0:T(8,128)} %bitcast.141, bf16[4,128,3072]{2,1,0:T(8,128)(2,1)} %copy-done.4, ...), custom_call_target="tpu_custom_call" | custom-call | flops 503316480 | bytes 47185920 | tf_op jit(solution)/shard_map/scan_both/pallas_call | solution.py:302
  414.8 18.3 %fusion.50 = (bf16[3072]{0:T(1024)(128)(2,1)}, bf16[512,3072]{1,0:T(8,128)(2,1)S(1)}, bf16[512,3072]{1,0:T(8,128)(2,1)}, bf16[512,3072]{1,0:T(8,128)(2,1)}) fusion(f32[512,3072]{1,0:T(8,128)} %get-tuple-element.213, f32[3072]{0:T(1024)S(1)} %copy-done.60, bf16[4,128,3072]{2,1,0:T(8,128)(2,1)} %copy-done.4, f32[4,128,3072]{2,1,0:T(8,128)} %get-tuple-element.25, ...), kind=kLoop, calls=%fused_computation.227 | loop fusion | flops 39318528 | bytes 50362368 | tf_op jit(solution)/shard_map/reduce_sum | solution.py:404
  435.9 7.8 fusion.13
  443.7 6.7 multiply_reduce_fusion
  469.7 9.4 fusion
  479.2 9.5 convolution_add_fusion
  492.9 8.6 concatenate.22
  544.0 9.6 fusion.29
  562.5 14.3 %collective-permute-done.74 = bf16[256,384]{1,0:T(8,128)(2,1)S(1)} collective-permute-done((bf16[256,384]{1,0:T(8,128)(2,1)S(1)}, bf16[256,384]{1,0:T(8,128)(2,1)S(1)}, u32[]{:S(2)}, u32[]{:S(2)}) %collective-permute-start.74) | collective-permute-done | bytes 196640 | tf_op jit(solution)/shard_map/ppermute | solution.py:60
  638.0 21.0 %collective-permute-done.44 = bf16[512,384]{1,0:T(8,128)(2,1)S(1)} collective-permute-done((bf16[512,384]{1,0:T(8,128)(2,1)}, bf16[512,384]{1,0:T(8,128)(2,1)S(1)}, u32[]{:S(2)}, u32[]{:S(2)}) %collective-permute-start.44) | collective-permute-done | bytes 393248 | tf_op jit(solution)/shard_map/ppermute | solution.py:60
  667.5 24.5 %collective-permute-done.86 = bf16[512,384]{1,0:T(8,128)(2,1)S(1)} collective-permute-done((bf16[512,384]{1,0:T(8,128)(2,1)}, bf16[512,384]{1,0:T(8,128)(2,1)S(1)}, u32[]{:S(2)}, u32[]{:S(2)}) %collective-permute-start.86) | collective-permute-done | bytes 393248 | tf_op jit(solution)/shard_map/ppermute | solution.py:60
  692.8 23.9 %collective-permute-done.46 = bf16[512,384]{1,0:T(8,128)(2,1)S(1)} collective-permute-done((bf16[512,384]{1,0:T(8,128)(2,1)}, bf16[512,384]{1,0:T(8,128)(2,1)S(1)}, u32[]{:S(2)}, u32[]{:S(2)}) %collective-permute-start.46) | collective-permute-done | bytes 393248 | tf_op jit(solution)/shard_map/ppermute | solution.py:60
  717.4 15.8 %collective-permute-done.87 = bf16[512,384]{1,0:T(8,128)(2,1)S(1)} collective-permute-done((bf16[512,384]{1,0:T(8,128)(2,1)}, bf16[512,384]{1,0:T(8,128)(2,1)S(1)}, u32[]{:S(2)}, u32[]{:S(2)}) %collective-permute-start.87) | collective-permute-done | bytes 393248 | tf_op jit(solution)/shard_map/ppermute | solution.py:60
  736.1 15.7 %collective-permute-start.33 = (bf16[512,384]{1,0:T(8,128)(2,1)S(1)}, bf16[512,384]{1,0:T(8,128)(2,1)S(1)}, u32[]{:S(2)}, u32[]{:S(2)}) collective-permute-start(bf16[512,384]{1,0:T(8,128)(2,1)S(1)} %copy-done.40), channel_id=1, source_target_pairs={{0,2},{1,3},{2,0},{3,1},{4,6},{5,7},{6,4},{7,5},{8,10},{9,11},{10,... | collective-permute-start | bytes 1179656 | tf_op jit(solution)/shard_map/ppermute | solution.py:60
  752.7 12.9 %collective-permute-start.34 = (bf16[512,384]{1,0:T(8,128)(2,1)S(1)}, bf16[512,384]{1,0:T(8,128)(2,1)S(1)}, u32[]{:S(2)}, u32[]{:S(2)}) collective-permute-start(bf16[512,384]{1,0:T(8,128)(2,1)S(1)} %copy-done.39), channel_id=1, source_target_pairs={{0,3},{1,2},{2,1},{3,0},{4,7},{5,6},{6,5},{7,4},{8,11},{9,10},{10,... | collective-permute-start | bytes 1179656 | tf_op jit(solution)/shard_map/ppermute | solution.py:60
  779.7 13.2 %collective-permute-done.20 = f32[4,16,3072]{2,1,0:T(8,128)S(1)} collective-permute-done((f32[4,16,3072]{2,1,0:T(8,128)S(1)}, f32[4,16,3072]{2,1,0:T(8,128)S(1)}, u32[]{:S(2)}, u32[]{:S(2)}) %collective-permute-start.20) | collective-permute-done | bytes 786464 | tf_op jit(solution)/shard_map/ppermute | solution.py:102
  793.0 9.8 collective-permute-start.21
  807.3 21.4 %collective-permute-done.36 = bf16[512,384]{1,0:T(8,128)(2,1)S(1)} collective-permute-done((bf16[512,384]{1,0:T(8,128)(2,1)S(1)}, bf16[512,384]{1,0:T(8,128)(2,1)S(1)}, u32[]{:S(2)}, u32[]{:S(2)}) %collective-permute-start.36) | collective-permute-done | bytes 393248 | tf_op jit(solution)/shard_map/ppermute | solution.py:60
  835.9 7.6 collective-permute-done.38
  845.3 11.2 %fusion.56 = (bf16[1536,384]{1,0:T(8,128)(2,1)S(1)}, f32[1536,384]{1,0:T(8,128)S(1)}) fusion(bf16[4096,1536]{1,0:T(8,128)(2,1)} %all-gather.3.cloned.1.call-done, bf16[4096,384]{1,0:T(8,128)(2,1)} %constant_dynamic-update-slice_fusion.43), kind=kOutput, calls=%fused_computation.231 | convolution fusion | flops 4832428032 | bytes 19267584 | tf_op jit(solution)/shard_map/dot_general | solution.py:35
  860.1 10.3 %fusion.57 = (bf16[1536,384]{1,0:T(8,128)(2,1)S(1)}, f32[1536,384]{1,0:T(8,128)}) fusion(bf16[4096,1536]{1,0:T(8,128)(2,1)S(1)} %copy-done.3, bf16[4096,384]{1,0:T(8,128)(2,1)} %constant_dynamic-update-slice_fusion.35), kind=kOutput, calls=%fused_computation.232 | convolution fusion | flops 4832428032 | bytes 19267584 | tf_op jit(solution)/shard_map/dot_general | solution.py:35
  874.0 9.0 fusion.58
  887.7 49.5 %collective-permute-start.52 = (bf16[384,384]{1,0:T(8,128)(2,1)S(1)}, bf16[384,384]{1,0:T(8,128)(2,1)S(1)}, u32[]{:S(2)}, u32[]{:S(2)}) collective-permute-start(bf16[384,384]{1,0:T(8,128)(2,1)S(1)} %get-tuple-element.120), channel_id=1, source_target_pairs={{0,0},{1,4},{2,1},{3,5},{4,2},{5,6},{6,3},{7,7},{8,8},{9,12},{10,9... | collective-permute-start | bytes 884744 | tf_op jit(solution)/shard_map/ppermute | solution.py:454
  952.6 10.6 %collective-permute-done.54 = bf16[384,768]{1,0:T(8,128)(2,1)S(1)} collective-permute-done((bf16[384,768]{1,0:T(8,128)(2,1)S(1)}, bf16[384,768]{1,0:T(8,128)(2,1)S(1)}, u32[]{:S(2)}, u32[]{:S(2)}) %collective-permute-start.54) | collective-permute-done | bytes 589856 | tf_op jit(solution)/shard_map/ppermute | solution.py:86
  968.2 8.0 collective-permute-done.56
  (491 shorter events, 325.4 us)
Async XLA Ops:
  7.2 838.1 %all-gather.3.cloned.1.call-start = ((), (), s32[]{:S(2)}) async-start(), calls=%async_computation | async-start | bytes 14155776 | tf_op jit(solution)/shard_map/all_gather | solution.py:356
  12.7 861.3 %all-gather.5.cloned.1.call-start = ((), (), s32[]{:S(2)}) async-start(), calls=%async_computation.1 | async-start | bytes 14155776 | tf_op jit(solution)/shard_map/all_gather | solution.py:357
  154.0 37.7 %collective-permute-start.12 = (f32[4,16,3072]{2,1,0:T(8,128)S(1)}, f32[4,16,3072]{2,1,0:T(8,128)}, u32[]{:S(2)}, u32[]{:S(2)}) collective-permute-start(f32[4,16,3072]{2,1,0:T(8,128)S(1)} %get-tuple-element.186), channel_id=1, source_target_pairs={{2,0},{3,1},{4,2},{5,3},{6,4},{7,5},{10,8},{11,9},{12,10},{13,11},... | collective-permute-start | bytes 2359304 | tf_op jit(solution)/shard_map/ppermute | solution.py:94
  155.3 36.4 %collective-permute-start.5 = (f32[4,16,3072]{2,1,0:T(8,128)S(1)}, f32[4,16,3072]{2,1,0:T(8,128)}, u32[]{:S(2)}, u32[]{:S(2)}) collective-permute-start(f32[4,16,3072]{2,1,0:T(8,128)S(1)} %get-tuple-element.187), channel_id=1, source_target_pairs={{0,2},{1,3},{2,4},{3,5},{4,6},{5,7},{8,10},{9,11},{10,12},{11,13},... | collective-permute-start | bytes 2359304 | tf_op jit(solution)/shard_map/ppermute | solution.py:94
  193.4 85.9 %collective-permute-start.14 = (f32[4,16,3072]{2,1,0:T(8,128)S(1)}, f32[4,16,3072]{2,1,0:T(8,128)S(1)}, u32[]{:S(2)}, u32[]{:S(2)}) collective-permute-start(f32[4,16,3072]{2,1,0:T(8,128)S(1)} %get-tuple-element.184), channel_id=1, source_target_pairs={{4,0},{5,1},{6,2},{7,3},{12,8},{13,9},{14,10},{15,11},{20,16},{21,... | collective-permute-start | bytes 2359304 | tf_op jit(solution)/shard_map/ppermute | solution.py:94
  194.7 84.6 %collective-permute-start.7 = (f32[4,16,3072]{2,1,0:T(8,128)S(1)}, f32[4,16,3072]{2,1,0:T(8,128)S(1)}, u32[]{:S(2)}, u32[]{:S(2)}) collective-permute-start(f32[4,16,3072]{2,1,0:T(8,128)S(1)} %get-tuple-element.185), channel_id=1, source_target_pairs={{0,4},{1,5},{2,6},{3,7},{8,12},{9,13},{10,14},{11,15},{16,20},{17,... | collective-permute-start | bytes 2359304 | tf_op jit(solution)/shard_map/ppermute | solution.py:94
  453.9 85.4 %collective-permute-start.15 = (f32[4,3,3072]{2,1,0:T(4,128)}, f32[4,3,3072]{2,1,0:T(4,128)}, u32[]{:S(2)}, u32[]{:S(2)}) collective-permute-start(f32[4,3,3072]{2,1,0:T(4,128)} %fusion.39), channel_id=1, source_target_pairs={{1,0},{2,1},{3,2},{4,3},{5,4},{6,5},{7,6},{9,8},{10,9},{11,10},{12... | collective-permute-start | bytes 442376 | tf_op jit(solution)/shard_map/ppermute | solution.py:94
  457.1 129.4 %collective-permute-start.16 = (f32[4,3,3072]{2,1,0:T(4,128)}, f32[4,3,3072]{2,1,0:T(4,128)}, u32[]{:S(2)}, u32[]{:S(2)}) collective-permute-start(f32[4,3,3072]{2,1,0:T(4,128)} %fusion.39), channel_id=1, source_target_pairs={{0,1},{8,9},{16,17},{24,25}} | collective-permute-start | bytes 442376 | tf_op jit(solution)/shard_map/ppermute | solution.py:102
  459.5 42.0 %collective-permute-start.57 = (bf16[64,384]{1,0:T(8,128)(2,1)}, bf16[64,384]{1,0:T(8,128)(2,1)}, u32[]{:S(2)}, u32[]{:S(2)}) collective-permute-start(bf16[64,384]{1,0:T(8,128)(2,1)} %get-tuple-element.192), channel_id=1, source_target_pairs={{0,1},{1,0},{2,3},{3,2},{4,5},{5,4},{6,7},{7,6},{8,9},{9,8},{10,11... | collective-permute-start | bytes 147464 | tf_op jit(solution)/shard_map/ppermute | solution.py:60
  461.3 44.0 %collective-permute-start.58 = (bf16[64,384]{1,0:T(8,128)(2,1)}, bf16[64,384]{1,0:T(8,128)(2,1)}, u32[]{:S(2)}, u32[]{:S(2)}) collective-permute-start(bf16[64,384]{1,0:T(8,128)(2,1)} %get-tuple-element.193), channel_id=1, source_target_pairs={{0,2},{1,3},{2,0},{3,1},{4,6},{5,7},{6,4},{7,5},{8,10},{9,11},{10,... | collective-permute-start | bytes 147464 | tf_op jit(solution)/shard_map/ppermute | solution.py:60
  461.7 44.8 %collective-permute-start.59 = (bf16[64,384]{1,0:T(8,128)(2,1)}, bf16[64,384]{1,0:T(8,128)(2,1)}, u32[]{:S(2)}, u32[]{:S(2)}) collective-permute-start(bf16[64,384]{1,0:T(8,128)(2,1)} %get-tuple-element.194), channel_id=1, source_target_pairs={{0,3},{1,2},{2,1},{3,0},{4,7},{5,6},{6,5},{7,4},{8,11},{9,10},{10,... | collective-permute-start | bytes 147464 | tf_op jit(solution)/shard_map/ppermute | solution.py:60
  520.7 35.7 %collective-permute-start.70 = (bf16[256,384]{1,0:T(8,128)(2,1)S(1)}, bf16[256,384]{1,0:T(8,128)(2,1)S(1)}, u32[]{:S(2)}, u32[]{:S(2)}) collective-permute-start(bf16[256,384]{1,0:T(8,128)(2,1)S(1)} %get-tuple-element.158), channel_id=1, source_target_pairs={{0,1},{1,0},{2,3},{3,2},{4,5},{5,4},{6,7},{7,6},{8,9},{9,8},{10,11... | collective-permute-start | bytes 589832 | tf_op jit(solution)/shard_map/ppermute | solution.py:60
  522.3 35.0 %collective-permute-start.71 = (bf16[256,384]{1,0:T(8,128)(2,1)S(1)}, bf16[256,384]{1,0:T(8,128)(2,1)S(1)}, u32[]{:S(2)}, u32[]{:S(2)}) collective-permute-start(bf16[256,384]{1,0:T(8,128)(2,1)S(1)} %get-tuple-element.159), channel_id=1, source_target_pairs={{0,2},{1,3},{2,0},{3,1},{4,6},{5,7},{6,4},{7,5},{8,10},{9,11},{10,... | collective-permute-start | bytes 589832 | tf_op jit(solution)/shard_map/ppermute | solution.py:60
  594.7 171.6 %collective-permute-start.19 = (f32[4,16,3072]{2,1,0:T(8,128)S(1)}, f32[4,16,3072]{2,1,0:T(8,128)S(1)}, u32[]{:S(2)}, u32[]{:S(2)}) collective-permute-start(f32[4,16,3072]{2,1,0:T(8,128)S(1)} %get-tuple-element.123), channel_id=1, source_target_pairs={{0,1},{8,9},{16,17},{24,25}} | collective-permute-start | bytes 2359304 | tf_op jit(solution)/shard_map/ppermute | solution.py:102
  625.2 33.8 %collective-permute-start.44 = (bf16[512,384]{1,0:T(8,128)(2,1)}, bf16[512,384]{1,0:T(8,128)(2,1)S(1)}, u32[]{:S(2)}, u32[]{:S(2)}) collective-permute-start(bf16[512,384]{1,0:T(8,128)(2,1)} %get-tuple-element.143), channel_id=1, source_target_pairs={{0,3},{1,2},{2,1},{3,0},{4,7},{5,6},{6,5},{7,4},{8,11},{9,10},{10,... | collective-permute-start | bytes 1179656 | tf_op jit(solution)/shard_map/ppermute | solution.py:60
  634.9 57.1 %collective-permute-start.86 = (bf16[512,384]{1,0:T(8,128)(2,1)}, bf16[512,384]{1,0:T(8,128)(2,1)S(1)}, u32[]{:S(2)}, u32[]{:S(2)}) collective-permute-start(bf16[512,384]{1,0:T(8,128)(2,1)} %get-tuple-element.134), channel_id=1, source_target_pairs={{0,4},{1,5},{2,6},{3,7},{4,0},{5,1},{6,2},{7,3},{8,12},{9,13},{10,... | collective-permute-start | bytes 1179656 | tf_op jit(solution)/shard_map/ppermute | solution.py:60
  659.0 57.6 %collective-permute-start.46 = (bf16[512,384]{1,0:T(8,128)(2,1)}, bf16[512,384]{1,0:T(8,128)(2,1)S(1)}, u32[]{:S(2)}, u32[]{:S(2)}) collective-permute-start(bf16[512,384]{1,0:T(8,128)(2,1)} %get-tuple-element.141), channel_id=1, source_target_pairs={{0,5},{1,4},{2,7},{3,6},{4,1},{5,0},{6,3},{7,2},{8,13},{9,12},{10,... | collective-permute-start | bytes 1179656 | tf_op jit(solution)/shard_map/ppermute | solution.py:60
  663.8 69.4 %collective-permute-start.87 = (bf16[512,384]{1,0:T(8,128)(2,1)}, bf16[512,384]{1,0:T(8,128)(2,1)S(1)}, u32[]{:S(2)}, u32[]{:S(2)}) collective-permute-start(bf16[512,384]{1,0:T(8,128)(2,1)} %get-tuple-element.133), channel_id=1, source_target_pairs={{0,5},{1,4},{2,7},{3,6},{4,1},{5,0},{6,3},{7,2},{8,13},{9,12},{10,... | collective-permute-start | bytes 1179656 | tf_op jit(solution)/shard_map/ppermute | solution.py:60
  665.1 68.9 %collective-permute-start.47 = (bf16[512,384]{1,0:T(8,128)(2,1)S(1)}, bf16[512,384]{1,0:T(8,128)(2,1)S(1)}, u32[]{:S(2)}, u32[]{:S(2)}) collective-permute-start(bf16[512,384]{1,0:T(8,128)(2,1)S(1)} %copy-done.31), channel_id=1, source_target_pairs={{0,6},{1,7},{2,4},{3,5},{4,2},{5,3},{6,0},{7,1},{8,14},{9,15},{10,... | collective-permute-start | bytes 1179656 | tf_op jit(solution)/shard_map/ppermute | solution.py:60
  692.0 44.1 %collective-permute-start.88 = (bf16[512,384]{1,0:T(8,128)(2,1)S(1)}, bf16[512,384]{1,0:T(8,128)(2,1)S(1)}, u32[]{:S(2)}, u32[]{:S(2)}) collective-permute-start(bf16[512,384]{1,0:T(8,128)(2,1)S(1)} %copy-done.34), channel_id=1, source_target_pairs={{0,6},{1,7},{2,4},{3,5},{4,2},{5,3},{6,0},{7,1},{8,14},{9,15},{10,... | collective-permute-start | bytes 1179656 | tf_op jit(solution)/shard_map/ppermute | solution.py:60
  716.6 36.0 %collective-permute-start.48 = (bf16[512,384]{1,0:T(8,128)(2,1)S(1)}, bf16[512,384]{1,0:T(8,128)(2,1)S(1)}, u32[]{:S(2)}, u32[]{:S(2)}) collective-permute-start(bf16[512,384]{1,0:T(8,128)(2,1)S(1)} %copy-done.30), channel_id=1, source_target_pairs={{0,7},{1,6},{2,5},{3,4},{4,3},{5,2},{6,1},{7,0},{8,15},{9,14},{10,... | collective-permute-start | bytes 1179656 | tf_op jit(solution)/shard_map/ppermute | solution.py:60
  733.2 36.9 %collective-permute-start.89 = (bf16[512,384]{1,0:T(8,128)(2,1)S(1)}, bf16[512,384]{1,0:T(8,128)(2,1)S(1)}, u32[]{:S(2)}, u32[]{:S(2)}) collective-permute-start(bf16[512,384]{1,0:T(8,128)(2,1)S(1)} %copy-done.33), channel_id=1, source_target_pairs={{0,7},{1,6},{2,5},{3,4},{4,3},{5,2},{6,1},{7,0},{8,15},{9,14},{10,... | collective-permute-start | bytes 1179656 | tf_op jit(solution)/shard_map/ppermute | solution.py:60
  734.0 59.0 %collective-permute-start.32 = (bf16[512,384]{1,0:T(8,128)(2,1)S(1)}, bf16[512,384]{1,0:T(8,128)(2,1)S(1)}, u32[]{:S(2)}, u32[]{:S(2)}) collective-permute-start(bf16[512,384]{1,0:T(8,128)(2,1)S(1)} %copy-done.41), channel_id=1, source_target_pairs={{0,1},{1,0},{2,3},{3,2},{4,5},{5,4},{6,7},{7,6},{8,9},{9,8},{10,11... | collective-permute-start | bytes 1179656 | tf_op jit(solution)/shard_map/ppermute | solution.py:60
  736.1 67.5 %collective-permute-start.33 = (bf16[512,384]{1,0:T(8,128)(2,1)S(1)}, bf16[512,384]{1,0:T(8,128)(2,1)S(1)}, u32[]{:S(2)}, u32[]{:S(2)}) collective-permute-start(bf16[512,384]{1,0:T(8,128)(2,1)S(1)} %copy-done.40), channel_id=1, source_target_pairs={{0,2},{1,3},{2,0},{3,1},{4,6},{5,7},{6,4},{7,5},{8,10},{9,11},{10,... | collective-permute-start | bytes 1179656 | tf_op jit(solution)/shard_map/ppermute | solution.py:60
  752.7 53.0 %collective-permute-start.34 = (bf16[512,384]{1,0:T(8,128)(2,1)S(1)}, bf16[512,384]{1,0:T(8,128)(2,1)S(1)}, u32[]{:S(2)}, u32[]{:S(2)}) collective-permute-start(bf16[512,384]{1,0:T(8,128)(2,1)S(1)} %copy-done.39), channel_id=1, source_target_pairs={{0,3},{1,2},{2,1},{3,0},{4,7},{5,6},{6,5},{7,4},{8,11},{9,10},{10,... | collective-permute-start | bytes 1179656 | tf_op jit(solution)/shard_map/ppermute | solution.py:60
  792.9 35.8 %collective-permute-start.36 = (bf16[512,384]{1,0:T(8,128)(2,1)S(1)}, bf16[512,384]{1,0:T(8,128)(2,1)S(1)}, u32[]{:S(2)}, u32[]{:S(2)}) collective-permute-start(bf16[512,384]{1,0:T(8,128)(2,1)S(1)} %copy-done.37), channel_id=1, source_target_pairs={{0,5},{1,4},{2,7},{3,6},{4,1},{5,0},{6,3},{7,2},{8,13},{9,12},{10,... | collective-permute-start | bytes 1179656 | tf_op jit(solution)/shard_map/ppermute | solution.py:60
  793.0 51.3 %collective-permute-start.21 = (f32[4,16,3072]{2,1,0:T(8,128)S(1)}, f32[4,16,3072]{2,1,0:T(8,128)S(1)}, u32[]{:S(2)}, u32[]{:S(2)}) collective-permute-start(f32[4,16,3072]{2,1,0:T(8,128)S(1)} %broadcast_select_fusion.2), channel_id=1, source_target_pairs={{0,4},{1,5},{2,6},{3,7},{8,12},{9,13},{10,14},{11,15},{16,20},{17,... | collective-permute-start | bytes 2359304 | tf_op jit(solution)/shard_map/ppermute | solution.py:102
  805.7 37.8 %collective-permute-start.38 = (bf16[512,384]{1,0:T(8,128)(2,1)S(1)}, bf16[512,384]{1,0:T(8,128)(2,1)S(1)}, u32[]{:S(2)}, u32[]{:S(2)}) collective-permute-start(bf16[512,384]{1,0:T(8,128)(2,1)S(1)} %copy-done.35), channel_id=1, source_target_pairs={{0,7},{1,6},{2,5},{3,4},{4,3},{5,2},{6,1},{7,0},{8,15},{9,14},{10,... | collective-permute-start | bytes 1179656 | tf_op jit(solution)/shard_map/ppermute | solution.py:60
  883.2 54.2 %collective-permute-start.92 = (bf16[96,1536]{1,0:T(8,128)(2,1)S(1)}, bf16[96,1536]{1,0:T(8,128)(2,1)S(1)}, u32[]{:S(2)}, u32[]{:S(2)}) collective-permute-start(bf16[96,1536]{1,0:T(8,128)(2,1)S(1)} %get-tuple-element.166), channel_id=1, source_target_pairs={{0,24},{8,16},{16,8},{24,0},{1,25},{9,17},{17,9},{25,1},{2,26},{10... | collective-permute-start | bytes 884744 | tf_op jit(solution)/shard_map/ppermute | solution.py:76
  883.5 53.8 %collective-permute-start.91 = (bf16[96,1536]{1,0:T(8,128)(2,1)S(1)}, bf16[96,1536]{1,0:T(8,128)(2,1)S(1)}, u32[]{:S(2)}, u32[]{:S(2)}) collective-permute-start(bf16[96,1536]{1,0:T(8,128)(2,1)S(1)} %get-tuple-element.167), channel_id=1, source_target_pairs={{0,16},{8,24},{16,0},{24,8},{1,17},{9,25},{17,1},{25,9},{2,18},{10... | collective-permute-start | bytes 884744 | tf_op jit(solution)/shard_map/ppermute | solution.py:76
  884.7 52.6 %collective-permute-start.90 = (bf16[96,1536]{1,0:T(8,128)(2,1)S(1)}, bf16[96,1536]{1,0:T(8,128)(2,1)S(1)}, u32[]{:S(2)}, u32[]{:S(2)}) collective-permute-start(bf16[96,1536]{1,0:T(8,128)(2,1)S(1)} %get-tuple-element.165), channel_id=1, source_target_pairs={{0,8},{8,0},{16,24},{24,16},{1,9},{9,1},{17,25},{25,17},{2,10},{10... | collective-permute-start | bytes 884744 | tf_op jit(solution)/shard_map/ppermute | solution.py:76
  887.7 56.4 %collective-permute-start.52 = (bf16[384,384]{1,0:T(8,128)(2,1)S(1)}, bf16[384,384]{1,0:T(8,128)(2,1)S(1)}, u32[]{:S(2)}, u32[]{:S(2)}) collective-permute-start(bf16[384,384]{1,0:T(8,128)(2,1)S(1)} %get-tuple-element.120), channel_id=1, source_target_pairs={{0,0},{1,4},{2,1},{3,5},{4,2},{5,6},{6,3},{7,7},{8,8},{9,12},{10,9... | collective-permute-start | bytes 884744 | tf_op jit(solution)/shard_map/ppermute | solution.py:454
  (134 other events, 3194.0 us)
Sparse Core Ops, SparseCore 0:
  12.8 121.3 all-gather.2
  160.3 154.5 all-gather.4

commit v2 on v1

--- a/solution.py
+++ b/solution.py
@@ -62,19 +62,19 @@
     return gathered
 
 
-def sum_scatter_rows(block, axis):
-    count = lax.axis_size(axis)
-    rows = block.shape[0] // count
-    low = block.astype(BF16)
-    total = None
-    for step in range(count):
-        target, _ = partners(axis, step)
-        if step == 0:
-            total = lax.dynamic_slice_in_dim(block, target * rows, rows, 0)
-        else:
-            piece = lax.dynamic_slice_in_dim(low, target * rows, rows, 0)
-            total = total + lax.ppermute(piece, axis, partner_route(axis, step)).astype(F32)
-    return total
+def sum_scatter(blocks, axis):
+    count, mine = lax.axis_size(axis), lax.axis_index(axis)
+    if count & (count - 1):
+        return lax.psum_scatter(blocks, axis, scatter_dimension=0)
+    levels = count.bit_length() - 1
+    held = blocks.reshape((2,) * levels + blocks.shape[1:])
+    for level in range(levels):
+        bit = (mine >> level) & 1
+        at = levels - 1 - level
+        sent = lax.dynamic_index_in_dim(held, 1 - bit, at, keepdims=False).astype(BF16)
+        arrived = lax.ppermute(sent, axis, [(i, i ^ (1 << level)) for i in range(count)])
+        held = lax.dynamic_index_in_dim(held, bit, at, keepdims=False).astype(F32) + arrived.astype(F32)
+    return held
 
 
 def gather_rows(block, axis):
@@ -105,19 +105,123 @@
     return block
 
 
-def carried(state, total, first, a_mat, axis, sign):
-    count, mine = lax.axis_size(axis), lax.axis_index(axis)
-    edge = mine == (0 if sign > 0 else count - 1)
-    held, span = shifted(state, axis, sign), shifted(total, axis, sign)
-    held = jnp.where(edge, first, held)
-    reach = 1
-    while reach < count:
-        far = shifted(held, axis, sign * reach)
-        far_span = shifted(span, axis, sign * reach)
-        held = held + jnp.exp(span * a_mat) * far
-        span = span + far_span
-        reach *= 2
-    return held
+MESH = pl.DeviceIdType.MESH
+
+
+def carry_kernel(
+    pieces, end_ref, mu_ref, total_ref, entry_ref, a_ref, start_ref, lam_ref,
+    ahead, back, from_left, from_right, sent_right, sent_left, got_left, got_right,
+):
+    count, mine = lax.axis_size("seq"), lax.axis_index("seq")
+    width = end_ref.shape[2] // pieces
+    has_left, has_right = mine > 0, mine < count - 1
+    left, right = jnp.maximum(mine - 1, 0), jnp.minimum(mine + 1, count - 1)
+
+    barrier = pltpu.get_barrier_semaphore()
+
+    @pl.when(has_left)
+    def _():
+        pl.semaphore_signal(barrier, inc=1, device_id={"seq": left}, device_id_type=MESH)
+
+    @pl.when(has_right)
+    def _():
+        pl.semaphore_signal(barrier, inc=1, device_id={"seq": right}, device_id_type=MESH)
+
+    pl.semaphore_wait(barrier, has_left.astype(jnp.int32) + has_right.astype(jnp.int32))
+
+    def at(piece):
+        return pl.ds(pl.multiple_of(piece * width, LANES), width)
+
+    def to_right(piece):
+        return pltpu.make_async_remote_copy(
+            src_ref=ahead.at[:, :, at(piece)], dst_ref=from_left.at[:, :, at(piece)],
+            send_sem=sent_right.at[piece], recv_sem=got_left.at[piece],
+            device_id={"seq": right}, device_id_type=MESH,
+        )
+
+    def to_left(piece):
+        return pltpu.make_async_remote_copy(
+            src_ref=back.at[:, :, at(piece)], dst_ref=from_right.at[:, :, at(piece)],
+            send_sem=sent_left.at[piece], recv_sem=got_right.at[piece],
+            device_id={"seq": left}, device_id_type=MESH,
+        )
+
+    def decay(piece):
+        return jnp.exp(total_ref[:, :, at(piece)] * a_ref[:, at(piece)][None])
+
+    def step(tick, nothing):
+        piece = tick - mine
+
+        @pl.when(jnp.logical_and(piece >= 0, piece < pieces))
+        def _():
+            @pl.when(has_left)
+            def _():
+                to_right(piece).wait_recv()
+                start_ref[:, :, at(piece)] = from_left[:, :, at(piece)]
+
+            @pl.when(jnp.logical_not(has_left))
+            def _():
+                start_ref[:, :, at(piece)] = entry_ref[:, :, at(piece)]
+
+            @pl.when(has_right)
+            def _():
+                ahead[:, :, at(piece)] = end_ref[:, :, at(piece)] + decay(piece) * start_ref[:, :, at(piece)]
+                to_right(piece).start()
+
+        other = tick - (count - 1 - mine)
+
+        @pl.when(jnp.logical_and(other >= 0, other < pieces))
+        def _():
+            @pl.when(has_right)
+            def _():
+                to_left(other).wait_recv()
+                lam_ref[:, :, at(other)] = from_right[:, :, at(other)]
+
+            @pl.when(jnp.logical_not(has_right))
+            def _():
+                lam_ref[:, :, at(other)] = jnp.zeros(lam_ref.shape[:2] + (width,), F32)
+
+            @pl.when(has_left)
+            def _():
+                back[:, :, at(other)] = mu_ref[:, :, at(other)] + decay(other) * lam_ref[:, :, at(other)]
+                to_left(other).start()
+
+        return nothing
+
+    lax.fori_loop(0, pieces + count - 1, step, 0)
+
+    def finish(piece, nothing):
+        @pl.when(has_right)
+        def _():
+            to_right(piece).wait_send()
+
+        @pl.when(has_left)
+        def _():
+            to_left(piece).wait_send()
+
+        return nothing
+
+    lax.fori_loop(0, pieces, finish, 0)
+
+
+def carry(ends, entry_mu, total, entry_state, a_mat):
+    pieces = 6
+    while ends.shape[2] % (pieces * LANES):
+        pieces -= 1
+    shape = jax.ShapeDtypeStruct(ends.shape, F32)
+    held = pltpu.VMEM(ends.shape, F32)
+    vmem = pl.BlockSpec(memory_space=pltpu.VMEM)
+    return pl.pallas_call(
+        functools.partial(carry_kernel, pieces),
+        in_specs=[vmem] * 5,
+        out_specs=[vmem] * 2,
+        out_shape=[shape, shape],
+        scratch_shapes=[held] * 4 + [pltpu.SemaphoreType.DMA((pieces,))] * 4,
+        compiler_params=pltpu.CompilerParams(
+            collective_id=1, has_side_effects=True, vmem_limit_bytes=32 * 2**20
+        ),
+        name="carry",
+    )(ends, entry_mu, total, entry_state, a_mat)
 
 
 def spread_row(ref, rows, at, tile, states):
@@ -129,12 +233,14 @@
     return slice(tile * LANES, (tile + 1) * LANES)
 
 
-def ends_kernel(d_ref, act_ref, y_ref, b_ref, c_ref, a_ref, end_ref, mu_ref, drive):
+def ends_kernel(d_ref, act_ref, gate_ref, dg_ref, b_ref, c_ref, a_ref, end_ref, mu_ref, drive, up):
     states = a_ref.shape[0]
     length, width = d_ref.shape[1:]
     tiles = width // LANES
     rate = [a_ref[:, column(j)] * LOG2E for j in range(tiles)]
     drive[0] = d_ref[0] * act_ref[0].astype(F32)
+    gate = gate_ref[0]
+    up[0] = dg_ref[0] * (gate * jax.nn.sigmoid(gate))
 
     def chunk(i, carry):
         h, p, mu = (list(part) for part in carry)
@@ -145,7 +251,7 @@
                 decay = jnp.exp2(spread_row(d_ref, rows, r, j, states) * rate[j])
                 h[j] = h[j] * decay + spread_row(drive, rows, r, j, states) * b
                 p[j] = p[j] * decay
-                mu[j] = mu[j] + p[j] * (spread_row(y_ref, rows, r, j, states) * c)
+                mu[j] = mu[j] + p[j] * (spread_row(up, rows, r, j, states) * c)
         return tuple(h), tuple(p), tuple(mu)
 
     zeros = tuple(jnp.zeros((states, LANES), F32) for _ in range(tiles))
@@ -163,7 +269,7 @@
     return width
 
 
-def block_ends(delta, act, d_scanned, b_wide, c_wide, a_mat):
+def block_ends(delta, act, gate_in, d_gated, b_wide, c_wide, a_mat):
     segs, length, inner = delta.shape
     states = a_mat.shape[0]
     width = widest(inner, 512)
@@ -174,31 +280,99 @@
     return pl.pallas_call(
         ends_kernel,
         grid=(segs, inner // width),
-        in_specs=[tokens, tokens, tokens, wide, wide, pl.BlockSpec((states, width), lambda s, e: (0, e))],
+        in_specs=[tokens] * 4 + [wide, wide, pl.BlockSpec((states, width), lambda s, e: (0, e))],
         out_specs=[state, state],
         out_shape=[shape, shape],
-        scratch_shapes=[pltpu.VMEM((1, length, width), F32)],
+        scratch_shapes=[pltpu.VMEM((1, length, width), F32)] * 2,
         compiler_params=pltpu.CompilerParams(vmem_limit_bytes=VMEM_BYTES),
         cost_estimate=pl.CostEstimate(
             flops=9 * delta.size * states, bytes_accessed=12 * delta.size, transcendentals=delta.size * states
         ),
         name="block_ends",
-    )(delta, act, d_scanned, b_wide, c_wide, a_mat)
+    )(delta, act, gate_in, d_gated, b_wide, c_wide, a_mat)
 
 
 def scan_kernel(
-    d_ref, act_ref, dy_ref, b_ref, c_ref, c_diag, b_diag, ones_ref, a_ref, start_ref, end_ref,
-    y_ref, dv_ref, dd_ref, db_ref, dc_ref, da_ref,
-    history, drive, low_a, low_b, through_a, through_b,
+    hosted, n_blocks_static, d_ref, act_ref, gate_ref, dg_ref, b_ref, c_ref, c_diag, b_diag, ones_ref, a_ref, skip_ref, start_ref, end_ref,
+    gated_ref, dgate_ref, dpre_ref, dact_ref, db_ref, dc_ref, da_ref, sums_ref, gated_all, gate_all,
+    history, drive, up, low_a, low_b, through_a, through_b, db_acc, dc_acc, sum_acc,
+    gated_out, gate_out, gated_sent, gated_got, gate_sent, gate_got, own_sem,
 ):
     states = a_ref.shape[0]
     length, width = d_ref.shape[1:]
     tiles, chunks = width // LANES, length // CHUNK
-    span = min(width, 256)
+    span = math.gcd(width, 256)
     parts = width // span
     rate = [a_ref[:, column(j)] * LOG2E for j in range(tiles)]
+    seg, block, n_blocks = pl.program_id(0), pl.program_id(1), pl.num_programs(1)
+    n_dp, n_seq = lax.axis_size("dp"), lax.axis_size("seq")
+    my_dp, my_seq = lax.axis_index("dp"), lax.axis_index("seq")
+    tick = seg * n_blocks + block
+    slot = lax.rem(tick, 2)
+    channels = n_blocks_static * width // n_seq
+    owners = width // channels if hosted else 0
+
+    @pl.when(tick == 0)
+    def _():
+        barrier = pltpu.get_barrier_semaphore()
+        for p in range(1, n_dp):
+            pl.semaphore_signal(barrier, inc=1, device_id={"dp": lax.rem(my_dp + p, n_dp)}, device_id_type=MESH)
+        for p in range(1, n_seq if hosted else 1):
+            pl.semaphore_signal(barrier, inc=1, device_id={"seq": lax.rem(my_seq + p, n_seq)}, device_id_type=MESH)
+        pl.semaphore_wait(barrier, n_dp - 1 + (n_seq - 1 if hosted else 0))
+
+    def gated_copies(s, e, slot):
+        at = (my_dp, s, slice(None), pl.ds(pl.multiple_of(e * width, LANES), width))
+        own = pltpu.make_async_copy(gated_out.at[slot], gated_all.at[at], own_sem.at[slot, 0])
+        far = [
+            pltpu.make_async_remote_copy(
+                src_ref=gated_out.at[slot], dst_ref=gated_all.at[at],
+                send_sem=gated_sent.at[slot, p], recv_sem=gated_got.at[my_dp],
+                device_id={"dp": lax.rem(my_dp + p, n_dp)}, device_id_type=MESH,
+            )
+            for p in range(1, n_dp)
+        ]
+        return own, far
+
+    def gate_copies(s, e, slot):
+        for q in range(owners):
+            owner = e * owners + q
+            source = gate_out.at[slot, :, q * channels : (q + 1) * channels]
+            own = pltpu.make_async_copy(source, gate_all.at[my_seq, s], own_sem.at[slot, 1 + q])
+            far = pltpu.make_async_remote_copy(
+                src_ref=source, dst_ref=gate_all.at[my_seq, s],
+                send_sem=gate_sent.at[slot, q], recv_sem=gate_got.at[my_seq],
+                device_id={"seq": owner}, device_id_type=MESH,
+            )
+            yield owner, own, far
+
+    def send(s, e, slot):
+        own, far = gated_copies(s, e, slot)
+        own.start()
+        for copy in far:
+            copy.start()
+        for owner, own, far in gate_copies(s, e, slot):
+            pl.when(owner == my_seq)(own.start)
+            pl.when(owner != my_seq)(far.start)
+
+    def drain(s, e, slot):
+        own, far = gated_copies(s, e, slot)
+        own.wait()
+        for copy in far:
+            copy.wait_send()
+        for owner, own, far in gate_copies(s, e, slot):
+            pl.when(owner == my_seq)(own.wait)
+            pl.when(owner != my_seq)(far.wait_send)
+
+    @pl.when(tick >= 2)
+    def _():
+        drain((tick - 2) // n_blocks, lax.rem(tick - 2, n_blocks), slot)
+
     history[0:states, :] = start_ref[0]
     drive[0] = d_ref[0] * act_ref[0].astype(F32)
+    gate_block = gate_ref[0]
+    up[0] = dg_ref[0] * (gate_block * jax.nn.sigmoid(gate_block))
+    sum_acc[...] = jnp.zeros_like(sum_acc)
 
     def rows_of(i):
         return pl.ds(pl.multiple_of(i * CHUNK, CHUNK), CHUNK)
@@ -207,8 +381,19 @@
         return pl.ds(pl.multiple_of((i * CHUNK + r) * states, states), states)
 
     def sum_y(i, low, part):
-        at = slice(part * span, (part + 1) * span)
-        y_ref[0, rows_of(i), at] = jnp.dot(c_diag[0, i], low[:, at], preferred_element_type=F32)
+        at, rows = slice(part * span, (part + 1) * span), rows_of(i)
+        produced = jnp.dot(c_diag[0, i], low[:, at], preferred_element_type=F32)
+        scanned = produced + skip_ref[:, at] * act_ref[0, rows, at].astype(F32)
+        gate = gate_ref[0, rows, at]
+        sigmoid = jax.nn.sigmoid(gate)
+        gated = (scanned * (gate * sigmoid)).astype(BF16)
+        slope = sigmoid * (1.0 + gate * (1.0 - sigmoid))
+        d_gate = (dg_ref[0, rows, at] * scanned * slope).astype(BF16)
+        gated_ref[0, rows, at] = gated
+        dgate_ref[0, rows, at] = d_gate
+        gated_out[slot, rows, at] = gated
+        if hosted:
+            gate_out[slot, rows, at] = d_gate
 
     def forward(i, h, low, before, low_before):
         rows = rows_of(i)
@@ -220,8 +405,10 @@
                 h[j] = h[j] * decay + spread_row(drive, rows, r, j, states) * b
                 history[kept(i, r + 1), column(j)] = h[j]
                 low[r * states : (r + 1) * states, column(j)] = h[j].astype(BF16)
-            if waiting and r % (CHUNK // parts) == 1:
+            if waiting and r % max(1, CHUNK // parts) == 1:
                 sum_y(before, low_before, waiting.pop(0))
+        for part in waiting:
+            sum_y(before, low_before, part)
         return h
 
     def forward_pair(pair, carry):
@@ -231,49 +418,60 @@
     lax.fori_loop(0, chunks // 2, forward_pair, tuple(start_ref[0, :, column(j)] for j in range(tiles)))
     for part in range(parts):
         sum_y(chunks - 1, low_b, part)
+    send(seg, block, slot)
 
     @pl.when(pl.program_id(1) == 0)
     def _():
-        db_ref[...] = jnp.zeros_like(db_ref)
-        dc_ref[...] = jnp.zeros_like(dc_ref)
-
-    def sum_back(i, low, through, part, which):
-        at = slice(part * span, (part + 1) * span)
-        if which == 0:
-            dv_ref[0, rows_of(i), at] = jnp.dot(b_diag[0, i], low[:, at], preferred_element_type=F32)
+        db_acc[...] = jnp.zeros_like(db_acc)
+        dc_acc[...] = jnp.zeros_like(dc_acc)
+
+    def sum_back(i, low, through, part, count=None):
+        at, rows = slice(part * span, (part + 1) * span), rows_of(i)
+        d_drive = jnp.dot(b_diag[0, i], low[:, at], preferred_element_type=F32)
+        d_rate = jnp.dot(ones_ref[...], through[:, at], preferred_element_type=F32)
+        delta, act, d_scanned = d_ref[0, rows, at], act_ref[0, rows, at].astype(F32), up[0, rows, at]
+        near = delta * (1.0 - delta * (0.5 - delta * (1.0 / 6.0 - delta * (1.0 / 24.0))))
+        slope = jnp.where(delta < 0.03, near, 1.0 - jnp.exp(-delta))
+        d_pre = (LN2 * d_rate + d_drive * act) * slope
+        dpre_ref[0, rows, at] = d_pre.astype(BF16)
+        dact_ref[0, rows, at] = skip_ref[:, at] * d_scanned + d_drive * delta
+        if count is None:
+            sum_acc[0, :, at] += d_pre
+            sum_acc[1, :, at] += d_scanned * act
         else:
-            dd_ref[0, rows_of(i), at] = jnp.dot(ones_ref[...], through[:, at], preferred_element_type=F32)
-
-    def backward(i, lam, da, low, through, before, low_before, through_before):
+            sum_acc[0, :, at] += jnp.where(count, d_pre, 0.0)
+            sum_acc[1, :, at] += jnp.where(count, d_scanned * act, 0.0)
+
+    def backward(i, lam, da, low, through, before, low_before, through_before, count=None):
         rows = rows_of(i)
-        waiting = [(part, which) for part in range(parts) for which in (0, 1)]
+        waiting = list(range(parts))
         for r in reversed(range(CHUNK)):
             c = c_ref[0, i * CHUNK + r]
             db = dc = None
             for j in range(tiles):
                 step = spread_row(d_ref, rows, r, j, states)
-                up = spread_row(dy_ref, rows, r, j, states)
-                adjoint = lam[j] + up * c
+                upstream = spread_row(up, rows, r, j, states)
+                adjoint = lam[j] + upstream * c
                 db_j = adjoint * spread_row(drive, rows, r, j, states)
-                dc_j = up * history[kept(i, r + 1), column(j)]
+                dc_j = upstream * history[kept(i, r + 1), column(j)]
                 db, dc = (db_j, dc_j) if db is None else (db + db_j, dc + dc_j)
                 low[r * states : (r + 1) * states, column(j)] = adjoint.astype(BF16)
                 lam[j] = adjoint * jnp.exp2(step * rate[j])
                 flow = lam[j] * history[kept(i, r), column(j)]
                 through[r * states : (r + 1) * states, column(j)] = (flow * rate[j]).astype(BF16)
                 da[j] = da[j] + flow * step
-            db_ref[0, i * CHUNK + r] += db
-            dc_ref[0, i * CHUNK + r] += dc
-            if waiting and (CHUNK - 1 - r) % max(1, CHUNK // (2 * parts)) == 1:
-                sum_back(before, low_before, through_before, *waiting.pop(0))
-        for item in waiting:
-            sum_back(before, low_before, through_before, *item)
+            db_acc[i * CHUNK + r] += db
+            dc_acc[i * CHUNK + r] += dc
+            if waiting and (CHUNK - 1 - r) % max(1, CHUNK // parts) == 1:
+                sum_back(before, low_before, through_before, waiting.pop(0), count)
+        for part in waiting:
+            sum_back(before, low_before, through_before, part, count)
         return lam, da
 
     def backward_pair(pair, carry):
         lam, da = (list(part) for part in carry)
         i = chunks - 1 - 2 * pair
-        lam, da = backward(i, lam, da, low_a, through_a, jnp.minimum(i + 1, chunks - 1), low_b, through_b)
+        lam, da = backward(i, lam, da, low_a, through_a, jnp.minimum(i + 1, chunks - 1), low_b, through_b, pair > 0)
         lam, da = backward(i - 1, lam, da, low_b, through_b, i, low_a, through_a)
         return tuple(lam), tuple(da)
 
@@ -282,45 +480,97 @@
         0, chunks // 2, backward_pair, (tuple(end_ref[0, :, column(j)] for j in range(tiles)), zeros)
     )
     for part in range(parts):
-        sum_back(0, low_b, through_b, part, 0)
-        sum_back(0, low_b, through_b, part, 1)
+        sum_back(0, low_b, through_b, part)
     for j in range(tiles):
         da_ref[0, :, column(j)] = da[j]
-
-
-def scan_both(delta, act, d_scanned, b_wide, c_wide, c_diag, b_diag, ones_diag, a_mat, start, end):
+    sums_ref[0, 0:1, :] = jnp.sum(sum_acc[0], axis=0, keepdims=True)
+    sums_ref[0, 1:2, :] = jnp.sum(sum_acc[1], axis=0, keepdims=True)
+    sums_ref[0, 2:8, :] = jnp.zeros((6, width), F32)
+
+    @pl.when(pl.program_id(1) == pl.num_programs(1) - 1)
+    def _():
+        db_ref[0] = jnp.sum(db_acc[...], axis=-1)
+        dc_ref[0] = jnp.sum(dc_acc[...], axis=-1)
+
+    @pl.when(tick == pl.num_programs(0) * n_blocks - 1)
+    def _():
+        drain((tick - 1) // n_blocks, lax.rem(tick - 1, n_blocks), 1 - slot)
+        drain(seg, block, slot)
+        for p in range(1, n_dp):
+            source = lax.rem(my_dp + p, n_dp)
+            pltpu.make_async_remote_copy(
+                src_ref=gated_all.at[source], dst_ref=gated_all.at[source],
+                send_sem=gated_sent.at[0, 0], recv_sem=gated_got.at[source],
+                device_id={"dp": source}, device_id_type=MESH,
+            ).wait_recv()
+        for p in range(1, n_seq if hosted else 1):
+            source = lax.rem(my_seq + p, n_seq)
+            pltpu.make_async_remote_copy(
+                src_ref=gate_all.at[source], dst_ref=gate_all.at[source],
+                send_sem=gate_sent.at[0, 0], recv_sem=gate_got.at[source],
+                device_id={"seq": source}, device_id_type=MESH,
+            ).wait_recv()
+
+
+def scan_both(delta, act, gate_in, d_gated, b_wide, c_wide, c_diag, b_diag, ones_diag, a_mat, d_skip, start, end):
     segs, length, inner = delta.shape
     states = a_mat.shape[0]
-    width = widest(inner, 1024)
+    width = widest(inner, 768)
     tokens = pl.BlockSpec((1, length, width), lambda s, e: (s, 0, e))
     wide = pl.BlockSpec((1, length, states, LANES), lambda s, e: (s, 0, 0, 0))
     diag = pl.BlockSpec((1,) + c_diag.shape[1:], lambda s, e: (s, 0, 0, 0))
     state = pl.BlockSpec((1, states, width), lambda s, e: (s, 0, e))
+    narrow = pl.BlockSpec((1, length, states), lambda s, e: (s, 0, 0))
     by_token = jax.ShapeDtypeStruct((segs, length, inner), F32)
-    by_lane = jax.ShapeDtypeStruct((segs, length, states, LANES), F32)
+    by_token_low = jax.ShapeDtypeStruct((segs, length, inner), BF16)
+    by_state = jax.ShapeDtypeStruct((segs, length, states), F32)
     low = pltpu.VMEM((CHUNK * states, width), BF16)
+    lanes = pltpu.VMEM((length, states, LANES), F32)
+    n_dp, n_seq = lax.axis_size("dp"), lax.axis_size("seq")
+    channels = inner // n_seq
+    hosted = channels % LANES == 0 and width % channels == 0
+    dma = pltpu.SemaphoreType.DMA
+    out = pltpu.VMEM((2, length, width), BF16)
     return pl.pallas_call(
-        scan_kernel,
+        functools.partial(scan_kernel, hosted, inner // width),
         grid=(segs, inner // width),
         in_specs=[
-            tokens, tokens, tokens, wide, wide, diag, diag,
+            tokens, tokens, tokens, tokens, wide, wide, diag, diag,
             pl.BlockSpec(ones_diag.shape, lambda s, e: (0, 0)),
             pl.BlockSpec((states, width), lambda s, e: (0, e)),
+            pl.BlockSpec((1, width), lambda s, e: (0, e)),
             state, state,
         ],
-        out_specs=[tokens, tokens, tokens, wide, wide, state],
-        out_shape=[by_token, by_token, by_token, by_lane, by_lane, jax.ShapeDtypeStruct((segs, states, inner), F32)],
+        out_specs=[
+            tokens, tokens, tokens, tokens, narrow, narrow, state,
+            pl.BlockSpec((1, 8, width), lambda s, e: (s, 0, e)),
+            pl.BlockSpec(memory_space=pl.ANY),
+            pl.BlockSpec(memory_space=pl.ANY),
+        ],
+        out_shape=[
+            by_token_low, by_token_low, by_token_low, by_token, by_state, by_state,
+            jax.ShapeDtypeStruct((segs, states, inner), F32),
+            jax.ShapeDtypeStruct((segs, 8, inner), F32),
+            jax.ShapeDtypeStruct((n_dp, segs, length, inner), BF16),
+            jax.ShapeDtypeStruct((n_seq, segs, length, channels), BF16),
+        ],
         scratch_shapes=[
             pltpu.VMEM(((length + 1) * states, width), F32),
             pltpu.VMEM((1, length, width), F32),
-            low, low, low, low,
+            pltpu.VMEM((1, length, width), F32),
+            low, low, low, low, lanes, lanes,
+            pltpu.VMEM((2, CHUNK, width), F32),
+            out, out,
+            dma((2, n_dp)), dma((n_dp,)), dma((2, n_seq)), dma((n_seq,)), dma((2, 1 + n_seq)),
         ],
-        compiler_params=pltpu.CompilerParams(vmem_limit_bytes=VMEM_BYTES),
+        compiler_params=pltpu.CompilerParams(
+            collective_id=2, has_side_effects=True, vmem_limit_bytes=VMEM_BYTES
+        ),
         cost_estimate=pl.CostEstimate(
-            flops=20 * delta.size * states, bytes_accessed=30 * delta.size, transcendentals=2 * delta.size * states
+            flops=20 * delta.size * states, bytes_accessed=24 * delta.size, transcendentals=2 * delta.size * states
         ),
         name="scan_both",
-    )(delta, act, d_scanned, b_wide, c_wide, c_diag, b_diag, ones_diag, a_mat, start, end)
+    )(delta, act, gate_in, d_gated, b_wide, c_wide, c_diag, b_diag, ones_diag, a_mat, d_skip[None], start, end)
 
 
 def diagonal_blocks(value):
@@ -354,7 +604,7 @@
     normed = (token_float * inverse * norm_gain).astype(BF16)
     cot = flat(cotangent)
     normed_all = lax.all_gather(normed, "seq", axis=0, tiled=True)
-    cot_all = lax.all_gather(cot, "seq", axis=0, tiled=True)
+    cot_columns = swap_columns(cot, "dp")
     conv_in = matmul(normed, in_proj[:, :inner]).astype(BF16)
     gate_in = matmul(normed, in_proj[:, inner:])
     d_gated = matmul_nt(cot, out_proj)
@@ -370,42 +620,31 @@
     pre_delta = matmul(dt_low, dt_proj) + dt_bias
     delta = split(jax.nn.softplus(pre_delta))
     a_mat = -jnp.exp(a_log)
-    gate_act, gate_slope = silu_parts(gate_in)
-    d_scanned = d_gated * gate_act
+    gate_in, d_gated = split(gate_in), split(d_gated)
 
     b_wide = jnp.broadcast_to(b_in[..., None], b_in.shape + (LANES,))
     c_wide = jnp.broadcast_to(c_in[..., None], c_in.shape + (LANES,))
-    ends, entry_mu = block_ends(delta, activated, split(d_scanned), b_wide, c_wide, a_mat)
+    ends, entry_mu = block_ends(delta, activated, gate_in, d_gated, b_wide, c_wide, a_mat)
     total = jnp.sum(delta, axis=1, keepdims=True)
-    start = carried(ends, total, entry_state, a_mat, "seq", 1)
-    end = carried(entry_mu, total, 0.0, a_mat, "seq", -1)
+    start, end = carry(ends, entry_mu, total, entry_state, a_mat)
     d_entry = from_first(entry_mu + jnp.exp(total * a_mat) * end, "seq")
     ones_diag = diagonal_blocks(jnp.ones((1, CHUNK, states), F32))[0, 0]
-    produced, d_drive, d_delta_scan, d_b, d_c, d_amat = scan_both(
-        delta, activated, split(d_scanned), b_wide, c_wide,
-        diagonal_blocks(c_in), diagonal_blocks(b_in), ones_diag, a_mat, start, end,
-    )
-    d_b = jnp.sum(flat(d_b), axis=-1)
-    d_c = jnp.sum(flat(d_c), axis=-1)
-    delta, act_float = flat(delta), flat(activated).astype(F32)
-    produced, d_drive, d_delta_scan = flat(produced), flat(d_drive), flat(d_delta_scan)
-
-    scanned = produced + d_skip * act_float
-    gated = (scanned * gate_act).astype(BF16)
-    d_gate = (d_gated * scanned * gate_slope).astype(BF16)
-    out_columns = swap_columns(gated, "seq")
-    gate_columns = swap_columns(d_gate, "seq")
+    gated, d_gate, d_pre_low, d_act, d_b, d_c, d_amat, sums, gated_all, gate_columns = scan_both(
+        delta, activated, gate_in, d_gated, b_wide, c_wide,
+        diagonal_blocks(c_in), diagonal_blocks(b_in), ones_diag, a_mat, d_skip, start, end,
+    )
+    gated, d_gate, d_pre_low, d_act = flat(gated), flat(d_gate), flat(d_pre_low), flat(d_act)
+    gated_all = gated_all.reshape(-1, inner)
+    gate_columns = gate_columns.reshape(n_seq * count, -1)
+    if (inner // n_seq) % LANES:
+        gate_columns = swap_columns(d_gate, "seq")
     output = token_float + matmul(gated, out_proj)
-    d_d_skip = jnp.sum(d_scanned * act_float, axis=0)
-
-    d_act = d_skip * d_scanned + d_drive * delta
-    d_delta = LN2 * d_delta_scan + d_drive * act_float
-    d_pre = d_delta * jax.nn.sigmoid(pre_delta)
-    d_dt_bias = jnp.sum(d_pre, axis=0)
-    d_pre_low = d_pre.astype(BF16)
+
+    sums = jnp.sum(sums, axis=0)
+    d_dt_bias, d_d_skip = sums[0], sums[1]
     d_dt_proj = matmul_tn(dt_low, d_pre_low)
     d_dt_low = matmul_nt(d_pre_low, dt_proj)
-    d_coeffs = jnp.concatenate([d_dt_low, d_b, d_c], axis=-1).astype(BF16)
+    d_coeffs = jnp.concatenate([d_dt_low, flat(d_b), flat(d_c)], axis=-1).astype(BF16)
     d_x_proj = matmul_tn(d_coeffs, flat(activated))
     d_a_log = jnp.sum(d_amat, axis=0) * a_mat
     d_act = split(d_act + matmul_nt(d_coeffs, x_proj))
@@ -415,11 +654,9 @@
     d_conv_weight = jnp.stack(
         [jnp.sum(d_conv_out * padded[:, tap : tap + length], axis=(0, 1)) for tap in range(taps)]
     )
-    head = jnp.pad(d_conv_out[:, :halo], ((0, 0), (0, halo), (0, 0)))
     halo_grad = sum(
         conv_weight[tap] * jnp.pad(d_conv_out[:, : halo - tap], ((0, 0), (tap, 0), (0, 0))) for tap in range(halo)
     )
-    del head
     returned = shifted(halo_grad, "seq", -1)
     tail = jnp.pad(d_conv_out, ((0, 0), (0, halo), (0, 0)))
     d_conv_in = sum(conv_weight[tap] * tail[:, halo - tap : halo - tap + length] for tap in range(taps))
@@ -427,26 +664,25 @@
     d_conv_in = flat(d_conv_in).astype(BF16)
     d_conv_state = from_first(halo_grad, "seq")
 
+    n_dp = lax.axis_size("dp")
     small = jnp.concatenate([d_x_proj, d_dt_proj, d_a_log, d_dt_bias[None], d_d_skip[None]], axis=0)
+    small = jnp.pad(small, ((0, -small.shape[0] % 16), (0, 0))).astype(BF16)
+    small_columns = swap_columns(small, "seq")
     edges = jnp.concatenate([d_conv_weight, d_conv_bias[None]], axis=0)
-
-    def pad_rows(value):
-        return jnp.pad(value, ((0, -value.shape[0] % (16 * lax.axis_size("dp"))), (0, 0))).astype(BF16)
-
-    def summed_small(value):
-        padded_rows = pad_rows(value)
-        parts = swap_columns(padded_rows, "seq").reshape(n_seq, padded_rows.shape[0], -1)
-        whole = sum_scatter_rows(jnp.sum(parts.astype(F32), axis=0), "dp")
-        return gather_rows(whole.astype(BF16), "dp").astype(F32)
-
-    small = summed_small(small)
-    conv_columns = swap_columns(d_conv_in, "seq")
-    edges = summed_small(edges)
-    out_part = sum_scatter_rows(matmul_tn(out_columns, cot_all), "dp")
-    d_out_proj = gather_rows(out_part.astype(BF16), "dp").astype(F32)
-
-    gate_part = sum_scatter_rows(matmul_tn(normed_all, gate_columns), "dp").astype(BF16)
-    conv_part = sum_scatter_rows(matmul_tn(normed_all, conv_columns), "dp").astype(BF16)
+    edges = jnp.pad(edges, ((0, -edges.shape[0] % 16), (0, 0))).astype(BF16)
+    conv_columns = swap_columns(jnp.concatenate([d_conv_in, edges], axis=0), "seq").reshape(n_seq, -1, inner // n_seq)
+    edge_columns = conv_columns[:, count:]
+    conv_columns = conv_columns[:, :count].reshape(n_seq * count, -1)
+
+    def blocks(value, axis):
+        return value.reshape((lax.axis_size(axis), -1) + value.shape[1:])
+
+    out_part = sum_scatter(blocks(matmul_tn(gated_all, cot_columns), "seq"), "seq")
+    d_out_proj = gather_rows(out_part.astype(BF16)[None], "dp").transpose(1, 0, 2).reshape(out_part.shape[0], -1)
+    d_out_proj = d_out_proj.astype(F32)
+
+    gate_part = sum_scatter(blocks(matmul_tn(normed_all, gate_columns), "dp"), "dp").astype(BF16)
+    conv_part = sum_scatter(blocks(matmul_tn(normed_all, conv_columns), "dp"), "dp").astype(BF16)
     half = n_seq // 2
     even = mine % 2 == 0
     straight = [(i, i // 2 + (0 if i % 2 == 0 else half)) for i in range(n_seq)]
@@ -468,8 +704,21 @@
         + inverse * scaled
         - token_float * cubed * jnp.mean(scaled * token_float, axis=-1, keepdims=True)
     )
-    gain_parts = swap_columns(d_norm_gain[None], "seq")
-    d_norm_gain = jnp.sum(gather_rows(jnp.sum(gain_parts, axis=0, keepdims=True), "dp"), axis=0)
+    gain = sum_scatter(blocks(d_norm_gain, "seq"), "seq")
+    channels = inner // n_seq
+    per_device = jnp.concatenate(
+        [
+            jnp.sum(small_columns.reshape(n_seq, -1, channels).astype(F32), axis=0),
+            jnp.sum(edge_columns.astype(F32), axis=0),
+            jnp.pad(gain, (0, -gain.shape[0] % channels)).reshape(-1, channels),
+        ],
+        axis=0,
+    )
+    per_device = per_device.astype(BF16)
+    summed = jnp.sum(gather_rows(per_device[None], "dp").astype(F32), axis=0)
+    edges = summed[small.shape[0] : small.shape[0] + edges.shape[0]]
+    d_norm_gain = summed[small.shape[0] + edges.shape[0] :].reshape(-1)[: gain.shape[0]]
+    small = summed
 
     return (
         split(output),

time: 998 us -> 767 us (0.77)
  the two profiles are of different devices: /device:TPU:1 before, /device:TPU:24 now
where the time goes in v2:
time: 767 us; the launch traced here: 759 us
  Pallas kernels  216 us (28%)
  local copies, waits for them, and re-layouts  159 us (21%)
  waiting for transfers between devices  118 us (15%)
  matrix products  104 us (14%)
  starting transfers between devices  75.3 us (10%)
  other arithmetic  70.9 us (9%)
  between operations  16.1 us (2%)
    pallas_call x1, Pallas kernels, scan_both(): pl.pallas_call(functools.partial(scan_kernel, hosted, inner // width), gr...  148 us
    dynamic_update_slice x10, local copies, waits for them, and re-layouts, gather_rows(): lax.dynamic_update_slice_in_dim(gathered, piece, source * rows, 0)  51.8 us
    ppermute x10, waiting for transfers between devices, sum_scatter(): lax.ppermute(sent, axis, [(i, i ^ 1 << level) for i in range(count)])  47.7 us
    ppermute x17, waiting for transfers between devices, swap_columns(): piece = lax.ppermute(piece, axis, partner_route(axis, step))  44 us
    pallas_call x1, Pallas kernels, block_ends(): pl.pallas_call(ends_kernel, grid=(segs, inner // width), in_specs=[tokens...  41.3 us
    dot_general x5, matrix products, matmul_nt(): lax.dot_general(left, right, (((1,), (1,)), ((), ())), preferred_element_...  38.2 us
    dot_general x5, matrix products, matmul(): lax.dot_general(left, right, (((1,), (0,)), ((), ())), preferred_element_...  36.9 us
    ppermute x17, starting transfers between devices, swap_columns(): piece = lax.ppermute(piece, axis, partner_route(axis, step))  35.8 us
  transfers between devices with their start and end apart: 47, of which 11 were waited for; matrix products, arithmetic and copies ran while one was open for 41% of the time, Pallas kernels for 29%

profile of v2, /device:TPU:24, one launch (start us, length us, event | category | flops | bytes accessed | tf_op | source)
XLA Modules:
  0.0 758.7 jit_solution(18324826611846552122)
XLA Ops:
  12.2 8.2 %fusion.13 = bf16[512,3072]{1,0:T(8,128)(2,1)S(1)} fusion(bf16[512,1536]{1,0:T(8,128)(2,1)} %fusion.28, bf16[1536,6144]{1,0:T(8,128)(2,1)} %param.18), kind=kOutput, calls=%fused_computation.26 | convolution fusion | flops 4833411072 | bytes 14155776 | tf_op jit(solution)/shard_map/dot_general | solution.py:27
  24.9 11.2 %fusion.2.gate_ref = f32[4,128,3072]{2,1,0:T(8,128)} fusion(bf16[1536,6144]{1,0:T(8,128)(2,1)} %param.18, bf16[4,128,1536]{2,1,0:T(8,128)(2,1)S(1)} %copy-done.15, f32[1536]{0:T(1024)S(1)} %copy-done.49, f32[4,128]{1,0:T(4,128)S(1)} %get-tuple-element.190), kind=kOutput, calls=%fused_computation.3 | convolution fusion | flops 4834983936 | bytes 17309696 | tf_op jit(solution)/shard_map/dot_general | solution.py:27
  37.6 11.1 %fusion.dg_ref = f32[4,128,3072]{2,1,0:T(8,128)} fusion(bf16[4,128,1536]{2,1,0:T(8,128)(2,1)} %param.27, bf16[3072,1536]{1,0:T(8,128)(2,1)} %param.26), kind=kOutput, calls=%fused_computation.1 | convolution fusion | flops 4831838208 | bytes 17301504 | tf_op jit(solution)/shard_map/dot_general | solution.py:31
  54.5 5.8 multiply_convert_fusion
  63.5 6.8 bitcast_reduce_fusion.1
  88.6 41.3 %block_ends.1 = (f32[4,16,3072]{2,1,0:T(8,128)}, f32[4,16,3072]{2,1,0:T(8,128)}) custom-call(f32[4,128,3072]{2,1,0:T(8,128)} %bitcast.219, bf16[4,128,3072]{2,1,0:T(8,128)(2,1)} %copy-done.12, f32[4,128,3072]{2,1,0:T(8,128)} %fusion.2.gate_ref, f32[4,128,3072]{2,1,0:T(8,128)} %fusion.dg_ref, f32[4,128,16,128]{3,2,1,0:T(8,128)} %broadcast_in_dim.48.b_ref, ...), custom_call_target="tpu_custom_call" | custom-call | flops 226492416 | bytes 18874368 | tf_op jit(solution)/shard_map/block_ends/pallas_call | solution.py:280
  132.1 27.0 %carry.1 = (f32[4,16,3072]{2,1,0:T(8,128)S(1)}, f32[4,16,3072]{2,1,0:T(8,128)S(1)}) custom-call(f32[4,16,3072]{2,1,0:T(8,128)S(1)} %copy-done.9, f32[4,16,3072]{2,1,0:T(8,128)S(1)} %copy-done.2, f32[4,1,3072]{2,1,0:T(1,128)S(1)} %broadcast_in_dim.52.total_ref, f32[4,16,3072]{2,1,0:T(8,128)S(1)} %copy-done.6, f32[16,3072]{1,0:T(8,128)S(1)} %copy-done.4), custom_call_target="tpu_custom_call" | custom-call | tf_op jit(solution)/shard_map/carry/pallas_call | solution.py:214
  161.0 148.0 %scan_both.1 = (bf16[4,128,3072]{2,1,0:T(8,128)(2,1)}, bf16[4,128,3072]{2,1,0:T(8,128)(2,1)}, bf16[4,128,3072]{2,1,0:T(8,128)(2,1)}, f32[4,128,3072]{2,1,0:T(8,1...) custom-call(f32[4,128,3072]{2,1,0:T(8,128)} %bitcast.220, ...), custom_call_target="tpu_custom_call" | custom-call | flops 503316480 | bytes 37748736 | tf_op jit(solution)/shard_map/scan_both/pallas_call | solution.py:534
  314.3 4.0 bitcast_add_fusion
  318.8 6.9 multiply_reduce_fusion
  333.0 17.1 %copy.227 = bf16[3072,2048]{1,0:T(8,128)(2,1)} copy(bf16[3072,2048]{0,1:T(8,128)(2,1)} %bitcast.181) | data formatting | bytes 25165824 | tf_op jit(solution)/shard_map/dot_general | solution.py:35
  361.1 9.6 %convolution_add_fusion = f32[512,1536]{1,0:T(8,128)} fusion(bf16[512,3072]{1,0:T(8,128)(2,1)S(1)} %bitcast.224, bf16[3072,1536]{1,0:T(8,128)(2,1)} %param.26, bf16[512,1536]{1,0:T(8,128)(2,1)S(1)} %bitcast.176), kind=kOutput, calls=%fused_computation.32 | convolution fusion | flops 4833411072 | bytes 17301504 | tf_op jit(solution)/shard_map/dot_general | solution.py:27
  370.8 9.3 %fusion.4 = f32[512,1536]{1,0:T(8,128)} fusion(bf16[512,3072]{1,0:T(8,128)(2,1)S(1)} %bitcast.223, bf16[1536,6144]{1,0:T(8,128)(2,1)} %param.18), kind=kOutput, calls=%fused_computation.5 | convolution fusion | flops 4831838208 | bytes 15728640 | tf_op jit(solution)/shard_map/dot_general | solution.py:31
  381.9 10.5 %add_convert_fusion = bf16[4,128,3072]{2,1,0:T(8,128)(2,1)S(1)} fusion(f32[4,3,3072]{2,1,0:T(4,128)} %collective-permute-done.1, f32[4,128,3072]{2,1,0:T(8,128)} %get-tuple-element.155, f32[3072]{0:T(1024)S(1)} %bitcast.214, f32[3072]{0:T(1024)S(1)} %bitcast.212, f32[3072]{0:T(1024)S(1)} %bitcast.209, f32[3072]{0:T(1024)S(1)} %bitcast.206), kind=kLoop, calls=%fused_computation.19 | loop fusion | flops 14155776 | bytes 9633792 | tf_op jit(solution)/shard_map/convert_element_type | solution.py:664
  392.4 10.7 %fusion.33 = (f32[1536]{0:T(1024)S(1)}, f32[512]{0:T(512)S(1)}, f32[512,1536]{1,0:T(8,128)}) fusion(bf16[4,128,1536]{2,1,0:T(8,128)(2,1)S(1)} %copy-done.16, f32[512]{0:T(512)S(1)} %copy-done.57, f32[1536]{0:T(1024)S(1)} %copy-done.50, f32[512,1536]{1,0:T(8,128)S(1)} %copy-done.63, bf16[512,3072]{1,0:T(8,128)(2,1)S(1)} %bitcast.184, ...), kind=kOutput, calls=%fused_computation.53 | convolution fusion | flops 4838127616 | bytes 20463616 | tf_op jit(solution)/shard_map/dot_general | solution.py:31
  433.6 8.8 %collective-permute-done.12 = bf16[256,384]{1,0:T(8,128)(2,1)S(1)} collective-permute-done((bf16[256,384]{1,0:T(8,128)(2,1)}, bf16[256,384]{1,0:T(8,128)(2,1)S(1)}, u32[]{:S(2)}, u32[]{:S(2)}) %collective-permute-start.12) | collective-permute-done | bytes 196640 | tf_op jit(solution)/shard_map/ppermute | solution.py:60
  451.5 5.2 collective-permute-start.16
  459.2 7.8 %collective-permute-start.18 = (bf16[528,384]{1,0:T(8,128)(2,1)}, bf16[528,384]{1,0:T(8,128)(2,1)}, u32[]{:S(2)}, u32[]{:S(2)}) collective-permute-start(bf16[528,384]{1,0:T(8,128)(2,1)} %get-tuple-element.161), channel_id=1, source_target_pairs={{0,4},{1,5},{2,6},{3,7},{4,0},{5,1},{6,2},{7,3},{8,12},{9,13},{10,... | collective-permute-start | bytes 1216520 | tf_op jit(solution)/shard_map/ppermute | solution.py:60
  469.5 8.7 %fusion.38 = f32[2,2,2,384,384]{3,4,2,1,0:T(8,128)S(1)} fusion(bf16[2,2,2,384,2048]{4,3,2,1,0:T(8,128)(2,1)} %bitcast.180, bf16[2048,384]{0,1:T(8,128)(2,1)} %copy-done.32), kind=kOutput, calls=%fused_computation.61 | convolution fusion | flops 4831838208 | bytes 18874368 | tf_op jit(solution)/shard_map/dot_general | solution.py:35
  484.3 7.1 collective-permute-start.21
  495.3 35.2 %collective-permute-done.19 = bf16[528,384]{1,0:T(8,128)(2,1)S(1)} collective-permute-done((bf16[528,384]{1,0:T(8,128)(2,1)S(1)}, bf16[528,384]{1,0:T(8,128)(2,1)S(1)}, u32[]{:S(2)}, u32[]{:S(2)}) %collective-permute-start.19) | collective-permute-done | bytes 405536 | tf_op jit(solution)/shard_map/ppermute | solution.py:60
  535.4 16.7 %collective-permute-done.4 = f32[4,3,3072]{2,1,0:T(4,128)} collective-permute-done((f32[4,3,3072]{2,1,0:T(4,128)}, f32[4,3,3072]{2,1,0:T(4,128)}, u32[]{:S(2)}, u32[]{:S(2)}) %collective-permute-start.4) | collective-permute-done | bytes 147488 | tf_op jit(solution)/shard_map/ppermute | solution.py:102
  558.2 7.7 %collective-permute-done.27 = bf16[1,273,384]{1,2,0:T(8,128)(2,1)S(1)} collective-permute-done((bf16[1,273,384]{1,2,0:T(8,128)(2,1)S(1)}, bf16[1,273,384]{1,2,0:T(8,128)(2,1)S(1)}, u32[]{:S(2)}, u32[]{:S(2)}) %collective-permute-start.27) | collective-permute-done | bytes 209696 | tf_op jit(solution)/shard_map/ppermute | solution.py:86
  574.2 16.8 %copy.247 = bf16[1536,4096]{1,0:T(8,128)(2,1)} copy(bf16[1536,4096]{0,1:T(8,128)(2,1)} %bitcast.179) | data formatting | bytes 25165824 | tf_op jit(solution)/shard_map/dot_general | solution.py:35
  591.0 11.0 %fusion.69 = f32[2,2,384,384]{3,2,1,0:T(8,128)S(1)} fusion(bf16[2,2,384,4096]{3,2,1,0:T(8,128)(2,1)} %bitcast.182, bf16[4096,384,1,1]{1,0,3,2:T(8,128)(2,1)} %bitcast.222), kind=kOutput, calls=%fused_computation.194 | convolution fusion | flops 4831838208 | bytes 18087936 | tf_op jit(solution)/shard_map/dot_general | solution.py:35
  603.0 6.7 fusion.68
  619.8 8.5 %collective-permute-done.28 = bf16[2,384,384]{2,1,0:T(8,128)(2,1)S(1)} collective-permute-done((bf16[2,384,384]{2,1,0:T(8,128)(2,1)S(1)}, bf16[2,384,384]{2,1,0:T(8,128)(2,1)S(1)}, u32[]{:S(2)}, u32[]{:S(2)}) %collective-permute-start.28) | collective-permute-done | bytes 589856 | tf_op jit(solution)/shard_map/ppermute | solution.py:75
  640.8 29.7 %collective-permute-done.42 = bf16[384,384]{0,1:T(8,128)(2,1)} collective-permute-done((bf16[384,384]{0,1:T(8,128)(2,1)S(1)}, bf16[384,384]{0,1:T(8,128)(2,1)}, u32[]{:S(2)}, u32[]{:S(2)}) %collective-permute-start.42) | collective-permute-done | bytes 294944 | tf_op jit(solution)/shard_map/ppermute | solution.py:75
  687.7 12.1 %dynamic_update_slice.124 = bf16[4,384,384]{2,0,1:T(4,128)(2,1)} dynamic-update-slice(bf16[4,384,384]{2,0,1:T(4,128)(2,1)} %broadcast_in_dim.57, bf16[1,384,384]{2,0,1:T(2,128)(2,1)S(1)} %copy.232, s32[]{:T(128)S(6)} %select_n.296, s32[]{:T(128)} %constant.104.clone.1, s32[]{:T(128)} %constant.104.clone.1) | dynamic-update-slice | bytes 589828 | tf_op jit(solution)/shard_map/dynamic_update_slice | solution.py:87
  702.0 12.1 %dynamic_update_slice.125 = bf16[4,384,384]{2,0,1:T(4,128)(2,1)} dynamic-update-slice(bf16[4,384,384]{2,0,1:T(4,128)(2,1)} %dynamic_update_slice.124, bf16[1,384,384]{2,0,1:T(2,128)(2,1)S(1)} %copy.233, s32[]{:T(128)S(6)} %select_n.297, s32[]{:T(128)} %constant.104.clone.1, s32[]{:T(128)} %constant.104.clone.1) | dynamic-update-slice | bytes 589828 | tf_op jit(solution)/shard_map/dynamic_update_slice | solution.py:87
  716.2 12.1 %dynamic_update_slice.126 = bf16[4,384,384]{2,0,1:T(4,128)(2,1)} dynamic-update-slice(bf16[4,384,384]{2,0,1:T(4,128)(2,1)} %dynamic_update_slice.125, bf16[1,384,384]{2,0,1:T(2,128)(2,1)S(1)} %copy.234, s32[]{:T(128)S(6)} %select_n.298, s32[]{:T(128)} %constant.104.clone.1, s32[]{:T(128)} %constant.104.clone.1) | dynamic-update-slice | bytes 589828 | tf_op jit(solution)/shard_map/dynamic_update_slice | solution.py:87
  730.5 12.1 %dynamic_update_slice.127 = bf16[4,384,384]{2,0,1:T(4,128)(2,1)} dynamic-update-slice(bf16[4,384,384]{2,0,1:T(4,128)(2,1)} %dynamic_update_slice.126, bf16[1,384,384]{2,0,1:T(2,128)(2,1)S(1)} %copy.235, s32[]{:T(128)S(6)} %select_n.299, s32[]{:T(128)} %constant.104.clone.1, s32[]{:T(128)} %constant.104.clone.1) | dynamic-update-slice | bytes 589828 | tf_op jit(solution)/shard_map/dynamic_update_slice | solution.py:87
  (386 shorter events, 196.9 us)
Async XLA Ops:
  7.2 567.0 %all-gather.2.cloned.1.call-start = ((), (), s32[]{:S(2)}) async-start(), calls=%async_computation | async-start | bytes 14155776 | tf_op jit(solution)/shard_map/all_gather | solution.py:606
  22.1 28.2 %collective-permute-start = (bf16[4,3,3072]{2,1,0:T(4,128)(2,1)S(1)}, bf16[4,3,3072]{2,1,0:T(4,128)(2,1)S(1)}, u32[]{:S(2)}, u32[]{:S(2)}) collective-permute-start(bf16[4,3,3072]{2,1,0:T(4,128)(2,1)S(1)} %slice.151), channel_id=1, source_target_pairs={{0,1},{1,2},{2,3},{3,4},{4,5},{5,6},{6,7},{8,9},{9,10},{10,11},{11... | collective-permute-start | bytes 221192 | tf_op jit(solution)/shard_map/ppermute | solution.py:94
  329.7 51.1 %collective-permute-start.1 = (f32[4,3,3072]{2,1,0:T(4,128)}, f32[4,3,3072]{2,1,0:T(4,128)}, u32[]{:S(2)}, u32[]{:S(2)}) collective-permute-start(f32[4,3,3072]{2,1,0:T(4,128)} %fusion.54), channel_id=1, source_target_pairs={{1,0},{2,1},{3,2},{4,3},{5,4},{6,5},{7,6},{9,8},{10,9},{11,10},{12... | collective-permute-start | bytes 442376 | tf_op jit(solution)/shard_map/ppermute | solution.py:94
  331.6 77.4 %collective-permute-start.2 = (f32[4,3,3072]{2,1,0:T(4,128)}, f32[4,3,3072]{2,1,0:T(4,128)}, u32[]{:S(2)}, u32[]{:S(2)}) collective-permute-start(f32[4,3,3072]{2,1,0:T(4,128)} %fusion.54), channel_id=1, source_target_pairs={{0,1},{8,9},{16,17},{24,25}} | collective-permute-start | bytes 442376 | tf_op jit(solution)/shard_map/ppermute | solution.py:102
  357.6 64.3 %collective-permute-start.8 = (bf16[256,384]{1,0:T(8,128)(2,1)}, bf16[256,384]{1,0:T(8,128)(2,1)}, u32[]{:S(2)}, u32[]{:S(2)}) collective-permute-start(bf16[256,384]{1,0:T(8,128)(2,1)} %get-tuple-element.176), channel_id=1, source_target_pairs={{0,1},{1,0},{2,3},{3,2},{4,5},{5,4},{6,7},{7,6},{8,9},{9,8},{10,11... | collective-permute-start | bytes 589832 | tf_op jit(solution)/shard_map/ppermute | solution.py:60
  358.7 65.1 %collective-permute-start.9 = (bf16[256,384]{1,0:T(8,128)(2,1)}, bf16[256,384]{1,0:T(8,128)(2,1)}, u32[]{:S(2)}, u32[]{:S(2)}) collective-permute-start(bf16[256,384]{1,0:T(8,128)(2,1)} %get-tuple-element.175), channel_id=1, source_target_pairs={{0,2},{1,3},{2,0},{3,1},{4,6},{5,7},{6,4},{7,5},{8,10},{9,11},{10,... | collective-permute-start | bytes 589832 | tf_op jit(solution)/shard_map/ppermute | solution.py:60
  358.7 70.8 %collective-permute-start.10 = (bf16[256,384]{1,0:T(8,128)(2,1)}, bf16[256,384]{1,0:T(8,128)(2,1)}, u32[]{:S(2)}, u32[]{:S(2)}) collective-permute-start(bf16[256,384]{1,0:T(8,128)(2,1)} %get-tuple-element.174), channel_id=1, source_target_pairs={{0,3},{1,2},{2,1},{3,0},{4,7},{5,6},{6,5},{7,4},{8,11},{9,10},{10,... | collective-permute-start | bytes 589832 | tf_op jit(solution)/shard_map/ppermute | solution.py:60
  380.8 51.2 %collective-permute-start.11 = (bf16[256,384]{1,0:T(8,128)(2,1)}, bf16[256,384]{1,0:T(8,128)(2,1)}, u32[]{:S(2)}, u32[]{:S(2)}) collective-permute-start(bf16[256,384]{1,0:T(8,128)(2,1)} %get-tuple-element.173), channel_id=1, source_target_pairs={{0,4},{1,5},{2,6},{3,7},{4,0},{5,1},{6,2},{7,3},{8,12},{9,13},{10,... | collective-permute-start | bytes 589832 | tf_op jit(solution)/shard_map/ppermute | solution.py:60
  432.0 25.9 %collective-permute-start.38 = (bf16[512,384]{1,0:T(8,128)(2,1)}, bf16[512,384]{1,0:T(8,128)(2,1)}, u32[]{:S(2)}, u32[]{:S(2)}) collective-permute-start(bf16[512,384]{1,0:T(8,128)(2,1)} %get-tuple-element.167), channel_id=1, source_target_pairs={{0,16},{8,24},{16,0},{24,8},{1,17},{9,25},{17,1},{25,9},{2,18},{10... | collective-permute-start | bytes 1179656 | tf_op jit(solution)/shard_map/ppermute | solution.py:60
  444.6 123.3 %collective-permute-start.5 = (f32[4,16,3072]{2,1,0:T(8,128)}, f32[4,16,3072]{2,1,0:T(8,128)}, u32[]{:S(2)}, u32[]{:S(2)}) collective-permute-start(f32[4,16,3072]{2,1,0:T(8,128)} %multiply_add_fusion), channel_id=1, source_target_pairs={{0,1},{8,9},{16,17},{24,25}} | collective-permute-start | bytes 2359304 | tf_op jit(solution)/shard_map/ppermute | solution.py:102
  449.7 29.7 %collective-permute-start.15 = (bf16[528,384]{1,0:T(8,128)(2,1)}, bf16[528,384]{1,0:T(8,128)(2,1)}, u32[]{:S(2)}, u32[]{:S(2)}) collective-permute-start(bf16[528,384]{1,0:T(8,128)(2,1)} %get-tuple-element.164), channel_id=1, source_target_pairs={{0,1},{1,0},{2,3},{3,2},{4,5},{5,4},{6,7},{7,6},{8,9},{9,8},{10,11... | collective-permute-start | bytes 1216520 | tf_op jit(solution)/shard_map/ppermute | solution.py:60
  451.5 29.3 %collective-permute-start.16 = (bf16[528,384]{1,0:T(8,128)(2,1)}, bf16[528,384]{1,0:T(8,128)(2,1)}, u32[]{:S(2)}, u32[]{:S(2)}) collective-permute-start(bf16[528,384]{1,0:T(8,128)(2,1)} %get-tuple-element.163), channel_id=1, source_target_pairs={{0,2},{1,3},{2,0},{3,1},{4,6},{5,7},{6,4},{7,5},{8,10},{9,11},{10,... | collective-permute-start | bytes 1216520 | tf_op jit(solution)/shard_map/ppermute | solution.py:60
  457.9 26.3 %collective-permute-start.17 = (bf16[528,384]{1,0:T(8,128)(2,1)}, bf16[528,384]{1,0:T(8,128)(2,1)}, u32[]{:S(2)}, u32[]{:S(2)}) collective-permute-start(bf16[528,384]{1,0:T(8,128)(2,1)} %get-tuple-element.162), channel_id=1, source_target_pairs={{0,3},{1,2},{2,1},{3,0},{4,7},{5,6},{6,5},{7,4},{8,11},{9,10},{10,... | collective-permute-start | bytes 1216520 | tf_op jit(solution)/shard_map/ppermute | solution.py:60
  459.2 33.3 %collective-permute-start.18 = (bf16[528,384]{1,0:T(8,128)(2,1)}, bf16[528,384]{1,0:T(8,128)(2,1)}, u32[]{:S(2)}, u32[]{:S(2)}) collective-permute-start(bf16[528,384]{1,0:T(8,128)(2,1)} %get-tuple-element.161), channel_id=1, source_target_pairs={{0,4},{1,5},{2,6},{3,7},{4,0},{5,1},{6,2},{7,3},{8,12},{9,13},{10,... | collective-permute-start | bytes 1216520 | tf_op jit(solution)/shard_map/ppermute | solution.py:60
  479.4 51.0 %collective-permute-start.19 = (bf16[528,384]{1,0:T(8,128)(2,1)S(1)}, bf16[528,384]{1,0:T(8,128)(2,1)S(1)}, u32[]{:S(2)}, u32[]{:S(2)}) collective-permute-start(bf16[528,384]{1,0:T(8,128)(2,1)S(1)} %copy-done.40), channel_id=1, source_target_pairs={{0,5},{1,4},{2,7},{3,6},{4,1},{5,0},{6,3},{7,2},{8,13},{9,12},{10,... | collective-permute-start | bytes 1216520 | tf_op jit(solution)/shard_map/ppermute | solution.py:60
  480.8 49.8 %collective-permute-start.20 = (bf16[528,384]{1,0:T(8,128)(2,1)S(1)}, bf16[528,384]{1,0:T(8,128)(2,1)S(1)}, u32[]{:S(2)}, u32[]{:S(2)}) collective-permute-start(bf16[528,384]{1,0:T(8,128)(2,1)S(1)} %copy-done.39), channel_id=1, source_target_pairs={{0,6},{1,7},{2,4},{3,5},{4,2},{5,3},{6,0},{7,1},{8,14},{9,15},{10,... | collective-permute-start | bytes 1216520 | tf_op jit(solution)/shard_map/ppermute | solution.py:60
  484.3 46.5 %collective-permute-start.21 = (bf16[528,384]{1,0:T(8,128)(2,1)S(1)}, bf16[528,384]{1,0:T(8,128)(2,1)S(1)}, u32[]{:S(2)}, u32[]{:S(2)}) collective-permute-start(bf16[528,384]{1,0:T(8,128)(2,1)S(1)} %copy-done.38), channel_id=1, source_target_pairs={{0,7},{1,6},{2,5},{3,4},{4,3},{5,2},{6,1},{7,0},{8,15},{9,14},{10,... | collective-permute-start | bytes 1216520 | tf_op jit(solution)/shard_map/ppermute | solution.py:60
  492.5 59.7 %collective-permute-start.4 = (f32[4,3,3072]{2,1,0:T(4,128)}, f32[4,3,3072]{2,1,0:T(4,128)}, u32[]{:S(2)}, u32[]{:S(2)}) collective-permute-start(f32[4,3,3072]{2,1,0:T(4,128)} %broadcast_select_fusion.8), channel_id=1, source_target_pairs={{0,4},{1,5},{2,6},{3,7},{8,12},{9,13},{10,14},{11,15},{16,20},{17,... | collective-permute-start | bytes 442376 | tf_op jit(solution)/shard_map/ppermute | solution.py:102
  530.4 41.2 %collective-permute-start.40 = (bf16[2,2,384,384]{2,3,1,0:T(8,128)(2,1)}, bf16[2,2,384,384]{2,3,1,0:T(8,128)(2,1)}, u32[]{:S(2)}, u32[]{:S(2)}) collective-permute-start(bf16[2,2,384,384]{2,3,1,0:T(8,128)(2,1)} %fusion.42), channel_id=1, source_target_pairs={{0,1},{1,0},{2,3},{3,2},{4,5},{5,4},{6,7},{7,6},{8,9},{9,8},{10,11... | collective-permute-start | bytes 3538952 | tf_op jit(solution)/shard_map/ppermute | solution.py:75
  532.7 25.4 %collective-permute-start.25 = (bf16[1,273,384]{1,2,0:T(8,128)(2,1)S(1)}, bf16[1,273,384]{1,2,0:T(8,128)(2,1)S(1)}, u32[]{:S(2)}, u32[]{:S(2)}) collective-permute-start(bf16[1,273,384]{1,2,0:T(8,128)(2,1)S(1)} %get-tuple-element.154), channel_id=1, source_target_pairs={{0,8},{8,0},{16,24},{24,16},{1,9},{9,1},{17,25},{25,17},{2,10},{10... | collective-permute-start | bytes 629000 | tf_op jit(solution)/shard_map/ppermute | solution.py:86
  534.2 24.0 %collective-permute-start.26 = (bf16[1,273,384]{1,2,0:T(8,128)(2,1)S(1)}, bf16[1,273,384]{1,2,0:T(8,128)(2,1)S(1)}, u32[]{:S(2)}, u32[]{:S(2)}) collective-permute-start(bf16[1,273,384]{1,2,0:T(8,128)(2,1)S(1)} %get-tuple-element.154), channel_id=1, source_target_pairs={{0,16},{8,24},{16,0},{24,8},{1,17},{9,25},{17,1},{25,9},{2,18},{10... | collective-permute-start | bytes 629000 | tf_op jit(solution)/shard_map/ppermute | solution.py:86
  570.0 41.0 %collective-permute-start.6 = (f32[4,16,3072]{2,1,0:T(8,128)}, f32[4,16,3072]{2,1,0:T(8,128)}, u32[]{:S(2)}, u32[]{:S(2)}) collective-permute-start(f32[4,16,3072]{2,1,0:T(8,128)} %broadcast_select_fusion), channel_id=1, source_target_pairs={{0,2},{1,3},{8,10},{9,11},{16,18},{17,19},{24,26},{25,27}} | collective-permute-start | bytes 2359304 | tf_op jit(solution)/shard_map/ppermute | solution.py:102
  573.2 56.3 %collective-permute-start.41 = (bf16[2,384,384]{1,2,0:T(8,128)(2,1)S(1)}, bf16[2,384,384]{1,2,0:T(8,128)(2,1)}, u32[]{:S(2)}, u32[]{:S(2)}) collective-permute-start(bf16[2,384,384]{1,2,0:T(8,128)(2,1)S(1)} %fusion.44), channel_id=1, source_target_pairs={{0,2},{1,3},{2,0},{3,1},{4,6},{5,7},{6,4},{7,5},{8,10},{9,11},{10,... | collective-permute-start | bytes 1769480 | tf_op jit(solution)/shard_map/ppermute | solution.py:75
  613.1 65.6 %collective-permute-start.7 = (f32[4,16,3072]{2,1,0:T(8,128)}, f32[4,16,3072]{2,1,0:T(8,128)}, u32[]{:S(2)}, u32[]{:S(2)}) collective-permute-start(f32[4,16,3072]{2,1,0:T(8,128)} %broadcast_select_fusion.1), channel_id=1, source_target_pairs={{0,4},{1,5},{2,6},{3,7},{8,12},{9,13},{10,14},{11,15},{16,20},{17,... | collective-permute-start | bytes 2359304 | tf_op jit(solution)/shard_map/ppermute | solution.py:102
  631.7 38.9 %collective-permute-start.42 = (bf16[384,384]{0,1:T(8,128)(2,1)S(1)}, bf16[384,384]{0,1:T(8,128)(2,1)}, u32[]{:S(2)}, u32[]{:S(2)}) collective-permute-start(bf16[384,384]{0,1:T(8,128)(2,1)S(1)} %fusion.51), channel_id=1, source_target_pairs={{0,4},{1,5},{2,6},{3,7},{4,0},{5,1},{6,2},{7,3},{8,12},{9,13},{10,... | collective-permute-start | bytes 884744 | tf_op jit(solution)/shard_map/ppermute | solution.py:75
  635.6 38.7 %collective-permute-start.33 = (bf16[384,384]{1,0:T(8,128)(2,1)S(1)}, bf16[384,384]{1,0:T(8,128)(2,1)}, u32[]{:S(2)}, u32[]{:S(2)}) collective-permute-start(bf16[384,384]{1,0:T(8,128)(2,1)S(1)} %broadcast_select_fusion.3), channel_id=1, source_target_pairs={{0,4},{1,0},{2,5},{3,1},{4,6},{5,2},{6,7},{7,3},{8,12},{9,8},{10,1... | collective-permute-start | bytes 884744 | tf_op jit(solution)/shard_map/ppermute | solution.py:691
  635.6 39.5 %collective-permute-start.32 = (bf16[384,384]{1,0:T(8,128)(2,1)S(1)}, bf16[384,384]{1,0:T(8,128)(2,1)}, u32[]{:S(2)}, u32[]{:S(2)}) collective-permute-start(bf16[384,384]{1,0:T(8,128)(2,1)S(1)} %get-tuple-element.150), channel_id=1, source_target_pairs={{0,0},{1,4},{2,1},{3,5},{4,2},{5,6},{6,3},{7,7},{8,8},{9,12},{10,9... | collective-permute-start | bytes 884744 | tf_op jit(solution)/shard_map/ppermute | solution.py:690
  673.0 41.0 %collective-permute-start.44 = (bf16[1,384,384]{1,2,0:T(8,128)(2,1)S(1)}, bf16[1,384,384]{1,2,0:T(8,128)(2,1)}, u32[]{:S(2)}, u32[]{:S(2)}) collective-permute-start(bf16[1,384,384]{1,2,0:T(8,128)(2,1)S(1)} %fusion.52), channel_id=1, source_target_pairs={{0,16},{8,24},{16,0},{24,8},{1,17},{9,25},{17,1},{25,9},{2,18},{10... | collective-permute-start | bytes 884744 | tf_op jit(solution)/shard_map/ppermute | solution.py:86
  674.3 54.0 %collective-permute-start.45 = (bf16[1,384,384]{1,2,0:T(8,128)(2,1)S(1)}, bf16[1,384,384]{1,2,0:T(8,128)(2,1)}, u32[]{:S(2)}, u32[]{:S(2)}) collective-permute-start(bf16[1,384,384]{1,2,0:T(8,128)(2,1)S(1)} %fusion.52), channel_id=1, source_target_pairs={{0,24},{8,16},{16,8},{24,0},{1,25},{9,17},{17,9},{25,1},{2,26},{10... | collective-permute-start | bytes 884744 | tf_op jit(solution)/shard_map/ppermute | solution.py:86
  677.3 68.4 %collective-permute-start.34 = (bf16[384,768]{1,0:T(8,128)(2,1)}, bf16[384,768]{1,0:T(8,128)(2,1)}, u32[]{:S(2)}, u32[]{:S(2)}) collective-permute-start(bf16[384,768]{1,0:T(8,128)(2,1)} %get-tuple-element.178), channel_id=1, source_target_pairs={{0,8},{8,0},{16,24},{24,16},{1,9},{9,1},{17,25},{25,17},{2,10},{10... | collective-permute-start | bytes 1769480 | tf_op jit(solution)/shard_map/ppermute | solution.py:86
  678.7 68.1 %collective-permute-start.35 = (bf16[384,768]{1,0:T(8,128)(2,1)}, bf16[384,768]{1,0:T(8,128)(2,1)}, u32[]{:S(2)}, u32[]{:S(2)}) collective-permute-start(bf16[384,768]{1,0:T(8,128)(2,1)} %get-tuple-element.178), channel_id=1, source_target_pairs={{0,16},{8,24},{16,0},{24,8},{1,17},{9,25},{17,1},{25,9},{2,18},{10... | collective-permute-start | bytes 1769480 | tf_op jit(solution)/shard_map/ppermute | solution.py:86
  681.6 66.3 %collective-permute-start.36 = (bf16[384,768]{1,0:T(8,128)(2,1)}, bf16[384,768]{1,0:T(8,128)(2,1)}, u32[]{:S(2)}, u32[]{:S(2)}) collective-permute-start(bf16[384,768]{1,0:T(8,128)(2,1)} %get-tuple-element.178), channel_id=1, source_target_pairs={{0,24},{8,16},{16,8},{24,0},{1,25},{9,17},{17,9},{25,1},{2,26},{10... | collective-permute-start | bytes 1769480 | tf_op jit(solution)/shard_map/ppermute | solution.py:86
  (86 other events, 1026.6 us)
Sparse Core Ops, SparseCore 0:
  12.2 115.6 all-gather.1

commit v3 on v2

--- a/solution.py
+++ b/solution.py
@@ -59,6 +59,19 @@
         if step:
             piece = lax.ppermute(piece, axis, partner_route(axis, step))
         gathered = lax.dynamic_update_slice_in_dim(gathered, piece, source * rows, 0)
+    return gathered
+
+
+def swap_rows(block, axis):
+    count = lax.axis_size(axis)
+    rows, width = block.shape[0] // count, block.shape[1]
+    gathered = jnp.zeros((rows, count * width), block.dtype)
+    for step in range(count):
+        target, source = partners(axis, step)
+        piece = lax.dynamic_slice_in_dim(block, target * rows, rows, 0)
+        if step:
+            piece = lax.ppermute(piece, axis, partner_route(axis, step))
+        gathered = lax.dynamic_update_slice_in_dim(gathered, piece, source * width, 1)
     return gathered
 
 
@@ -109,8 +122,8 @@
 
 
 def carry_kernel(
-    pieces, end_ref, mu_ref, total_ref, entry_ref, a_ref, start_ref, lam_ref,
-    ahead, back, from_left, from_right, sent_right, sent_left, got_left, got_right,
+    pieces, end_ref, mu_ref, total_ref, entry_ref, a_ref, start_ref, lam_ref, back,
+    ahead, from_left, from_right, sent_right, sent_left, got_left, got_right,
 ):
     count, mine = lax.axis_size("seq"), lax.axis_index("seq")
     width = end_ref.shape[2] // pieces
@@ -181,9 +194,10 @@
             def _():
                 lam_ref[:, :, at(other)] = jnp.zeros(lam_ref.shape[:2] + (width,), F32)
 
+            back[:, :, at(other)] = mu_ref[:, :, at(other)] + decay(other) * lam_ref[:, :, at(other)]
+
             @pl.when(has_left)
             def _():
-                back[:, :, at(other)] = mu_ref[:, :, at(other)] + decay(other) * lam_ref[:, :, at(other)]
                 to_left(other).start()
 
         return nothing
@@ -214,14 +228,19 @@
     return pl.pallas_call(
         functools.partial(carry_kernel, pieces),
         in_specs=[vmem] * 5,
-        out_specs=[vmem] * 2,
-        out_shape=[shape, shape],
-        scratch_shapes=[held] * 4 + [pltpu.SemaphoreType.DMA((pieces,))] * 4,
+        out_specs=[vmem] * 3,
+        out_shape=[shape, shape, shape],
+        scratch_shapes=[held] * 3 + [pltpu.SemaphoreType.DMA((pieces,))] * 4,
         compiler_params=pltpu.CompilerParams(
             collective_id=1, has_side_effects=True, vmem_limit_bytes=32 * 2**20
         ),
         name="carry",
     )(ends, entry_mu, total, entry_state, a_mat)
+
+
+def aligned(inner, axis="seq"):
+    channels = inner // lax.axis_size(axis)
+    return channels % LANES == 0 and widest(inner, 768) % channels == 0
 
 
 def spread_row(ref, rows, at, tile, states):
@@ -293,10 +312,10 @@
 
 
 def scan_kernel(
-    hosted, n_blocks_static, d_ref, act_ref, gate_ref, dg_ref, b_ref, c_ref, c_diag, b_diag, ones_ref, a_ref, skip_ref, start_ref, end_ref,
-    gated_ref, dgate_ref, dpre_ref, dact_ref, db_ref, dc_ref, da_ref, sums_ref, gated_all, gate_all,
+    hosted, n_blocks_static, d_ref, act_ref, gate_ref, dg_ref, b_ref, c_ref, c_diag, b_diag, ones_ref, a_ref, skip_ref, start_ref, end_ref, first_ref,
+    gated_ref, dgate_ref, dpre_ref, dact_ref, db_ref, dc_ref, da_ref, sums_ref, gated_all, gate_all, first_all,
     history, drive, up, low_a, low_b, through_a, through_b, db_acc, dc_acc, sum_acc,
-    gated_out, gate_out, gated_sent, gated_got, gate_sent, gate_got, own_sem,
+    gated_out, gate_out, gated_sent, gated_got, gate_sent, gate_got, own_sem, first_sent, first_got,
 ):
     states = a_ref.shape[0]
     length, width = d_ref.shape[1:]
@@ -312,14 +331,38 @@
     channels = n_blocks_static * width // n_seq
     owners = width // channels if hosted else 0
 
+    first_own = pltpu.make_async_copy(first_ref, first_all, first_got.at[0])
+    first_far = pltpu.make_async_remote_copy(
+        src_ref=first_all, dst_ref=first_all, send_sem=first_sent.at[0], recv_sem=first_got.at[0],
+        device_id={"seq": jnp.minimum(my_seq + 1, n_seq - 1)}, device_id_type=MESH,
+    )
+
     @pl.when(tick == 0)
     def _():
         barrier = pltpu.get_barrier_semaphore()
         for p in range(1, n_dp):
             pl.semaphore_signal(barrier, inc=1, device_id={"dp": lax.rem(my_dp + p, n_dp)}, device_id_type=MESH)
-        for p in range(1, n_seq if hosted else 1):
+        for p in range(1, n_seq):
             pl.semaphore_signal(barrier, inc=1, device_id={"seq": lax.rem(my_seq + p, n_seq)}, device_id_type=MESH)
-        pl.semaphore_wait(barrier, n_dp - 1 + (n_seq - 1 if hosted else 0))
+        pl.semaphore_wait(barrier, n_dp + n_seq - 2)
+
+        @pl.when(my_seq == 0)
+        def _():
+            first_own.start()
+
+    @pl.when(tick == jnp.minimum(my_seq, pl.num_programs(0) * n_blocks - 1))
+    def _():
+        @pl.when(my_seq == 0)
+        def _():
+            first_own.wait()
+
+        @pl.when(my_seq != 0)
+        def _():
+            first_far.wait_recv()
+
+        @pl.when(my_seq != n_seq - 1)
+        def _():
+            first_far.start()
 
     def gated_copies(s, e, slot):
         at = (my_dp, s, slice(None), pl.ds(pl.multiple_of(e * width, LANES), width))
@@ -503,6 +546,11 @@
                 send_sem=gated_sent.at[0, 0], recv_sem=gated_got.at[source],
                 device_id={"dp": source}, device_id_type=MESH,
             ).wait_recv()
+
+        @pl.when(my_seq != n_seq - 1)
+        def _():
+            first_far.wait_send()
+
         for p in range(1, n_seq if hosted else 1):
             source = lax.rem(my_seq + p, n_seq)
             pltpu.make_async_remote_copy(
@@ -512,7 +560,7 @@
             ).wait_recv()
 
 
-def scan_both(delta, act, gate_in, d_gated, b_wide, c_wide, c_diag, b_diag, ones_diag, a_mat, d_skip, start, end):
+def scan_both(delta, act, gate_in, d_gated, b_wide, c_wide, c_diag, b_diag, ones_diag, a_mat, d_skip, start, end, first):
     segs, length, inner = delta.shape
     states = a_mat.shape[0]
     width = widest(inner, 768)
@@ -528,7 +576,7 @@
     lanes = pltpu.VMEM((length, states, LANES), F32)
     n_dp, n_seq = lax.axis_size("dp"), lax.axis_size("seq")
     channels = inner // n_seq
-    hosted = channels % LANES == 0 and width % channels == 0
+    hosted = aligned(inner)
     dma = pltpu.SemaphoreType.DMA
     out = pltpu.VMEM((2, length, width), BF16)
     return pl.pallas_call(
@@ -540,10 +588,12 @@
             pl.BlockSpec((states, width), lambda s, e: (0, e)),
             pl.BlockSpec((1, width), lambda s, e: (0, e)),
             state, state,
+            pl.BlockSpec(memory_space=pl.ANY),
         ],
         out_specs=[
             tokens, tokens, tokens, tokens, narrow, narrow, state,
             pl.BlockSpec((1, 8, width), lambda s, e: (s, 0, e)),
+            pl.BlockSpec(memory_space=pl.ANY),
             pl.BlockSpec(memory_space=pl.ANY),
             pl.BlockSpec(memory_space=pl.ANY),
         ],
@@ -553,6 +603,7 @@
             jax.ShapeDtypeStruct((segs, 8, inner), F32),
             jax.ShapeDtypeStruct((n_dp, segs, length, inner), BF16),
             jax.ShapeDtypeStruct((n_seq, segs, length, channels), BF16),
+            jax.ShapeDtypeStruct(first.shape, F32),
         ],
         scratch_shapes=[
             pltpu.VMEM(((length + 1) * states, width), F32),
@@ -562,6 +613,7 @@
             pltpu.VMEM((2, CHUNK, width), F32),
             out, out,
             dma((2, n_dp)), dma((n_dp,)), dma((2, n_seq)), dma((n_seq,)), dma((2, 1 + n_seq)),
+            dma((1,)), dma((1,)),
         ],
         compiler_params=pltpu.CompilerParams(
             collective_id=2, has_side_effects=True, vmem_limit_bytes=VMEM_BYTES
@@ -570,14 +622,409 @@
             flops=20 * delta.size * states, bytes_accessed=24 * delta.size, transcendentals=2 * delta.size * states
         ),
         name="scan_both",
-    )(delta, act, gate_in, d_gated, b_wide, c_wide, c_diag, b_diag, ones_diag, a_mat, d_skip[None], start, end)
+    )(delta, act, gate_in, d_gated, b_wide, c_wide, c_diag, b_diag, ones_diag, a_mat, d_skip[None], start, end, first)
+
+
+def finish_kernel(
+    gain_at, conv_hbm, gate_hbm, columns_hbm, normed_hbm, proj_hbm, tokens_hbm, cot_hbm, small_hbm, halo_hbm, gain_ref,
+    d_tokens, d_in, small_out, halo_out,
+    conv, gate, gate_columns, conv_columns, normed, proj, tokens, cot, small, d_normed,
+    partial, arrived, placed, small_low, small_dp, small_mid, small_seq,
+    load, normed_load, proj_load, swap_sent, swap_got, swap_own, add_sent, add_got, put_sent, put_got, put_own,
+    copy_sent, copy_got, mid_sent, mid_got, far_sent, far_got, last_sent, last_got, halo_sent, halo_got,
+):
+    n_dp, n_seq = lax.axis_size("dp"), lax.axis_size("seq")
+    my_dp, my_seq = lax.axis_index("dp"), lax.axis_index("seq")
+    half = n_seq // 2
+    count, inner = conv_hbm.shape
+    width = tokens.shape[1]
+    channels = inner // n_seq
+    chunks = channels // LANES
+    rows_dp = width // n_dp
+    rows_small = small_low.shape[0] // n_dp
+    dp_peers = [lax.rem(my_dp + p, n_dp) for p in range(n_dp)]
+    seq_peers = [lax.rem(my_seq + p, n_seq) for p in range(n_seq)]
+
+    def remote(src, dst, sent, got, **to):
+        return pltpu.make_async_remote_copy(
+            src_ref=src, dst_ref=dst, send_sem=sent, recv_sem=got, device_id=to, device_id_type=MESH
+        )
+
+    loads = [
+        pltpu.make_async_copy(src, dst, load.at[k])
+        for k, (src, dst) in enumerate(
+            [(columns_hbm, gate_columns), (conv_hbm, conv), (gate_hbm, gate), (tokens_hbm, tokens), (cot_hbm, cot),
+             (small_hbm, small_low)]
+        )
+    ]
+    load_columns, load_conv, load_gate, load_tokens, load_cot, load_small = loads
+    load_normed = [pltpu.make_async_copy(normed_hbm.at[s], normed.at[s], normed_load.at[s]) for s in range(n_seq)]
+    depth = proj.shape[2]
+
+    def load_proj(k):
+        return pltpu.make_async_copy(proj_hbm.at[:, k * depth : (k + 1) * depth], proj.at[k % 2], proj_load.at[k % 2])
+
+    load_columns.start()
+    for copy in load_normed:
+        copy.start()
+    load_conv.start()
+    load_proj(0).start()
+    for copy in (load_gate, load_tokens, load_cot, load_small):
+        copy.start()
+
+    barrier = pltpu.get_barrier_semaphore()
+    for p in range(1, n_dp):
+        pl.semaphore_signal(barrier, inc=1, device_id={"dp": dp_peers[p]}, device_id_type=MESH)
+    for p in range(1, n_seq):
+        pl.semaphore_signal(barrier, inc=1, device_id={"seq": seq_peers[p]}, device_id_type=MESH)
+    pl.semaphore_wait(barrier, n_dp + n_seq - 2)
+
+    def column_of(device, c):
+        return pl.ds(pl.multiple_of(device * channels + c * LANES, LANES), LANES)
+
+    def swap(c, p):
+        return remote(
+            conv_hbm.at[:, column_of(seq_peers[p], c)], conv_columns.at[c, my_seq],
+            swap_sent.at[c, p], swap_got.at[c, my_seq], seq=seq_peers[p],
+        )
+
+    own_swaps = [
+        pltpu.make_async_copy(conv_hbm.at[:, column_of(my_seq, c)], conv_columns.at[c, my_seq], swap_own.at[c])
+        for c in range(chunks)
+    ]
+    for c in range(chunks):
+        own_swaps[c].start()
+        for p in range(1, n_seq):
+            swap(c, p).start()
+
+    def halo(p):
+        return remote(halo_hbm, halo_out, halo_sent.at[p], halo_got.at[0], seq=p)
+
+    halo_own = pltpu.make_async_copy(halo_hbm, halo_out, halo_got.at[0])
+
+    @pl.when(my_seq == 0)
+    def _():
+        halo_own.start()
+        for p in range(1, n_seq):
+            halo(p).start()
+
+    def product(c, columns):
+        tile = 768 if width % 768 == 0 else 256
+
+        def some_rows(r, nothing):
+            at = pl.ds(pl.multiple_of(r * tile, tile), tile)
+            total = jnp.dot(normed[0, at, :], columns(0), preferred_element_type=F32)
+            for s in range(1, n_seq):
+                total += jnp.dot(normed[s, at, :], columns(s), preferred_element_type=F32)
+            partial[c, at, :] = total.astype(BF16)
+            return nothing
+
+        lax.fori_loop(0, width // tile, some_rows, 0)
+
+    def rows_of(device):
+        return pl.ds(pl.multiple_of(device * rows_dp, 16), rows_dp)
+
+    def add(c, p):
+        return remote(
+            partial.at[c, rows_of(dp_peers[p])], arrived.at[c, my_dp], add_sent.at[c, p], add_got.at[c, my_dp],
+            dp=dp_peers[p],
+        )
+
+    def scatter(c):
+        for p in range(1, n_dp):
+            add(c, p).start()
+
+    def place(c):
+        k, is_gate = c % chunks, c < chunks
+        keeper = my_seq // 2 + (half if is_gate else 0)
+        side = lax.rem(my_seq, 2)
+        at = (rows_of(my_dp), pl.ds(pl.multiple_of(side * channels + k * LANES, LANES), LANES))
+        own = pltpu.make_async_copy(placed.at[c], d_in.at[at], put_own.at[c])
+        far = remote(placed.at[c], d_in.at[at], put_sent.at[c], put_got.at[k, side], seq=keeper)
+        return keeper, own, far
+
+    def gather_add(c):
+        total = partial[c, rows_of(my_dp), :].astype(F32)
+        for p in range(1, n_dp):
+            remote(
+                partial.at[c, rows_of(my_dp)], arrived.at[c, dp_peers[p]], add_sent.at[c, p],
+                add_got.at[c, dp_peers[p]], dp=dp_peers[p],
+            ).wait_recv()
+            total += arrived[c, dp_peers[p]].astype(F32)
+        placed[c] = total.astype(BF16)
+        keeper, own, far = place(c)
+        pl.when(keeper == my_seq)(own.start)
+        pl.when(keeper != my_seq)(far.start)
+
+    def spread(k, side, p):
+        at = (rows_of(my_dp), slice(side * channels + k * LANES, side * channels + (k + 1) * LANES))
+        return remote(
+            d_in.at[at], d_in.at[at], copy_sent.at[k, side, p], copy_got.at[k, side, my_dp], dp=dp_peers[p]
+        )
+
+    def pass_on(c):
+        k, is_gate = c % chunks, c < chunks
+
+        @pl.when((my_seq >= half) == is_gate)
+        def _():
+            for side in range(2):
+                source = 2 * lax.rem(my_seq, half) + side
+                at = (rows_of(my_dp), slice(side * channels + k * LANES, side * channels + (k + 1) * LANES))
+
+                @pl.when(source == my_seq)
+                def _():
+                    place(c)[1].wait()
+
+                @pl.when(source != my_seq)
+                def _():
+                    remote(placed.at[c], d_in.at[at], put_sent.at[c], put_got.at[k, side], seq=source).wait_recv()
+
+                for p in range(1, n_dp):
+                    spread(k, side, p).start()
+
+    load_columns.wait()
+    for copy in load_normed:
+        copy.wait()
+    for c in range(chunks):
+        product(c, lambda s, c=c: gate_columns[s, :, c * LANES : (c + 1) * LANES])
+        scatter(c)
+
+    load_conv.wait()
+    load_gate.wait()
+    steps = 2 * inner // depth
+    for k in range(steps):
+        if k + 1 < steps:
+            load_proj(k + 1).start()
+        load_proj(k).wait()
+        source, at = (conv, k * depth) if k * depth < inner else (gate, k * depth - inner)
+
+        def some_columns(n, nothing, k=k, source=source, at=at):
+            cols = pl.ds(pl.multiple_of(n * 256, 256), 256)
+            term = lax.dot_general(
+                source[:, at : at + depth], proj[k % 2, cols, :], (((1,), (1,)), ((), ())), preferred_element_type=F32
+            )
+            d_normed[:, cols] = term if k == 0 else d_normed[:, cols] + term
+            return nothing
+
+        lax.fori_loop(0, width // 256, some_columns, 0)
+        if k == steps // 2:
+            for c in range(chunks):
+                gather_add(c)
+
+    load_tokens.wait()
+    load_cot.wait()
+    gain = gain_ref[...]
+
+    def some_tokens(r, total):
+        at = pl.ds(pl.multiple_of(r * 32, 32), 32)
+        token = tokens[at, :].astype(F32)
+        inverse = lax.rsqrt(jnp.mean(token * token, axis=-1, keepdims=True) + EPS)
+        scaled = d_normed[at, :] * gain
+        mean = jnp.mean(scaled * token, axis=-1, keepdims=True)
+        d_tokens[at, :] = cot[at, :].astype(F32) + inverse * scaled - token * (inverse * inverse * inverse * mean)
+        return total + jnp.sum(d_normed[at, :] * token * inverse, axis=0, keepdims=True)
+
+    d_gain = lax.fori_loop(0, count // 32, some_tokens, jnp.zeros((1, width), F32))
+    load_small.wait()
+    first = gain_at // 16 * 16
+    small[...] = small_low[first : first + 16, :].astype(F32)
+    for row in range(width // channels):
+        for s in range(n_seq):
+            at = gain_at - first + row
+            small[at : at + 1, s * channels : (s + 1) * channels] = d_gain[:, row * channels : (row + 1) * channels]
+    small_low[first : first + 16, :] = small[...].astype(BF16)
+
+    def small_rows(device):
+        return pl.ds(pl.multiple_of(device * rows_small, 16), rows_small)
+
+    def small_add(p):
+        return remote(
+            small_low.at[small_rows(dp_peers[p])], small_dp.at[my_dp], mid_sent.at[p], mid_got.at[my_dp], dp=dp_peers[p]
+        )
+
+    for p in range(1, n_dp):
+        small_add(p).start()
+    for c in range(chunks):
+        pass_on(c)
+
+    total = small_low[small_rows(my_dp), :].astype(F32)
+    for p in range(1, n_dp):
+        remote(
+            small_low.at[small_rows(my_dp)], small_dp.at[dp_peers[p]], mid_sent.at[p], mid_got.at[dp_peers[p]],
+            dp=dp_peers[p],
+        ).wait_recv()
+        total += small_dp[dp_peers[p]].astype(F32)
+    small_mid[...] = total.astype(BF16)
+
+    def small_swap(p):
+        at = pl.ds(pl.multiple_of(seq_peers[p] * channels, LANES), channels)
+        return remote(
+            small_mid.at[:, at], small_seq.at[my_seq], far_sent.at[p], far_got.at[my_seq], seq=seq_peers[p]
+        )
+
+    for p in range(1, n_seq):
+        small_swap(p).start()
+
+    def convolved(c):
+        own_swaps[c].wait()
+        for p in range(1, n_seq):
+            remote(
+                conv_hbm.at[:, column_of(my_seq, c)], conv_columns.at[c, seq_peers[p]], swap_sent.at[c, p],
+                swap_got.at[c, seq_peers[p]], seq=seq_peers[p],
+            ).wait_recv()
+        product(chunks + c, lambda s: conv_columns[c, s])
+        scatter(chunks + c)
+
+    convolved(0)
+    total = small_mid[:, pl.ds(pl.multiple_of(my_seq * channels, LANES), channels)].astype(F32)
+    for p in range(1, n_seq):
+        remote(
+            small_mid.at[:, 0:channels], small_seq.at[seq_peers[p]], far_sent.at[p], far_got.at[seq_peers[p]],
+            seq=seq_peers[p],
+        ).wait_recv()
+        total += small_seq[seq_peers[p]].astype(F32)
+    small_out[small_rows(my_dp), :] = total.astype(BF16)
+
+    def small_spread(p):
+        at = small_rows(my_dp)
+        return remote(small_out.at[at], small_out.at[at], last_sent.at[p], last_got.at[my_dp], dp=dp_peers[p])
+
+    for p in range(1, n_dp):
+        small_spread(p).start()
+
+    for c in range(1, chunks):
+        convolved(c)
+        gather_add(chunks + c - 1)
+        if c >= 2:
+            pass_on(chunks + c - 2)
+    gather_add(2 * chunks - 1)
+    if chunks >= 2:
+        pass_on(2 * chunks - 2)
+    pass_on(2 * chunks - 1)
+
+    for c in range(chunks):
+        for p in range(1, n_seq):
+            swap(c, p).wait_send()
+    for c in range(2 * chunks):
+        for p in range(1, n_dp):
+            add(c, p).wait_send()
+        keeper, own, far = place(c)
+
+        @pl.when(keeper != my_seq)
+        def _(far=far):
+            far.wait_send()
+
+    for k in range(chunks):
+        for side in range(2):
+            at = slice(side * channels + k * LANES, side * channels + (k + 1) * LANES)
+            for p in range(1, n_dp):
+                spread(k, side, p).wait_send()
+                peer = dp_peers[p]
+                remote(
+                    d_in.at[rows_of(peer), at], d_in.at[rows_of(peer), at], copy_sent.at[k, side, p],
+                    copy_got.at[k, side, peer], dp=peer,
+                ).wait_recv()
+    for p in range(1, n_dp):
+        small_add(p).wait_send()
+        small_spread(p).wait_send()
+        peer = dp_peers[p]
+        remote(
+            small_out.at[small_rows(peer)], small_out.at[small_rows(peer)], last_sent.at[p], last_got.at[peer], dp=peer
+        ).wait_recv()
+    for p in range(1, n_seq):
+        small_swap(p).wait_send()
+
+    @pl.when(my_seq == 0)
+    def _():
+        halo_own.wait()
+        for p in range(1, n_seq):
+            halo(p).wait_send()
+
+    @pl.when(my_seq != 0)
+    def _():
+        halo(1).wait_recv()
+
+
+def finish(d_conv_in, d_gate, gate_columns, normed_all, in_proj, tokens, cot, small, gain_at, halo_grad, norm_gain):
+    n_dp, n_seq = lax.axis_size("dp"), lax.axis_size("seq")
+    count, inner = d_conv_in.shape
+    width = tokens.shape[1]
+    channels = inner // n_seq
+    chunks = channels // LANES
+    rows = small.shape[0]
+    depth = 1024 if inner % 1024 == 0 else LANES
+    dma = pltpu.SemaphoreType.DMA
+    vmem = pltpu.VMEM
+    anywhere = pl.BlockSpec(memory_space=pl.ANY)
+    inside = pl.BlockSpec(memory_space=pltpu.VMEM)
+    return pl.pallas_call(
+        functools.partial(finish_kernel, gain_at),
+        in_specs=[anywhere] * 9 + [inside],
+        out_specs=[inside, anywhere, inside, anywhere],
+        out_shape=[
+            jax.ShapeDtypeStruct((count, width), F32),
+            jax.ShapeDtypeStruct((width, 2 * channels), BF16),
+            jax.ShapeDtypeStruct((rows, channels), BF16),
+            jax.ShapeDtypeStruct(halo_grad.shape, F32),
+        ],
+        scratch_shapes=[
+            vmem((count, inner), BF16), vmem((count, inner), BF16),
+            vmem((n_seq, count, channels), BF16), vmem((chunks, n_seq, count, LANES), BF16),
+            vmem((n_seq, width, count), BF16), vmem((2, width, depth), BF16),
+            vmem((count, width), BF16), vmem((count, width), BF16), vmem((16, inner), F32),
+            vmem((count, width), F32),
+            vmem((2 * chunks, width, LANES), BF16), vmem((2 * chunks, n_dp, width // n_dp, LANES), BF16),
+            vmem((2 * chunks, width // n_dp, LANES), BF16),
+            vmem((rows, inner), BF16), vmem((n_dp, rows // n_dp, inner), BF16), vmem((rows // n_dp, inner), BF16),
+            vmem((n_seq, rows // n_dp, channels), BF16),
+            dma((6,)), dma((n_seq,)), dma((2,)),
+            dma((chunks, n_seq)), dma((chunks, n_seq)), dma((chunks,)),
+            dma((2 * chunks, n_dp)), dma((2 * chunks, n_dp)),
+            dma((2 * chunks,)), dma((chunks, 2)), dma((2 * chunks,)),
+            dma((chunks, 2, n_dp)), dma((chunks, 2, n_dp)),
+            dma((n_dp,)), dma((n_dp,)), dma((n_seq,)), dma((n_seq,)), dma((n_dp,)), dma((n_dp,)),
+            dma((n_seq,)), dma((1,)),
+        ],
+        compiler_params=pltpu.CompilerParams(
+            collective_id=3, has_side_effects=True, vmem_limit_bytes=60 * 2**20
+        ),
+        cost_estimate=pl.CostEstimate(
+            flops=12 * count * width * inner, bytes_accessed=40 * count * width, transcendentals=0
+        ),
+        name="finish",
+    )(
+        d_conv_in, d_gate, gate_columns, normed_all, in_proj, tokens, cot, small, halo_grad, norm_gain[None],
+    )
 
 
 def diagonal_blocks(value):
     segs, length, states = value.shape
-    spread = value.reshape(segs, length // CHUNK, CHUNK, 1, states)
-    spread = spread * jnp.eye(CHUNK, dtype=value.dtype)[:, :, None]
-    return spread.reshape(segs, length // CHUNK, CHUNK, CHUNK * states).astype(BF16)
+    spread = jnp.tile(jnp.eye(states, dtype=BF16), (1, CHUNK))
+    tiled = matmul(value.reshape(segs * length, states).astype(BF16), spread)
+    mask = jnp.repeat(jnp.eye(CHUNK, dtype=F32), states, axis=1)
+    return (tiled.reshape(segs, length // CHUNK, CHUNK, CHUNK * states) * mask).astype(BF16)
+
+
+def norm_kernel(token_ref, gain_ref, normed_ref, turned_ref):
+    token = token_ref[...].astype(F32)
+    inverse = lax.rsqrt(jnp.mean(token * token, axis=-1, keepdims=True) + EPS)
+    normed = token * inverse * gain_ref[...]
+    normed_ref[...] = normed.astype(BF16)
+    turned_ref[...] = normed.T.astype(BF16)
+
+
+def norm(tokens, norm_gain):
+    count, width = tokens.shape
+    rows = 128
+    return pl.pallas_call(
+        norm_kernel,
+        grid=(count // rows,),
+        in_specs=[pl.BlockSpec((rows, width), lambda r: (r, 0)), pl.BlockSpec((1, width), lambda r: (0, 0))],
+        out_specs=[pl.BlockSpec((rows, width), lambda r: (r, 0)), pl.BlockSpec((width, rows), lambda r: (0, r))],
+        out_shape=[jax.ShapeDtypeStruct((count, width), BF16), jax.ShapeDtypeStruct((width, count), BF16)],
+        compiler_params=pltpu.CompilerParams(vmem_limit_bytes=32 * 2**20),
+        name="norm",
+    )(tokens, norm_gain[None])
 
 
 def body(
@@ -601,10 +1048,14 @@
 
     token_float = flat(tokens).astype(F32)
     inverse = lax.rsqrt(jnp.mean(token_float * token_float, axis=-1, keepdims=True) + EPS)
-    normed = (token_float * inverse * norm_gain).astype(BF16)
+    normed, normed_turned = norm(flat(tokens), norm_gain)
     cot = flat(cotangent)
-    normed_all = lax.all_gather(normed, "seq", axis=0, tiled=True)
-    cot_columns = swap_columns(cot, "dp")
+    fast = aligned(inner)
+    if fast:
+        normed_all = lax.all_gather(normed_turned, "seq", axis=0, tiled=False)
+    else:
+        normed_all = lax.all_gather(normed, "seq", axis=0, tiled=True)
+    cot_rows = swap_rows(cot.T, "dp")
     conv_in = matmul(normed, in_proj[:, :inner]).astype(BF16)
     gate_in = matmul(normed, in_proj[:, inner:])
     d_gated = matmul_nt(cot, out_proj)
@@ -626,12 +1077,12 @@
     c_wide = jnp.broadcast_to(c_in[..., None], c_in.shape + (LANES,))
     ends, entry_mu = block_ends(delta, activated, gate_in, d_gated, b_wide, c_wide, a_mat)
     total = jnp.sum(delta, axis=1, keepdims=True)
-    start, end = carry(ends, entry_mu, total, entry_state, a_mat)
-    d_entry = from_first(entry_mu + jnp.exp(total * a_mat) * end, "seq")
+    start, end, first = carry(ends, entry_mu, total, entry_state, a_mat)
+    start, normed_all = lax.optimization_barrier((start, normed_all))
     ones_diag = diagonal_blocks(jnp.ones((1, CHUNK, states), F32))[0, 0]
-    gated, d_gate, d_pre_low, d_act, d_b, d_c, d_amat, sums, gated_all, gate_columns = scan_both(
+    gated, d_gate, d_pre_low, d_act, d_b, d_c, d_amat, sums, gated_all, gate_columns, d_entry = scan_both(
         delta, activated, gate_in, d_gated, b_wide, c_wide,
-        diagonal_blocks(c_in), diagonal_blocks(b_in), ones_diag, a_mat, d_skip, start, end,
+        diagonal_blocks(c_in), diagonal_blocks(b_in), ones_diag, a_mat, d_skip, start, end, first,
     )
     gated, d_gate, d_pre_low, d_act = flat(gated), flat(d_gate), flat(d_pre_low), flat(d_act)
     gated_all = gated_all.reshape(-1, inner)
@@ -639,6 +1090,9 @@
     if (inner // n_seq) % LANES:
         gate_columns = swap_columns(d_gate, "seq")
     output = token_float + matmul(gated, out_proj)
+    out_part = matmul(cot_rows, gated_all).astype(BF16)
+    out_part = lax.psum_scatter(out_part, "seq", scatter_dimension=1, tiled=True)
+    d_out_proj = lax.all_gather(out_part, "dp", axis=0, tiled=True).T.astype(F32)
 
     sums = jnp.sum(sums, axis=0)
     d_dt_bias, d_d_skip = sums[0], sums[1]
@@ -662,63 +1116,87 @@
     d_conv_in = sum(conv_weight[tap] * tail[:, halo - tap : halo - tap + length] for tap in range(taps))
     d_conv_in = d_conv_in + jnp.pad(returned, ((0, 0), (length - halo, 0), (0, 0)))
     d_conv_in = flat(d_conv_in).astype(BF16)
-    d_conv_state = from_first(halo_grad, "seq")
-
-    n_dp = lax.axis_size("dp")
-    small = jnp.concatenate([d_x_proj, d_dt_proj, d_a_log, d_dt_bias[None], d_d_skip[None]], axis=0)
-    small = jnp.pad(small, ((0, -small.shape[0] % 16), (0, 0))).astype(BF16)
-    small_columns = swap_columns(small, "seq")
-    edges = jnp.concatenate([d_conv_weight, d_conv_bias[None]], axis=0)
-    edges = jnp.pad(edges, ((0, -edges.shape[0] % 16), (0, 0))).astype(BF16)
-    conv_columns = swap_columns(jnp.concatenate([d_conv_in, edges], axis=0), "seq").reshape(n_seq, -1, inner // n_seq)
-    edge_columns = conv_columns[:, count:]
-    conv_columns = conv_columns[:, :count].reshape(n_seq * count, -1)
-
-    def blocks(value, axis):
-        return value.reshape((lax.axis_size(axis), -1) + value.shape[1:])
-
-    out_part = sum_scatter(blocks(matmul_tn(gated_all, cot_columns), "seq"), "seq")
-    d_out_proj = gather_rows(out_part.astype(BF16)[None], "dp").transpose(1, 0, 2).reshape(out_part.shape[0], -1)
-    d_out_proj = d_out_proj.astype(F32)
-
-    gate_part = sum_scatter(blocks(matmul_tn(normed_all, gate_columns), "dp"), "dp").astype(BF16)
-    conv_part = sum_scatter(blocks(matmul_tn(normed_all, conv_columns), "dp"), "dp").astype(BF16)
-    half = n_seq // 2
-    even = mine % 2 == 0
-    straight = [(i, i // 2 + (0 if i % 2 == 0 else half)) for i in range(n_seq)]
-    crossed = [(i, i // 2 + (half if i % 2 == 0 else 0)) for i in range(n_seq)]
-    first = lax.ppermute(jnp.where(even, conv_part, gate_part), "seq", straight)
-    second = lax.ppermute(jnp.where(even, gate_part, conv_part), "seq", crossed)
-    low_half = mine < half
-    d_in_part = jnp.concatenate(
-        [jnp.where(low_half, first, second), jnp.where(low_half, second, first)], axis=1
-    )
-    d_in_proj = gather_rows(d_in_part, "dp").astype(F32)
-
-    d_normed = matmul_nt(d_conv_in, in_proj[:, :inner]) + matmul_nt(d_gate, in_proj[:, inner:])
-    d_norm_gain = jnp.sum(d_normed * token_float * inverse, axis=0)
-    scaled = d_normed * norm_gain
-    cubed = inverse * inverse * inverse
-    d_tokens = (
-        cot.astype(F32)
-        + inverse * scaled
-        - token_float * cubed * jnp.mean(scaled * token_float, axis=-1, keepdims=True)
-    )
-    gain = sum_scatter(blocks(d_norm_gain, "seq"), "seq")
-    channels = inner // n_seq
-    per_device = jnp.concatenate(
-        [
-            jnp.sum(small_columns.reshape(n_seq, -1, channels).astype(F32), axis=0),
-            jnp.sum(edge_columns.astype(F32), axis=0),
-            jnp.pad(gain, (0, -gain.shape[0] % channels)).reshape(-1, channels),
-        ],
-        axis=0,
-    )
-    per_device = per_device.astype(BF16)
-    summed = jnp.sum(gather_rows(per_device[None], "dp").astype(F32), axis=0)
-    edges = summed[small.shape[0] : small.shape[0] + edges.shape[0]]
-    d_norm_gain = summed[small.shape[0] + edges.shape[0] :].reshape(-1)[: gain.shape[0]]
-    small = summed
+    if fast:
+        small = jnp.concatenate(
+            [
+                part.astype(BF16)
+                for part in (
+                    d_x_proj, d_dt_proj, d_a_log, d_dt_bias[None], d_d_skip[None], d_conv_weight, d_conv_bias[None]
+                )
+            ],
+            axis=0,
+        )
+        edge_at = 2 * rank + 3 * states + 2
+        channels = inner // n_seq
+        gain_rows = width // channels
+        gain_at = small.shape[0]
+        if gain_at % 16 + gain_rows > 16:
+            gain_at += -gain_at % 16
+        rows = gain_at + gain_rows
+        rows += -rows % (16 * lax.axis_size("dp"))
+        small = jnp.pad(small, ((0, rows - small.shape[0]), (0, 0)))
+        d_tokens, d_in_proj, small, d_conv_state = finish(
+            d_conv_in, d_gate, gate_columns.reshape(n_seq, count, channels), normed_all, in_proj, flat(tokens), cot,
+            small, gain_at, halo_grad, norm_gain,
+        )
+        d_in_proj, small = d_in_proj.astype(F32), small.astype(F32)
+        edges = small[edge_at:gain_at]
+        d_norm_gain = small[gain_at : gain_at + gain_rows].reshape(n_seq, -1)
+        d_norm_gain = lax.dynamic_index_in_dim(d_norm_gain, mine, 0, keepdims=False)
+    else:
+        d_conv_state = from_first(halo_grad, "seq")
+
+        n_dp = lax.axis_size("dp")
+        small = jnp.concatenate([d_x_proj, d_dt_proj, d_a_log, d_dt_bias[None], d_d_skip[None]], axis=0)
+        small = jnp.pad(small, ((0, -small.shape[0] % 16), (0, 0))).astype(BF16)
+        small_columns = swap_columns(small, "seq")
+        edges = jnp.concatenate([d_conv_weight, d_conv_bias[None]], axis=0)
+        edges = jnp.pad(edges, ((0, -edges.shape[0] % 16), (0, 0))).astype(BF16)
+        conv_columns = swap_columns(jnp.concatenate([d_conv_in, edges], axis=0), "seq").reshape(n_seq, -1, inner // n_seq)
+        edge_columns = conv_columns[:, count:]
+        conv_columns = conv_columns[:, :count].reshape(n_seq * count, -1)
+
+        def blocks(value, axis):
+            return value.reshape((lax.axis_size(axis), -1) + value.shape[1:])
+
+        gate_part = sum_scatter(blocks(matmul_tn(normed_all, gate_columns), "dp"), "dp").astype(BF16)
+        conv_part = sum_scatter(blocks(matmul_tn(normed_all, conv_columns), "dp"), "dp").astype(BF16)
+        half = n_seq // 2
+        even = mine % 2 == 0
+        straight = [(i, i // 2 + (0 if i % 2 == 0 else half)) for i in range(n_seq)]
+        crossed = [(i, i // 2 + (half if i % 2 == 0 else 0)) for i in range(n_seq)]
+        first = lax.ppermute(jnp.where(even, conv_part, gate_part), "seq", straight)
+        second = lax.ppermute(jnp.where(even, gate_part, conv_part), "seq", crossed)
+        low_half = mine < half
+        d_in_part = jnp.concatenate(
+            [jnp.where(low_half, first, second), jnp.where(low_half, second, first)], axis=1
+        )
+        d_in_proj = gather_rows(d_in_part, "dp").astype(F32)
+
+        d_normed = matmul_nt(d_conv_in, in_proj[:, :inner]) + matmul_nt(d_gate, in_proj[:, inner:])
+        d_norm_gain = jnp.sum(d_normed * token_float * inverse, axis=0)
+        scaled = d_normed * norm_gain
+        cubed = inverse * inverse * inverse
+        d_tokens = (
+            cot.astype(F32)
+            + inverse * scaled
+            - token_float * cubed * jnp.mean(scaled * token_float, axis=-1, keepdims=True)
+        )
+        gain = sum_scatter(blocks(d_norm_gain, "seq"), "seq")
+        channels = inner // n_seq
+        per_device = jnp.concatenate(
+            [
+                jnp.sum(small_columns.reshape(n_seq, -1, channels).astype(F32), axis=0),
+                jnp.sum(edge_columns.astype(F32), axis=0),
+                jnp.pad(gain, (0, -gain.shape[0] % channels)).reshape(-1, channels),
+            ],
+            axis=0,
+        )
+        per_device = per_device.astype(BF16)
+        summed = jnp.sum(gather_rows(per_device[None], "dp").astype(F32), axis=0)
+        edges = summed[small.shape[0] : small.shape[0] + edges.shape[0]]
+        d_norm_gain = summed[small.shape[0] + edges.shape[0] :].reshape(-1)[: gain.shape[0]]
+        small = summed
 
     return (
         split(output),

time: 767 us -> 581 us (0.76)
  the two profiles are of different devices: /device:TPU:24 before, /device:TPU:1 now
where the time goes in v3:
time: 581 us; the launch traced here: 576 us
  Pallas kernels  387 us (67%)
  matrix products  72 us (12%)
  local copies, waits for them, and re-layouts  50.8 us (9%)
  other arithmetic  39 us (7%)
  between operations  14.7 us (3%)
  starting transfers between devices  12.8 us (2%)
    pallas_call x1, Pallas kernels, scan_both(): pl.pallas_call(functools.partial(scan_kernel, hosted, inner // width), gr...  165 us
    pallas_call x1, Pallas kernels, finish(): pl.pallas_call(functools.partial(finish_kernel, gain_at), in_specs=[anywh...  149 us
    dot_general x9, matrix products, matmul(): lax.dot_general(left, right, (((1,), (0,)), ((), ())), preferred_element_...  50.1 us
    pallas_call x1, Pallas kernels, block_ends(): pl.pallas_call(ends_kernel, grid=(segs, inner // width), in_specs=[tokens...  41.3 us
    pallas_call x1, Pallas kernels, carry(): pl.pallas_call(functools.partial(carry_kernel, pieces), in_specs=[vmem] *...  29.3 us
    unnamed x85, local copies, waits for them, and re-layouts  25.7 us
    dot_general x3, matrix products, matmul_nt(): lax.dot_general(left, right, (((1,), (1,)), ((), ())), preferred_element_...  18 us
    convert_element_type x1, other arithmetic, body(): d_conv_in = flat(d_conv_in).astype(BF16)  11.7 us
  transfers between devices with their start and end apart: 8, of which 0 were waited for; matrix products, arithmetic and copies ran while one was open for 21% of the time, Pallas kernels for 38%

profile of v3, /device:TPU:1, one launch (start us, length us, event | category | flops | bytes accessed | tf_op | source)
XLA Modules:
  0.0 576.4 jit_solution(14220532472052868399)
XLA Ops:
  9.4 2.4 norm.1
  11.9 9.0 %fusion.7 = bf16[512,3072]{1,0:T(8,128)(2,1)S(1)} fusion(bf16[512,1536]{1,0:T(8,128)(2,1)S(1)} %get-tuple-element.38, bf16[1536,6144]{1,0:T(8,128)(2,1)} %proj_hbm.1), kind=kOutput, calls=%fused_computation.19 | convolution fusion | flops 4833411072 | bytes 14155776 | tf_op jit(solution)/shard_map/dot_general | solution.py:27
  21.0 1.7 copy-done.15
  22.7 4.6 collective-permute-start
  27.3 2.3 dynamic-slice_bitcast_fusion
  34.9 10.9 %fusion.2 = f32[512,3072]{1,0:T(8,128)} fusion(bf16[512,1536]{1,0:T(8,128)(2,1)S(1)} %get-tuple-element.38, bf16[1536,6144]{1,0:T(8,128)(2,1)} %proj_hbm.1), kind=kOutput, calls=%fused_computation.3 | convolution fusion | flops 4831838208 | bytes 17301504 | tf_op jit(solution)/shard_map/dot_general | solution.py:27
  45.8 11.0 %fusion.dg_ref = f32[4,128,3072]{2,1,0:T(8,128)} fusion(bf16[4,128,1536]{2,1,0:T(8,128)(2,1)S(1)} %copy-done.17, bf16[3072,1536]{1,0:T(8,128)(2,1)} %param.26), kind=kOutput, calls=%fused_computation.1 | convolution fusion | flops 4831838208 | bytes 17301504 | tf_op jit(solution)/shard_map/dot_general | solution.py:31
  58.2 5.8 %multiply_convert_fusion = (bf16[4,128,3072]{2,1,0:T(8,128)(2,1)S(1)}, f32[4,128,3072]{2,1,0:T(8,128)}) fusion(f32[4,131,3072]{2,1,0:T(8,128)S(1)} %maximum_convert_fusion, f32[3072]{0:T(1024)S(1)} %bitcast.105, f32[3072]{0:T(1024)S(1)} %bitcast.102, f32[3072]{0:T(1024)S(1)} %bitcast.99, f32[3072]{0:T(1024)S(1)} %bitcast.96, f32[3072]{0:T(1024)S(1)} %copy-done.35), kind=kLoop, calls=%fused_computation.16 | loop fusion | flops 20447232 | bytes 34664448 | tf_op jit(solution)/shard_map/convert_element_type | solution.py:1066
  64.0 1.7 copy-done.12
  67.9 6.7 %bitcast_reduce_fusion = (f32[4,3072]{1,0:T(4,128)S(1)}, f32[512,3072]{1,0:T(8,128)}) fusion(f32[3072]{0:T(1024)S(1)} %copy-done.36, bf16[96,3072]{1,0:T(8,128)(2,1)S(1)} %copy-done.22, f32[512,128]{0,1:T(8,128)S(1)} %fusion.27), kind=kOutput, calls=%fused_computation.62 | convolution fusion | flops 314560512 | bytes 7041024 | tf_op jit(solution)/shard_map/dot_general | solution.py:27
  75.0 2.6 broadcast_in_dim.41.b_ref
  77.7 2.8 broadcast_in_dim.43.c_ref
  80.5 41.3 %block_ends.1 = (f32[4,16,3072]{2,1,0:T(8,128)}, f32[4,16,3072]{2,1,0:T(8,128)}) custom-call(f32[4,128,3072]{2,1,0:T(8,128)} %bitcast.113, bf16[4,128,3072]{2,1,0:T(8,128)(2,1)} %copy-done.12, f32[4,128,3072]{2,1,0:T(8,128)} %bitcast.111, f32[4,128,3072]{2,1,0:T(8,128)} %fusion.dg_ref, f32[4,128,16,128]{3,2,1,0:T(8,128)} %broadcast_in_dim.41.b_ref, ...), custom_call_target="tpu_custom_call" | custom-call | flops 226492416 | bytes 18874368 | tf_op jit(solution)/shard_map/block_ends/pallas_call | solution.py:299
  124.1 29.3 %carry.1 = (f32[4,16,3072]{2,1,0:T(8,128)S(1)}, f32[4,16,3072]{2,1,0:T(8,128)S(1)}, f32[4,16,3072]{2,1,0:T(8,128)S(1)}) custom-call(f32[4,16,3072]{2,1,0:T(8,128)S(1)} %copy-done.5, f32[4,16,3072]{2,1,0:T(8,128)S(1)} %copy-done.6, f32[4,1,3072]{2,1,0:T(1,128)S(1)} %broadcast_in_dim.46.total_ref, f32[4,16,3072]{2,1,0:T(8,128)S(1)} %copy-done.4, ...), custom_call_target="tpu_custom_call" | custom-call | tf_op jit(solution)/shard_map/carry/pallas_call | solution.py:228
  160.2 165.1 %scan_both.1 = (bf16[4,128,3072]{2,1,0:T(8,128)(2,1)}, bf16[4,128,3072]{2,1,0:T(8,128)(2,1)}, bf16[4,128,3072]{2,1,0:T(8,128)(2,1)}, f32[4,128,3072]{2,1,0:T(8,1...) custom-call(f32[4,128,3072]{2,1,0:T(8,128)} %bitcast.114, ...), custom_call_target="tpu_custom_call" | custom-call | flops 503316480 | bytes 37748736 | tf_op jit(solution)/shard_map/scan_both/pallas_call | solution.py:582
  328.6 3.0 convolution_convert_fusion.3
  331.6 8.5 %convolution_convert_fusion = bf16[384,3072]{1,0:T(8,128)(2,1)S(1)} fusion(bf16[384,2048]{0,1:T(8,128)(2,1)} %copy-done.18, bf16[2048,3072]{1,0:T(8,128)(2,1)} %bitcast.110), kind=kOutput, calls=%fused_computation.20 | convolution fusion | flops 4833017856 | bytes 16515072 | tf_op jit(solution)/shard_map/dot_general | solution.py:27
  340.2 2.4 copy.53
  342.7 4.0 bitcast_add_fusion
  347.5 7.4 %multiply_reduce_fusion = (bf16[3072]{0:T(1024)(128)(2,1)}, bf16[3072]{0:T(1024)(128)(2,1)}, bf16[3072]{0:T(1024)(128)(2,1)}, bf16[3072]{0:T(1024)(128)(2,1)}, b...) fusion(f32[4,131,3072]{2,1,0:T(8,128)S(1)} %bitcast.76, f32[4,128,3072]{2,1,0:T(8,128)} %get-tuple-element.100, ...), kind=kLoop, calls=%fused_computation.8 | loop fusion | flops 26723328 | bytes 44070912 | tf_op jit(solution)/shard_map/reduce_sum | solution.py:1109
  355.0 2.5 copy-done.14
  358.4 5.5 collective-permute-start.1
  364.6 3.4 convolution_convert_fusion.2
  369.1 11.3 %convolution_add_fusion = f32[512,1536]{1,0:T(8,128)} fusion(bf16[512,3072]{1,0:T(8,128)(2,1)} %bitcast.118, bf16[3072,1536]{1,0:T(8,128)(2,1)} %param.26, bf16[512,1536]{1,0:T(8,128)(2,1)S(1)} %bitcast.74), kind=kOutput, calls=%fused_computation.24 | convolution fusion | flops 4833411072 | bytes 17301504 | tf_op jit(solution)/shard_map/dot_general | solution.py:27
  382.2 3.2 concatenate.13
  386.7 11.7 %add_convert_fusion = bf16[4,128,3072]{2,1,0:T(8,128)(2,1)} fusion(f32[4,3,3072]{2,1,0:T(4,128)} %collective-permute-done.1, f32[4,128,3072]{2,1,0:T(8,128)} %copy-done.14, f32[3072]{0:T(1024)S(1)} %bitcast.106, f32[3072]{0:T(1024)S(1)} %bitcast.104, f32[3072]{0:T(1024)S(1)} %bitcast.101, f32[3072]{0:T(1024)S(1)} %bitcast.98), kind=kLoop, calls=%fused_computation.12 | loop fusion | flops 14155776 | bytes 9633792 | tf_op jit(solution)/shard_map/convert_element_type | solution.py:1118
  398.5 1.8 copy.54
  400.3 148.9 %finish.1 = (f32[512,1536]{1,0:T(8,128)}, bf16[1536,768]{1,0:T(8,128)(2,1)}, bf16[256,384]{1,0:T(8,128)(2,1)}, f32[4,3,3072]{2,1,0:T(4,128)}) custom-call(bf16[512,3072]{1,0:T(8,128)(2,1)} %bitcast.85, bf16[512,3072]{1,0:T(8,128)(2,1)} %bitcast.115, bf16[8,512,384]{2,1,0:T(8,128)(2,1)} %bitcast.116, bf16[8,1536,512]{2,1,0:T(8,128)(2,1)} %bitcast.108, ...), custom_call_target="tpu_custom_call" | custom-call | flops 28991029248 | bytes 31457280 | tf_op jit(solution)/shard_map/finish/pallas_call | solution.py:960
  550.3 1.6 slice.155
  553.2 4.2 convert_element_type.131
  563.0 2.0 copy.47
  565.0 3.8 copy.62
  (151 shorter events, 39.3 us)
Async XLA Ops:
  7.2 58.5 %copy-start = (bf16[3072,128]{1,0:T(8,128)(2,1)S(1)}, bf16[3072,128]{1,0:T(8,128)(2,1)}, u32[]{:S(2)}) copy-start(bf16[3072,128]{1,0:T(8,128)(2,1)} %param.21) | copy-start | bytes 2359300
  7.2 153.0 %all-gather.6.cloned.1.call-start = ((), (), s32[]{:S(2)}) async-start(), calls=%async_computation.2 | async-start | bytes 14155776 | tf_op jit(solution)/shard_map/all_gather | solution.py:1055
  8.0 12.9 %copy-start.7 = (f32[1,1536]{1,0:T(1,128)}, f32[1,1536]{1,0:T(1,128)S(1)}, u32[]{:S(2)}) copy-start(f32[1,1536]{1,0:T(1,128)S(1)} %broadcast_in_dim.39.gain_ref) | copy-start | bytes 18436
  11.9 386.6 %reduce-scatter.4.cloned.1.call-start = ((), (), s32[]{:S(2)}) async-start(), calls=%async_computation.3 | async-start | bytes 2654208
  11.9 22.2 %copy-start.29 = (f32[4,3072]{1,0:T(4,128)S(1)}, f32[4,3072]{1,0:T(4,128)}, u32[]{:S(2)}) copy-start(f32[4,3072]{1,0:T(4,128)} %param.19) | copy-start | bytes 147460
  11.9 22.2 %copy-start.21 = (f32[16,3072]{1,0:T(8,128)S(1)}, f32[16,3072]{1,0:T(8,128)}, u32[]{:S(2)}) copy-start(f32[16,3072]{1,0:T(8,128)} %param.24) | copy-start | bytes 589828
  22.7 34.3 %collective-permute-start = (bf16[4,3,3072]{2,1,0:T(4,128)(2,1)S(1)}, bf16[4,3,3072]{2,1,0:T(4,128)(2,1)S(1)}, u32[]{:S(2)}, u32[]{:S(2)}) collective-permute-start(bf16[4,3,3072]{2,1,0:T(4,128)(2,1)S(1)} %slice.139), channel_id=1, source_target_pairs={{0,1},{1,2},{2,3},{3,4},{4,5},{5,6},{6,7},{8,9},{9,10},{10,11},{11... | collective-permute-start | bytes 221192 | tf_op jit(solution)/shard_map/ppermute | solution.py:107
  29.6 127.3 %collective-permute-start.2 = (bf16[384,512]{0,1:T(8,128)(2,1)}, bf16[384,512]{0,1:T(8,128)(2,1)}, u32[]{:S(2)}, u32[]{:S(2)}) collective-permute-start(bf16[384,512]{0,1:T(8,128)(2,1)} %get-tuple-element.103), channel_id=1, source_target_pairs={{0,8},{8,0},{16,24},{24,16},{1,9},{9,1},{17,25},{25,17},{2,10},{10... | collective-permute-start | bytes 1179656 | tf_op jit(solution)/shard_map/ppermute | solution.py:73
  30.8 127.2 %collective-permute-start.3 = (bf16[384,512]{0,1:T(8,128)(2,1)}, bf16[384,512]{0,1:T(8,128)(2,1)}, u32[]{:S(2)}, u32[]{:S(2)}) collective-permute-start(bf16[384,512]{0,1:T(8,128)(2,1)} %get-tuple-element.102), channel_id=1, source_target_pairs={{0,16},{8,24},{16,0},{24,8},{1,17},{9,25},{17,1},{25,9},{2,18},{10... | collective-permute-start | bytes 1179656 | tf_op jit(solution)/shard_map/ppermute | solution.py:73
  32.0 127.0 %collective-permute-start.4 = (bf16[384,512]{0,1:T(8,128)(2,1)}, bf16[384,512]{0,1:T(8,128)(2,1)}, u32[]{:S(2)}, u32[]{:S(2)}) collective-permute-start(bf16[384,512]{0,1:T(8,128)(2,1)} %get-tuple-element.101), channel_id=1, source_target_pairs={{0,24},{8,16},{16,8},{24,0},{1,25},{9,17},{17,9},{25,1},{2,26},{10... | collective-permute-start | bytes 1179656 | tf_op jit(solution)/shard_map/ppermute | solution.py:73
  34.9 10.9 %copy-start.17 = (bf16[4,128,1536]{2,1,0:T(8,128)(2,1)S(1)}, bf16[4,128,1536]{2,1,0:T(8,128)(2,1)}, u32[]{:S(2)}) copy-start(bf16[4,128,1536]{2,1,0:T(8,128)(2,1)} %param.27) | copy-start | bytes 4718596
  45.8 11.2 %copy-start.28 = (bf16[4,3,3072]{2,0,1:T(4,128)(2,1)S(1)}, bf16[4,3,3072]{2,0,1:T(4,128)(2,1)}, u32[]{:S(2)}) copy-start(bf16[4,3,3072]{2,0,1:T(4,128)(2,1)} %param.15) | copy-start | bytes 221188
  45.8 11.3 %copy-start.16 = (bf16[512,3072]{1,0:T(8,128)(2,1)S(1)}, bf16[512,3072]{1,0:T(8,128)(2,1)}, u32[]{:S(2)}) copy-start(bf16[512,3072]{1,0:T(8,128)(2,1)} %copy-done.15) | copy-start | bytes 9437188
  58.2 9.8 %copy-start.22 = (bf16[96,3072]{1,0:T(8,128)(2,1)S(1)}, bf16[96,3072]{1,0:T(8,128)(2,1)}, u32[]{:S(2)}) copy-start(bf16[96,3072]{1,0:T(8,128)(2,1)} %param.22) | copy-start | bytes 1769476
  58.2 9.7 %copy-start.36 = (f32[3072]{0:T(1024)S(1)}, f32[3072]{0:T(1024)}, u32[]{:S(2)}) copy-start(f32[3072]{0:T(1024)} %param.23) | copy-start | bytes 36868
  80.5 41.3 %copy-start.3 = (f32[16,3072]{1,0:T(8,128)S(1)}, f32[16,3072]{1,0:T(8,128)}, u32[]{:S(2)}) copy-start(f32[16,3072]{1,0:T(8,128)} %exponential_negate_fusion.a_ref) | copy-start | bytes 589828
  80.5 41.3 %copy-start.4 = (f32[4,16,3072]{2,1,0:T(8,128)S(1)}, f32[4,16,3072]{2,1,0:T(8,128)}, u32[]{:S(2)}) copy-start(f32[4,16,3072]{2,1,0:T(8,128)} %entry_ref.1) | copy-start | bytes 2359300
  160.1 165.2 %copy-start.18 = (bf16[384,2048]{0,1:T(8,128)(2,1)}, bf16[384,2048]{0,1:T(8,128)(2,1)S(1)}, u32[]{:S(2)}) copy-start(bf16[384,2048]{0,1:T(8,128)(2,1)S(1)} %constant_dynamic-update-slice_fusion.2) | copy-start | bytes 4718596
  160.2 168.5 %copy-start.23 = (bf16[96,3072]{1,0:T(8,128)(2,1)S(1)}, bf16[96,3072]{1,0:T(8,128)(2,1)}, u32[]{:S(2)}) copy-start(bf16[96,3072]{1,0:T(8,128)(2,1)} %param.22) | copy-start | bytes 1769476
  342.6 219.0 %all-gather.4.cloned.1.call-start = ((), (), s32[]{:S(2)}) async-start(), calls=%async_computation.1 | async-start | bytes 1474560 | tf_op jit(solution)/shard_map/all_gather | solution.py:1095
  347.5 16.3 %copy-start.20 = (f32[4,16,3072]{2,1,0:T(8,128)S(1)}, f32[4,16,3072]{2,1,0:T(8,128)}, u32[]{:S(2)}) copy-start(f32[4,16,3072]{2,1,0:T(8,128)} %get-tuple-element.54) | copy-start | bytes 2359300
  347.5 21.5 %copy-start.2 = (bf16[4,128,1536]{2,1,0:T(8,128)(2,1)S(1)}, bf16[4,128,1536]{2,1,0:T(8,128)(2,1)}, u32[]{:S(2)}) copy-start(bf16[4,128,1536]{2,1,0:T(8,128)(2,1)} %param.14) | copy-start | bytes 4718596
  358.4 28.4 %collective-permute-start.1 = (f32[4,3,3072]{2,1,0:T(4,128)}, f32[4,3,3072]{2,1,0:T(4,128)}, u32[]{:S(2)}, u32[]{:S(2)}) collective-permute-start(f32[4,3,3072]{2,1,0:T(4,128)} %fusion.14.halo_hbm), channel_id=1, source_target_pairs={{1,0},{2,1},{3,2},{4,3},{5,4},{6,5},{7,6},{9,8},{10,9},{11,10},{12... | collective-permute-start | bytes 442376 | tf_op jit(solution)/shard_map/ppermute | solution.py:107
  369.0 11.4 %copy-start.13 = (bf16[4,128,3072]{2,1,0:T(8,128)(2,1)S(1)}, bf16[4,128,3072]{2,1,0:T(8,128)(2,1)}, u32[]{:S(2)}) copy-start(bf16[4,128,3072]{2,1,0:T(8,128)(2,1)} %copy-done.12) | copy-start | bytes 9437188
  369.0 11.4 %copy-start.25 = (bf16[512,16]{0,1:T(8,128)(2,1)S(1)}, bf16[512,16]{0,1:T(8,128)(2,1)}, u32[]{:S(2)}) copy-start(bf16[512,16]{0,1:T(8,128)(2,1)} %copy.43) | copy-start | bytes 49156
  369.0 11.3 %copy-start.26 = (bf16[512,16]{0,1:T(8,128)(2,1)S(1)}, bf16[512,16]{0,1:T(8,128)(2,1)}, u32[]{:S(2)}) copy-start(bf16[512,16]{0,1:T(8,128)(2,1)} %copy.44) | copy-start | bytes 49156
  369.1 12.0 %copy-start.34 = (bf16[3072]{0:T(1024)(128)(2,1)S(1)}, bf16[3072]{0:T(1024)(128)(2,1)}, u32[]{:S(2)}) copy-start(bf16[3072]{0:T(1024)(128)(2,1)} %get-tuple-element.94) | copy-start | bytes 18436
  369.1 12.0 %copy-start.33 = (bf16[3072]{0:T(1024)(128)(2,1)S(1)}, bf16[3072]{0:T(1024)(128)(2,1)}, u32[]{:S(2)}) copy-start(bf16[3072]{0:T(1024)(128)(2,1)} %get-tuple-element.93) | copy-start | bytes 18436
  369.1 12.0 %copy-start.32 = (bf16[3072]{0:T(1024)(128)(2,1)S(1)}, bf16[3072]{0:T(1024)(128)(2,1)}, u32[]{:S(2)}) copy-start(bf16[3072]{0:T(1024)(128)(2,1)} %get-tuple-element.92) | copy-start | bytes 18436
  369.1 12.0 %copy-start.31 = (bf16[3072]{0:T(1024)(128)(2,1)S(1)}, bf16[3072]{0:T(1024)(128)(2,1)}, u32[]{:S(2)}) copy-start(bf16[3072]{0:T(1024)(128)(2,1)} %get-tuple-element.91) | copy-start | bytes 18436
  369.1 12.0 %copy-start.30 = (bf16[3072]{0:T(1024)(128)(2,1)S(1)}, bf16[3072]{0:T(1024)(128)(2,1)}, u32[]{:S(2)}) copy-start(bf16[3072]{0:T(1024)(128)(2,1)} %get-tuple-element.90) | copy-start | bytes 18436
  549.3 8.9 %copy-start.24 = (f32[4,3,3072]{2,1,0:T(4,128)S(1)}, f32[4,3,3072]{2,1,0:T(4,128)}, u32[]{:S(2)}) copy-start(f32[4,3,3072]{2,1,0:T(4,128)} %get-tuple-element.78) | copy-start | bytes 442372
  (15 other events, 41.1 us)
Sparse Core Ops, SparseCore 0:
  12.0 119.2 all-gather.5
  342.8 41.9 reduce-scatter.3
  400.5 36.1 all-gather.3

commit v4 on v3

--- a/solution.py
+++ b/solution.py
@@ -312,10 +312,11 @@
 
 
 def scan_kernel(
-    hosted, n_blocks_static, d_ref, act_ref, gate_ref, dg_ref, b_ref, c_ref, c_diag, b_diag, ones_ref, a_ref, skip_ref, start_ref, end_ref, first_ref,
+    hosted, n_blocks_static, n_ticks, d_ref, act_ref, gate_ref, dg_ref, b_ref, c_ref, c_diag, b_diag, ones_ref, a_ref, skip_ref, start_ref, end_ref, first_ref,
     gated_ref, dgate_ref, dpre_ref, dact_ref, db_ref, dc_ref, da_ref, sums_ref, gated_all, gate_all, first_all,
     history, drive, up, low_a, low_b, through_a, through_b, db_acc, dc_acc, sum_acc,
     gated_out, gate_out, gated_sent, gated_got, gate_sent, gate_got, own_sem, first_sent, first_got,
+    near_got, relay_sent, relay_got,
 ):
     states = a_ref.shape[0]
     length, width = d_ref.shape[1:]
@@ -330,6 +331,7 @@
     slot = lax.rem(tick, 2)
     channels = n_blocks_static * width // n_seq
     owners = width // channels if hosted else 0
+    relayed = n_dp == 4
 
     first_own = pltpu.make_async_copy(first_ref, first_all, first_got.at[0])
     first_far = pltpu.make_async_remote_copy(
@@ -350,7 +352,7 @@
         def _():
             first_own.start()
 
-    @pl.when(tick == jnp.minimum(my_seq, pl.num_programs(0) * n_blocks - 1))
+    @pl.when(tick == jnp.minimum(my_seq * max(1, n_ticks // n_seq), n_ticks - 1))
     def _():
         @pl.when(my_seq == 0)
         def _():
@@ -367,15 +369,40 @@
     def gated_copies(s, e, slot):
         at = (my_dp, s, slice(None), pl.ds(pl.multiple_of(e * width, LANES), width))
         own = pltpu.make_async_copy(gated_out.at[slot], gated_all.at[at], own_sem.at[slot, 0])
+        if relayed:
+            ids = [(my_dp ^ (1 + way), near_got.at[way, s * n_blocks + e], way) for way in range(2)]
+        else:
+            ids = [(lax.rem(my_dp + p, n_dp), gated_got.at[my_dp], p) for p in range(1, n_dp)]
         far = [
             pltpu.make_async_remote_copy(
                 src_ref=gated_out.at[slot], dst_ref=gated_all.at[at],
-                send_sem=gated_sent.at[slot, p], recv_sem=gated_got.at[my_dp],
-                device_id={"dp": lax.rem(my_dp + p, n_dp)}, device_id_type=MESH,
+                send_sem=gated_sent.at[slot, p], recv_sem=got,
+                device_id={"dp": peer}, device_id_type=MESH,
             )
-            for p in range(1, n_dp)
+            for peer, got, p in ids
         ]
         return own, far
+
+    def passed(s, e, way):
+        rows = slice(way * (length // 2), (way + 1) * (length // 2))
+        at = (my_dp ^ (1 + way), s, rows, pl.ds(pl.multiple_of(e * width, LANES), width))
+        return pltpu.make_async_remote_copy(
+            src_ref=gated_all.at[at], dst_ref=gated_all.at[at],
+            send_sem=relay_sent.at[way, s * n_blocks + e], recv_sem=relay_got.at[way],
+            device_id={"dp": my_dp ^ (2 - way)}, device_id_type=MESH,
+        )
+
+    def relay(t):
+        s, e = t // n_blocks, lax.rem(t, n_blocks)
+        for way in range(2):
+            peer = my_dp ^ (1 + way)
+            at = (peer, s, slice(None), pl.ds(pl.multiple_of(e * width, LANES), width))
+            pltpu.make_async_remote_copy(
+                src_ref=gated_out.at[0], dst_ref=gated_all.at[at],
+                send_sem=gated_sent.at[0, way], recv_sem=near_got.at[way, t],
+                device_id={"dp": peer}, device_id_type=MESH,
+            ).wait_recv()
+            passed(s, e, way).start()
 
     def gate_copies(s, e, slot):
         for q in range(owners):
@@ -462,6 +489,11 @@
     for part in range(parts):
         sum_y(chunks - 1, low_b, part)
     send(seg, block, slot)
+    if relayed:
+
+        @pl.when(tick >= 1)
+        def _():
+            relay(tick - 1)
 
     @pl.when(pl.program_id(1) == 0)
     def _():
@@ -538,8 +570,26 @@
     @pl.when(tick == pl.num_programs(0) * n_blocks - 1)
     def _():
         drain((tick - 1) // n_blocks, lax.rem(tick - 1, n_blocks), 1 - slot)
+        if relayed:
+            relay(tick)
         drain(seg, block, slot)
-        for p in range(1, n_dp):
+        if relayed:
+
+            def finish_relay(t, nothing):
+                for way in range(2):
+                    passed(t // n_blocks_static, lax.rem(t, n_blocks_static), way).wait_send()
+                return nothing
+
+            lax.fori_loop(0, n_ticks, finish_relay, 0)
+            across = my_dp ^ 3
+            for way in range(2):
+                at = (across, slice(None), slice(way * (length // 2), (way + 1) * (length // 2)))
+                pltpu.make_async_remote_copy(
+                    src_ref=gated_all.at[at], dst_ref=gated_all.at[at],
+                    send_sem=gated_sent.at[0, 0], recv_sem=relay_got.at[way],
+                    device_id={"dp": across}, device_id_type=MESH,
+                ).wait_recv()
+        for p in range(1, 1 if relayed else n_dp):
             source = lax.rem(my_dp + p, n_dp)
             pltpu.make_async_remote_copy(
                 src_ref=gated_all.at[source], dst_ref=gated_all.at[source],
@@ -580,7 +630,7 @@
     dma = pltpu.SemaphoreType.DMA
     out = pltpu.VMEM((2, length, width), BF16)
     return pl.pallas_call(
-        functools.partial(scan_kernel, hosted, inner // width),
+        functools.partial(scan_kernel, hosted, inner // width, segs * (inner // width)),
         grid=(segs, inner // width),
         in_specs=[
             tokens, tokens, tokens, tokens, wide, wide, diag, diag,
@@ -614,6 +664,7 @@
             out, out,
             dma((2, n_dp)), dma((n_dp,)), dma((2, n_seq)), dma((n_seq,)), dma((2, 1 + n_seq)),
             dma((1,)), dma((1,)),
+            dma((2, segs * (inner // width))), dma((2, segs * (inner // width))), dma((2,)),
         ],
         compiler_params=pltpu.CompilerParams(
             collective_id=2, has_side_effects=True, vmem_limit_bytes=VMEM_BYTES
@@ -626,10 +677,10 @@
 
 
 def finish_kernel(
-    gain_at, conv_hbm, gate_hbm, columns_hbm, normed_hbm, proj_hbm, tokens_hbm, cot_hbm, small_hbm, halo_hbm, gain_ref,
+    conv_hbm, gate_hbm, columns_hbm, normed_hbm, proj_hbm, tokens_hbm, cot_hbm, small_hbm, halo_hbm, gain_ref,
     d_tokens, d_in, small_out, halo_out,
     conv, gate, gate_columns, conv_columns, normed, proj, tokens, cot, small, d_normed,
-    partial, arrived, placed, small_low, small_dp, small_mid, small_seq,
+    partial, arrived, placed, small_dp, small_mid, small_seq,
     load, normed_load, proj_load, swap_sent, swap_got, swap_own, add_sent, add_got, put_sent, put_got, put_own,
     copy_sent, copy_got, mid_sent, mid_got, far_sent, far_got, last_sent, last_got, halo_sent, halo_got,
 ):
@@ -641,7 +692,8 @@
     channels = inner // n_seq
     chunks = channels // LANES
     rows_dp = width // n_dp
-    rows_small = small_low.shape[0] // n_dp
+    rows_small = small_hbm.shape[0] // n_dp
+    gain_rows = small_mid.shape[0] - rows_small
     dp_peers = [lax.rem(my_dp + p, n_dp) for p in range(n_dp)]
     seq_peers = [lax.rem(my_seq + p, n_seq) for p in range(n_seq)]
 
@@ -654,7 +706,7 @@
         pltpu.make_async_copy(src, dst, load.at[k])
         for k, (src, dst) in enumerate(
             [(columns_hbm, gate_columns), (conv_hbm, conv), (gate_hbm, gate), (tokens_hbm, tokens), (cot_hbm, cot),
-             (small_hbm, small_low)]
+             (small_hbm.at[pl.ds(pl.multiple_of(my_dp * rows_small, 16), rows_small)], small)]
         )
     ]
     load_columns, load_conv, load_gate, load_tokens, load_cot, load_small = loads
@@ -692,10 +744,13 @@
         pltpu.make_async_copy(conv_hbm.at[:, column_of(my_seq, c)], conv_columns.at[c, my_seq], swap_own.at[c])
         for c in range(chunks)
     ]
-    for c in range(chunks):
+
+    def start_swap(c):
         own_swaps[c].start()
         for p in range(1, n_seq):
             swap(c, p).start()
+
+    start_swap(0)
 
     def halo(p):
         return remote(halo_hbm, halo_out, halo_sent.at[p], halo_got.at[0], seq=p)
@@ -708,6 +763,16 @@
         for p in range(1, n_seq):
             halo(p).start()
 
+    def small_rows(device):
+        return pl.ds(pl.multiple_of(device * rows_small, 16), rows_small)
+
+    def small_add(p):
+        return remote(
+            small_hbm.at[small_rows(dp_peers[p])], small_dp.at[my_dp], mid_sent.at[p], mid_got.at[my_dp], dp=dp_peers[p]
+        )
+
+    for p in range(1, n_dp):
+        small_add(p).start()
     def product(c, columns):
         tile = 768 if width % 768 == 0 else 256
 
@@ -788,6 +853,8 @@
     for c in range(chunks):
         product(c, lambda s, c=c: gate_columns[s, :, c * LANES : (c + 1) * LANES])
         scatter(c)
+    if chunks > 1:
+        start_swap(1)
 
     load_conv.wait()
     load_gate.wait()
@@ -810,6 +877,8 @@
         if k == steps // 2:
             for c in range(chunks):
                 gather_add(c)
+            for c in range(2, chunks):
+                start_swap(c)
 
     load_tokens.wait()
     load_cot.wait()
@@ -826,35 +895,21 @@
 
     d_gain = lax.fori_loop(0, count // 32, some_tokens, jnp.zeros((1, width), F32))
     load_small.wait()
-    first = gain_at // 16 * 16
-    small[...] = small_low[first : first + 16, :].astype(F32)
-    for row in range(width // channels):
-        for s in range(n_seq):
-            at = gain_at - first + row
-            small[at : at + 1, s * channels : (s + 1) * channels] = d_gain[:, row * channels : (row + 1) * channels]
-    small_low[first : first + 16, :] = small[...].astype(BF16)
-
-    def small_rows(device):
-        return pl.ds(pl.multiple_of(device * rows_small, 16), rows_small)
-
-    def small_add(p):
-        return remote(
-            small_low.at[small_rows(dp_peers[p])], small_dp.at[my_dp], mid_sent.at[p], mid_got.at[my_dp], dp=dp_peers[p]
-        )
-
-    for p in range(1, n_dp):
-        small_add(p).start()
+    gains = jnp.concatenate([d_gain[:, r * channels : (r + 1) * channels] for r in range(width // channels)], axis=0)
+    gains = jnp.pad(gains, ((0, gain_rows - width // channels), (0, 0)))
+    for s in range(n_seq):
+        small_mid[rows_small:, s * channels : (s + 1) * channels] = gains.astype(BF16)
     for c in range(chunks):
         pass_on(c)
 
-    total = small_low[small_rows(my_dp), :].astype(F32)
+    total = small[...].astype(F32)
     for p in range(1, n_dp):
         remote(
-            small_low.at[small_rows(my_dp)], small_dp.at[dp_peers[p]], mid_sent.at[p], mid_got.at[dp_peers[p]],
+            small, small_dp.at[dp_peers[p]], mid_sent.at[p], mid_got.at[dp_peers[p]],
             dp=dp_peers[p],
         ).wait_recv()
         total += small_dp[dp_peers[p]].astype(F32)
-    small_mid[...] = total.astype(BF16)
+    small_mid[0:rows_small, :] = total.astype(BF16)
 
     def small_swap(p):
         at = pl.ds(pl.multiple_of(seq_peers[p] * channels, LANES), channels)
@@ -876,6 +931,11 @@
         scatter(chunks + c)
 
     convolved(0)
+    gather_add(chunks)
+    for c in range(1, chunks):
+        convolved(c)
+        pass_on(chunks + c - 1)
+        gather_add(chunks + c)
     total = small_mid[:, pl.ds(pl.multiple_of(my_seq * channels, LANES), channels)].astype(F32)
     for p in range(1, n_seq):
         remote(
@@ -883,23 +943,13 @@
             seq=seq_peers[p],
         ).wait_recv()
         total += small_seq[seq_peers[p]].astype(F32)
-    small_out[small_rows(my_dp), :] = total.astype(BF16)
+    small_out[my_dp] = total.astype(BF16)
 
     def small_spread(p):
-        at = small_rows(my_dp)
-        return remote(small_out.at[at], small_out.at[at], last_sent.at[p], last_got.at[my_dp], dp=dp_peers[p])
+        return remote(small_out.at[my_dp], small_out.at[my_dp], last_sent.at[p], last_got.at[my_dp], dp=dp_peers[p])
 
     for p in range(1, n_dp):
         small_spread(p).start()
-
-    for c in range(1, chunks):
-        convolved(c)
-        gather_add(chunks + c - 1)
-        if c >= 2:
-            pass_on(chunks + c - 2)
-    gather_add(2 * chunks - 1)
-    if chunks >= 2:
-        pass_on(2 * chunks - 2)
     pass_on(2 * chunks - 1)
 
     for c in range(chunks):
@@ -929,7 +979,7 @@
         small_spread(p).wait_send()
         peer = dp_peers[p]
         remote(
-            small_out.at[small_rows(peer)], small_out.at[small_rows(peer)], last_sent.at[p], last_got.at[peer], dp=peer
+            small_out.at[peer], small_out.at[peer], last_sent.at[p], last_got.at[peer], dp=peer
         ).wait_recv()
     for p in range(1, n_seq):
         small_swap(p).wait_send()
@@ -945,38 +995,39 @@
         halo(1).wait_recv()
 
 
-def finish(d_conv_in, d_gate, gate_columns, normed_all, in_proj, tokens, cot, small, gain_at, halo_grad, norm_gain):
+def finish(d_conv_in, d_gate, gate_columns, normed_all, in_proj, tokens, cot, small, halo_grad, norm_gain):
     n_dp, n_seq = lax.axis_size("dp"), lax.axis_size("seq")
     count, inner = d_conv_in.shape
     width = tokens.shape[1]
     channels = inner // n_seq
     chunks = channels // LANES
-    rows = small.shape[0]
+    rows = small.shape[0] // n_dp
+    gain_rows = -(-width // channels // 16) * 16
     depth = 1024 if inner % 1024 == 0 else LANES
     dma = pltpu.SemaphoreType.DMA
     vmem = pltpu.VMEM
     anywhere = pl.BlockSpec(memory_space=pl.ANY)
     inside = pl.BlockSpec(memory_space=pltpu.VMEM)
     return pl.pallas_call(
-        functools.partial(finish_kernel, gain_at),
+        finish_kernel,
         in_specs=[anywhere] * 9 + [inside],
         out_specs=[inside, anywhere, inside, anywhere],
         out_shape=[
             jax.ShapeDtypeStruct((count, width), F32),
             jax.ShapeDtypeStruct((width, 2 * channels), BF16),
-            jax.ShapeDtypeStruct((rows, channels), BF16),
+            jax.ShapeDtypeStruct((n_dp, rows + gain_rows, channels), BF16),
             jax.ShapeDtypeStruct(halo_grad.shape, F32),
         ],
         scratch_shapes=[
             vmem((count, inner), BF16), vmem((count, inner), BF16),
             vmem((n_seq, count, channels), BF16), vmem((chunks, n_seq, count, LANES), BF16),
             vmem((n_seq, width, count), BF16), vmem((2, width, depth), BF16),
-            vmem((count, width), BF16), vmem((count, width), BF16), vmem((16, inner), F32),
+            vmem((count, width), BF16), vmem((count, width), BF16), vmem((rows, inner), BF16),
             vmem((count, width), F32),
             vmem((2 * chunks, width, LANES), BF16), vmem((2 * chunks, n_dp, width // n_dp, LANES), BF16),
             vmem((2 * chunks, width // n_dp, LANES), BF16),
-            vmem((rows, inner), BF16), vmem((n_dp, rows // n_dp, inner), BF16), vmem((rows // n_dp, inner), BF16),
-            vmem((n_seq, rows // n_dp, channels), BF16),
+            vmem((n_dp, rows, inner), BF16), vmem((rows + gain_rows, inner), BF16),
+            vmem((n_seq, rows + gain_rows, channels), BF16),
             dma((6,)), dma((n_seq,)), dma((2,)),
             dma((chunks, n_seq)), dma((chunks, n_seq)), dma((chunks,)),
             dma((2 * chunks, n_dp)), dma((2 * chunks, n_dp)),
@@ -1128,21 +1179,17 @@
         )
         edge_at = 2 * rank + 3 * states + 2
         channels = inner // n_seq
-        gain_rows = width // channels
-        gain_at = small.shape[0]
-        if gain_at % 16 + gain_rows > 16:
-            gain_at += -gain_at % 16
-        rows = gain_at + gain_rows
-        rows += -rows % (16 * lax.axis_size("dp"))
-        small = jnp.pad(small, ((0, rows - small.shape[0]), (0, 0)))
+        small = jnp.pad(small, ((0, -small.shape[0] % (16 * lax.axis_size("dp"))), (0, 0)))
+        rows = small.shape[0] // lax.axis_size("dp")
         d_tokens, d_in_proj, small, d_conv_state = finish(
             d_conv_in, d_gate, gate_columns.reshape(n_seq, count, channels), normed_all, in_proj, flat(tokens), cot,
-            small, gain_at, halo_grad, norm_gain,
+            small, halo_grad, norm_gain,
         )
         d_in_proj, small = d_in_proj.astype(F32), small.astype(F32)
-        edges = small[edge_at:gain_at]
-        d_norm_gain = small[gain_at : gain_at + gain_rows].reshape(n_seq, -1)
-        d_norm_gain = lax.dynamic_index_in_dim(d_norm_gain, mine, 0, keepdims=False)
+        gain = jnp.sum(small[:, rows : rows + width // channels], axis=0)
+        small = small[:, :rows].reshape(-1, channels)
+        edges = small[edge_at:]
+        d_norm_gain = lax.dynamic_index_in_dim(gain.reshape(n_seq, -1), mine, 0, keepdims=False)
     else:
         d_conv_state = from_first(halo_grad, "seq")
 

time: 581 us -> 565 us (0.972)
  Pallas kernels: 387 us -> 355 us
  starting transfers between devices: 12.8 us -> 22.6 us
    pallas_call x2, Pallas kernels: 314 us -> 283 us  [the longest x1 150 us: scan_both(): pl.pallas_call(functools.partial(scan_kernel, hosted, inner // width, seg...]
    ppermute x2, starting transfers between devices: 10.1 us -> 19.8 us  [shifted(): return lax.ppermute(block, axis, route)]
    unnamed x85 -> x64, local copies, waits for them, and re-layouts: 25.7 us -> 27.8 us
  transfers between devices with their start and end apart: 8 -> 8, of which waited for: 0 -> 0; matrix products, arithmetic and copies ran while one was open for 21% -> 22% of each run, Pallas kernels for 38% -> 36%
where the time goes in v4:
time: 565 us; the launch traced here: 560 us
  Pallas kernels  355 us (63%)
  matrix products  73.1 us (13%)
  local copies, waits for them, and re-layouts  55.4 us (10%)
  other arithmetic  39.4 us (7%)
  starting transfers between devices  22.6 us (4%)
  between operations  14.5 us (3%)
    pallas_call x1, Pallas kernels, scan_both(): pl.pallas_call(functools.partial(scan_kernel, hosted, inner // width, seg...  150 us
    pallas_call x1, Pallas kernels, finish(): pl.pallas_call(finish_kernel, in_specs=[anywhere] * 9 + [inside], out_spe...  133 us
    dot_general x9, matrix products, matmul(): lax.dot_general(left, right, (((1,), (0,)), ((), ())), preferred_element_...  51 us
    pallas_call x1, Pallas kernels, block_ends(): pl.pallas_call(ends_kernel, grid=(segs, inner // width), in_specs=[tokens...  41.1 us
    pallas_call x1, Pallas kernels, carry(): pl.pallas_call(functools.partial(carry_kernel, pieces), in_specs=[vmem] *...  28.8 us
    unnamed x64, local copies, waits for them, and re-layouts  27.8 us
    ppermute x2, starting transfers between devices, shifted(): return lax.ppermute(block, axis, route)  19.8 us
    dot_general x3, matrix products, matmul_nt(): lax.dot_general(left, right, (((1,), (1,)), ((), ())), preferred_element_...  18.1 us
  transfers between devices with their start and end apart: 8, of which 0 were waited for; matrix products, arithmetic and copies ran while one was open for 22% of the time, Pallas kernels for 36%

profile of v4, /device:TPU:1, one launch (start us, length us, event | category | flops | bytes accessed | tf_op | source)
XLA Modules:
  0.0 560.3 jit_solution(2006342380343634644)
XLA Ops:
  9.4 2.4 norm.1
  11.9 9.0 %fusion.7 = bf16[512,3072]{1,0:T(8,128)(2,1)S(1)} fusion(bf16[512,1536]{1,0:T(8,128)(2,1)S(1)} %get-tuple-element.38, bf16[1536,6144]{1,0:T(8,128)(2,1)} %proj_hbm.1), kind=kOutput, calls=%fused_computation.19 | convolution fusion | flops 4833411072 | bytes 14155776 | tf_op jit(solution)/shard_map/dot_general | solution.py:27
  22.7 4.6 collective-permute-start
  27.3 2.3 dynamic-slice_bitcast_fusion
  34.2 10.9 %fusion.2 = f32[512,3072]{1,0:T(8,128)} fusion(bf16[512,1536]{1,0:T(8,128)(2,1)S(1)} %get-tuple-element.38, bf16[1536,6144]{1,0:T(8,128)(2,1)} %proj_hbm.1), kind=kOutput, calls=%fused_computation.3 | convolution fusion | flops 4831838208 | bytes 17301504 | tf_op jit(solution)/shard_map/dot_general | solution.py:27
  45.2 11.1 %fusion.dg_ref = f32[4,128,3072]{2,1,0:T(8,128)} fusion(bf16[4,128,1536]{2,1,0:T(8,128)(2,1)S(1)} %copy-done.17, bf16[3072,1536]{1,0:T(8,128)(2,1)} %param.26), kind=kOutput, calls=%fused_computation.1 | convolution fusion | flops 4831838208 | bytes 17301504 | tf_op jit(solution)/shard_map/dot_general | solution.py:31
  59.5 6.0 %multiply_convert_fusion = (bf16[4,128,3072]{2,1,0:T(8,128)(2,1)S(1)}, f32[4,128,3072]{2,1,0:T(8,128)}) fusion(f32[4,131,3072]{2,1,0:T(8,128)S(1)} %maximum_convert_fusion, f32[3072]{0:T(1024)S(1)} %bitcast.112, f32[3072]{0:T(1024)S(1)} %bitcast.108, f32[3072]{0:T(1024)S(1)} %bitcast.105, f32[3072]{0:T(1024)S(1)} %bitcast.102, f32[3072]{0:T(1024)S(1)} %copy-done.25), kind=kLoop, calls=%fused_computation.16 | loop fusion | flops 20447232 | bytes 34664448 | tf_op jit(solution)/shard_map/convert_element_type | solution.py:1117
  69.3 6.6 %bitcast_reduce_fusion = (f32[4,3072]{1,0:T(4,128)S(1)}, f32[512,3072]{1,0:T(8,128)}) fusion(f32[3072]{0:T(1024)S(1)} %copy-done.26, bf16[96,3072]{1,0:T(8,128)(2,1)S(1)} %copy-done.20, f32[512,128]{0,1:T(8,128)S(1)} %fusion.26), kind=kOutput, calls=%fused_computation.62 | convolution fusion | flops 314560512 | bytes 7041024 | tf_op jit(solution)/shard_map/dot_general | solution.py:27
  76.4 2.6 broadcast_in_dim.41.b_ref
  79.1 2.8 broadcast_in_dim.43.c_ref
  81.9 41.1 %block_ends.1 = (f32[4,16,3072]{2,1,0:T(8,128)}, f32[4,16,3072]{2,1,0:T(8,128)}) custom-call(f32[4,128,3072]{2,1,0:T(8,128)} %bitcast.120, bf16[4,128,3072]{2,1,0:T(8,128)(2,1)} %copy-done.12, f32[4,128,3072]{2,1,0:T(8,128)} %bitcast.118, f32[4,128,3072]{2,1,0:T(8,128)} %fusion.dg_ref, f32[4,128,16,128]{3,2,1,0:T(8,128)} %broadcast_in_dim.41.b_ref, ...), custom_call_target="tpu_custom_call" | custom-call | flops 226492416 | bytes 18874368 | tf_op jit(solution)/shard_map/block_ends/pallas_call | solution.py:299
  125.4 28.8 %carry.1 = (f32[4,16,3072]{2,1,0:T(8,128)S(1)}, f32[4,16,3072]{2,1,0:T(8,128)S(1)}, f32[4,16,3072]{2,1,0:T(8,128)S(1)}) custom-call(f32[4,16,3072]{2,1,0:T(8,128)S(1)} %copy-done.5, f32[4,16,3072]{2,1,0:T(8,128)S(1)} %copy-done.6, f32[4,1,3072]{2,1,0:T(1,128)S(1)} %broadcast_in_dim.46.total_ref, f32[4,16,3072]{2,1,0:T(8,128)S(1)} %copy-done.4, ...), custom_call_target="tpu_custom_call" | custom-call | tf_op jit(solution)/shard_map/carry/pallas_call | solution.py:228
  159.6 1.8 constant_dynamic-update-slice_fusion
  161.4 1.8 constant_dynamic-update-slice_fusion.2
  163.1 150.0 %scan_both.1 = (bf16[4,128,3072]{2,1,0:T(8,128)(2,1)}, bf16[4,128,3072]{2,1,0:T(8,128)(2,1)}, bf16[4,128,3072]{2,1,0:T(8,128)(2,1)}, f32[4,128,3072]{2,1,0:T(8,1...) custom-call(f32[4,128,3072]{2,1,0:T(8,128)} %bitcast.121, ...), custom_call_target="tpu_custom_call" | custom-call | flops 503316480 | bytes 37748736 | tf_op jit(solution)/shard_map/scan_both/pallas_call | solution.py:632
  315.3 3.0 convolution_convert_fusion.3
  318.3 9.5 %convolution_convert_fusion = bf16[384,3072]{1,0:T(8,128)(2,1)} fusion(bf16[384,2048]{0,1:T(8,128)(2,1)} %constant_dynamic-update-slice_fusion.2, bf16[2048,3072]{1,0:T(8,128)(2,1)} %bitcast.117), kind=kOutput, calls=%fused_computation.20 | convolution fusion | flops 4833017856 | bytes 16515072 | tf_op jit(solution)/shard_map/dot_general | solution.py:27
  327.8 4.3 copy.53
  332.2 3.9 bitcast_add_fusion
  336.9 6.8 %multiply_reduce_fusion = (bf16[3072]{0:T(1024)(128)(2,1)S(1)}, bf16[3072]{0:T(1024)(128)(2,1)S(1)}, bf16[3072]{0:T(1024)(128)(2,1)S(1)}, bf16[3072]{0:T(1024)(1...) fusion(f32[4,131,3072]{2,1,0:T(8,128)S(1)} %bitcast.77, f32[4,128,3072]{2,1,0:T(8,128)} %get-tuple-element.100, ...), kind=kLoop, calls=%fused_computation.8 | loop fusion | flops 26723328 | bytes 44070912 | tf_op jit(solution)/shard_map/reduce_sum | solution.py:1160
  343.8 2.5 copy-done.14
  347.2 15.2 %collective-permute-start.1 = (f32[4,3,3072]{2,1,0:T(4,128)}, f32[4,3,3072]{2,1,0:T(4,128)}, u32[]{:S(2)}, u32[]{:S(2)}) collective-permute-start(f32[4,3,3072]{2,1,0:T(4,128)} %fusion.14.halo_hbm), channel_id=1, source_target_pairs={{1,0},{2,1},{3,2},{4,3},{5,4},{6,5},{7,6},{9,8},{10,9},{11,10},{12... | collective-permute-start | bytes 442376 | tf_op jit(solution)/shard_map/ppermute | solution.py:107
  363.6 3.4 convolution_convert_fusion.2
  367.0 11.2 %convolution_add_fusion = f32[512,1536]{1,0:T(8,128)} fusion(bf16[512,3072]{1,0:T(8,128)(2,1)} %bitcast.125, bf16[3072,1536]{1,0:T(8,128)(2,1)} %param.26, bf16[512,1536]{1,0:T(8,128)(2,1)S(1)} %bitcast.75), kind=kOutput, calls=%fused_computation.24 | convolution fusion | flops 4833411072 | bytes 17301504 | tf_op jit(solution)/shard_map/dot_general | solution.py:27
  380.0 3.2 concatenate.13
  384.5 11.8 %add_convert_fusion = bf16[4,128,3072]{2,1,0:T(8,128)(2,1)} fusion(f32[4,3,3072]{2,1,0:T(4,128)} %collective-permute-done.1, f32[4,128,3072]{2,1,0:T(8,128)} %copy-done.14, f32[3072]{0:T(1024)S(1)} %bitcast.113, f32[3072]{0:T(1024)S(1)} %bitcast.110, f32[3072]{0:T(1024)S(1)} %bitcast.107, f32[3072]{0:T(1024)S(1)} %bitcast.104), kind=kLoop, calls=%fused_computation.12 | loop fusion | flops 14155776 | bytes 9633792 | tf_op jit(solution)/shard_map/convert_element_type | solution.py:1169
  396.3 1.8 copy.54
  398.2 132.9 %finish.1 = (f32[512,1536]{1,0:T(8,128)}, bf16[1536,768]{1,0:T(8,128)(2,1)}, bf16[4,80,384]{2,1,0:T(8,128)(2,1)}, f32[4,3,3072]{2,1,0:T(4,128)}) custom-call(bf16[512,3072]{1,0:T(8,128)(2,1)} %bitcast.86, bf16[512,3072]{1,0:T(8,128)(2,1)} %bitcast.122, bf16[8,512,384]{2,1,0:T(8,128)(2,1)} %bitcast.123, bf16[8,1536,512]{2,1,0:T(8,128)(2,1)} %bitcast.115, ...), custom_call_target="tpu_custom_call" | custom-call | flops 28991029248 | bytes 31457280 | tf_op jit(solution)/shard_map/finish/pallas_call | solution.py:1011
  535.9 4.2 convert_element_type.131
  543.0 2.8 convert_bitcast_fusion
  545.8 3.1 copy.47
  548.9 3.8 copy.62
  (133 shorter events, 40.3 us)
Async XLA Ops:
  7.2 59.9 %copy-start = (bf16[3072,128]{1,0:T(8,128)(2,1)S(1)}, bf16[3072,128]{1,0:T(8,128)(2,1)}, u32[]{:S(2)}) copy-start(bf16[3072,128]{1,0:T(8,128)(2,1)} %param.21) | copy-start | bytes 2359300
  7.2 155.9 %all-gather.6.cloned.1.call-start = ((), (), s32[]{:S(2)}) async-start(), calls=%async_computation.2 | async-start | bytes 14155776 | tf_op jit(solution)/shard_map/all_gather | solution.py:1106
  8.0 12.9 %copy-start.7 = (f32[1,1536]{1,0:T(1,128)}, f32[1,1536]{1,0:T(1,128)S(1)}, u32[]{:S(2)}) copy-start(f32[1,1536]{1,0:T(1,128)S(1)} %broadcast_in_dim.39.gain_ref) | copy-start | bytes 18436
  8.0 1.4 copy-start.1
  11.9 384.4 %reduce-scatter.4.cloned.1.call-start = ((), (), s32[]{:S(2)}) async-start(), calls=%async_computation.3 | async-start | bytes 2654208
  11.9 21.6 %copy-start.24 = (f32[4,3072]{1,0:T(4,128)S(1)}, f32[4,3072]{1,0:T(4,128)}, u32[]{:S(2)}) copy-start(f32[4,3072]{1,0:T(4,128)} %param.19) | copy-start | bytes 147460
  11.9 21.6 %copy-start.19 = (f32[16,3072]{1,0:T(8,128)S(1)}, f32[16,3072]{1,0:T(8,128)}, u32[]{:S(2)}) copy-start(f32[16,3072]{1,0:T(8,128)} %param.24) | copy-start | bytes 589828
  20.9 1.7 copy-start.15
  22.7 35.7 %collective-permute-start = (bf16[4,3,3072]{2,1,0:T(4,128)(2,1)S(1)}, bf16[4,3,3072]{2,1,0:T(4,128)(2,1)S(1)}, u32[]{:S(2)}, u32[]{:S(2)}) collective-permute-start(bf16[4,3,3072]{2,1,0:T(4,128)(2,1)S(1)} %slice.148), channel_id=1, source_target_pairs={{0,1},{1,2},{2,3},{3,4},{4,5},{5,6},{6,7},{8,9},{9,10},{10,11},{11... | collective-permute-start | bytes 221192 | tf_op jit(solution)/shard_map/ppermute | solution.py:107
  29.6 128.2 %collective-permute-start.2 = (bf16[384,512]{0,1:T(8,128)(2,1)}, bf16[384,512]{0,1:T(8,128)(2,1)}, u32[]{:S(2)}, u32[]{:S(2)}) collective-permute-start(bf16[384,512]{0,1:T(8,128)(2,1)} %get-tuple-element.103), channel_id=1, source_target_pairs={{0,8},{8,0},{16,24},{24,16},{1,9},{9,1},{17,25},{25,17},{2,10},{10... | collective-permute-start | bytes 1179656 | tf_op jit(solution)/shard_map/ppermute | solution.py:73
  30.8 128.8 %collective-permute-start.3 = (bf16[384,512]{0,1:T(8,128)(2,1)}, bf16[384,512]{0,1:T(8,128)(2,1)}, u32[]{:S(2)}, u32[]{:S(2)}) collective-permute-start(bf16[384,512]{0,1:T(8,128)(2,1)} %get-tuple-element.102), channel_id=1, source_target_pairs={{0,16},{8,24},{16,0},{24,8},{1,17},{9,25},{17,1},{25,9},{2,18},{10... | collective-permute-start | bytes 1179656 | tf_op jit(solution)/shard_map/ppermute | solution.py:73
  32.0 129.3 %collective-permute-start.4 = (bf16[384,512]{0,1:T(8,128)(2,1)S(1)}, bf16[384,512]{0,1:T(8,128)(2,1)}, u32[]{:S(2)}, u32[]{:S(2)}) collective-permute-start(bf16[384,512]{0,1:T(8,128)(2,1)S(1)} %get-tuple-element.101), channel_id=1, source_target_pairs={{0,24},{8,16},{16,8},{24,0},{1,25},{9,17},{17,9},{25,1},{2,26},{10... | collective-permute-start | bytes 1179656 | tf_op jit(solution)/shard_map/ppermute | solution.py:73
  34.2 10.9 %copy-start.17 = (bf16[4,128,1536]{2,1,0:T(8,128)(2,1)S(1)}, bf16[4,128,1536]{2,1,0:T(8,128)(2,1)}, u32[]{:S(2)}) copy-start(bf16[4,128,1536]{2,1,0:T(8,128)(2,1)} %param.27) | copy-start | bytes 4718596
  45.2 13.2 %copy-start.23 = (bf16[4,3,3072]{2,0,1:T(4,128)(2,1)S(1)}, bf16[4,3,3072]{2,0,1:T(4,128)(2,1)}, u32[]{:S(2)}) copy-start(bf16[4,3,3072]{2,0,1:T(4,128)(2,1)} %param.15) | copy-start | bytes 221188
  45.2 13.3 %copy-start.16 = (bf16[512,3072]{1,0:T(8,128)(2,1)S(1)}, bf16[512,3072]{1,0:T(8,128)(2,1)}, u32[]{:S(2)}) copy-start(bf16[512,3072]{1,0:T(8,128)(2,1)} %copy-done.15) | copy-start | bytes 9437188
  56.3 3.2 copy-start.25
  59.4 6.0 %copy-start.11 = (f32[4,131,3072]{2,1,0:T(8,128)}, f32[4,131,3072]{2,1,0:T(8,128)S(1)}, u32[]{:S(2)}) copy-start(f32[4,131,3072]{2,1,0:T(8,128)S(1)} %maximum_convert_fusion) | copy-start | bytes 19316740
  59.5 9.9 %copy-start.20 = (bf16[96,3072]{1,0:T(8,128)(2,1)S(1)}, bf16[96,3072]{1,0:T(8,128)(2,1)}, u32[]{:S(2)}) copy-start(bf16[96,3072]{1,0:T(8,128)(2,1)} %param.22) | copy-start | bytes 1769476
  59.5 9.9 %copy-start.26 = (f32[3072]{0:T(1024)S(1)}, f32[3072]{0:T(1024)}, u32[]{:S(2)}) copy-start(f32[3072]{0:T(1024)} %param.23) | copy-start | bytes 36868
  65.4 1.7 copy-start.12
  81.9 41.2 %copy-start.3 = (f32[16,3072]{1,0:T(8,128)S(1)}, f32[16,3072]{1,0:T(8,128)}, u32[]{:S(2)}) copy-start(f32[16,3072]{1,0:T(8,128)} %exponential_negate_fusion.a_ref) | copy-start | bytes 589828
  81.9 41.2 %copy-start.4 = (f32[4,16,3072]{2,1,0:T(8,128)S(1)}, f32[4,16,3072]{2,1,0:T(8,128)}, u32[]{:S(2)}) copy-start(f32[4,16,3072]{2,1,0:T(8,128)} %entry_ref.1) | copy-start | bytes 2359300
  163.1 152.1 %copy-start.21 = (bf16[96,3072]{1,0:T(8,128)(2,1)S(1)}, bf16[96,3072]{1,0:T(8,128)(2,1)}, u32[]{:S(2)}) copy-start(bf16[96,3072]{1,0:T(8,128)(2,1)} %param.22) | copy-start | bytes 1769476
  332.1 210.9 %all-gather.4.cloned.1.call-start = ((), (), s32[]{:S(2)}) async-start(), calls=%async_computation.1 | async-start | bytes 1474560 | tf_op jit(solution)/shard_map/all_gather | solution.py:1146
  332.1 4.0 slice-start
  332.2 4.8 slice-start.1
  336.9 30.1 %copy-start.2 = (bf16[4,128,1536]{2,1,0:T(8,128)(2,1)S(1)}, bf16[4,128,1536]{2,1,0:T(8,128)(2,1)}, u32[]{:S(2)}) copy-start(bf16[4,128,1536]{2,1,0:T(8,128)(2,1)} %param.14) | copy-start | bytes 4718596
  343.7 2.6 copy-start.14
  347.2 37.4 %collective-permute-start.1 = (f32[4,3,3072]{2,1,0:T(4,128)}, f32[4,3,3072]{2,1,0:T(4,128)}, u32[]{:S(2)}, u32[]{:S(2)}) collective-permute-start(f32[4,3,3072]{2,1,0:T(4,128)} %fusion.14.halo_hbm), channel_id=1, source_target_pairs={{1,0},{2,1},{3,2},{4,3},{5,4},{6,5},{7,6},{9,8},{10,9},{11,10},{12... | collective-permute-start | bytes 442376 | tf_op jit(solution)/shard_map/ppermute | solution.py:107
  367.0 11.3 %copy-start.13 = (bf16[4,128,3072]{2,1,0:T(8,128)(2,1)S(1)}, bf16[4,128,3072]{2,1,0:T(8,128)(2,1)}, u32[]{:S(2)}) copy-start(bf16[4,128,3072]{2,1,0:T(8,128)(2,1)} %copy-done.12) | copy-start | bytes 9437188
  531.1 9.9 %copy-start.22 = (f32[4,3,3072]{2,1,0:T(4,128)S(1)}, f32[4,3,3072]{2,1,0:T(4,128)}, u32[]{:S(2)}) copy-start(f32[4,3,3072]{2,1,0:T(4,128)} %get-tuple-element.78) | copy-start | bytes 442372
  545.8 6.9 %copy-start.18 = (f32[4,16,3072]{2,1,0:T(8,128)S(1)}, f32[4,16,3072]{2,1,0:T(8,128)}, u32[]{:S(2)}) copy-start(f32[4,16,3072]{2,1,0:T(8,128)} %get-tuple-element.131) | copy-start | bytes 2359300
  (5 other events, 5.0 us)
Sparse Core Ops, SparseCore 0:
  12.0 119.2 all-gather.5
  332.2 45.0 reduce-scatter.3
  398.3 43.4 all-gather.3

commit v5 on v4

--- a/solution.py
+++ b/solution.py
@@ -219,7 +219,7 @@
 
 
 def carry(ends, entry_mu, total, entry_state, a_mat):
-    pieces = 6
+    pieces = 4
     while ends.shape[2] % (pieces * LANES):
         pieces -= 1
     shape = jax.ShapeDtypeStruct(ends.shape, F32)
@@ -240,7 +240,7 @@
 
 def aligned(inner, axis="seq"):
     channels = inner // lax.axis_size(axis)
-    return channels % LANES == 0 and widest(inner, 768) % channels == 0
+    return channels % LANES == 0 and widest(inner, 1536) % channels == 0
 
 
 def spread_row(ref, rows, at, tile, states):
@@ -291,7 +291,7 @@
 def block_ends(delta, act, gate_in, d_gated, b_wide, c_wide, a_mat):
     segs, length, inner = delta.shape
     states = a_mat.shape[0]
-    width = widest(inner, 512)
+    width = widest(inner, 768)
     tokens = pl.BlockSpec((1, length, width), lambda s, e: (s, 0, e))
     wide = pl.BlockSpec((1, length, states, LANES), lambda s, e: (s, 0, 0, 0))
     state = pl.BlockSpec((1, states, width), lambda s, e: (s, 0, e))
@@ -613,7 +613,7 @@
 def scan_both(delta, act, gate_in, d_gated, b_wide, c_wide, c_diag, b_diag, ones_diag, a_mat, d_skip, start, end, first):
     segs, length, inner = delta.shape
     states = a_mat.shape[0]
-    width = widest(inner, 768)
+    width = widest(inner, 1536)
     tokens = pl.BlockSpec((1, length, width), lambda s, e: (s, 0, e))
     wide = pl.BlockSpec((1, length, states, LANES), lambda s, e: (s, 0, 0, 0))
     diag = pl.BlockSpec((1,) + c_diag.shape[1:], lambda s, e: (s, 0, 0, 0))
@@ -1056,6 +1056,75 @@
     return (tiled.reshape(segs, length // CHUNK, CHUNK, CHUNK * states) * mask).astype(BF16)
 
 
+def conv_back_kernel(
+    d_act_ref, coeff_ref, proj_ref, conv_ref, before_ref, weight_ref, bias_ref,
+    d_in_ref, last_ref, halo_ref, sums_ref, padded, d_out,
+):
+    taps = weight_ref.shape[0]
+    halo = taps - 1
+    length, width = conv_ref.shape[1:]
+    padded[8 - halo : 8, :] = before_ref[0].astype(F32)
+    padded[8 : 8 + length, :] = conv_ref[0].astype(F32)
+    d_out[length : length + 8, :] = jnp.zeros((8, width), F32)
+    coeff = coeff_ref[0]
+    for j in range(width // LANES):
+        at = column(j)
+        weight = [weight_ref[tap : tap + 1, at] for tap in range(taps)]
+        inputs = [padded[8 - halo + tap : 8 - halo + tap + length, at] for tap in range(taps)]
+        conv_out = bias_ref[:, at] + sum(weight[tap] * inputs[tap] for tap in range(taps))
+        d_act = d_act_ref[0, :, at] + matmul_nt(coeff, proj_ref[at, :])
+        d_conv = d_act * silu_parts(conv_out)[1]
+        d_out[0:length, at] = d_conv
+        for tap in range(taps):
+            sums_ref[0, tap : tap + 1, at] = jnp.sum(d_conv * inputs[tap], axis=0, keepdims=True)
+        sums_ref[0, taps : taps + 1, at] = jnp.sum(d_conv, axis=0, keepdims=True)
+        d_in = sum(weight[tap] * d_out[halo - tap : halo - tap + length, at] for tap in range(taps))
+        d_in_ref[0, :, at] = d_in.astype(BF16)
+        last_ref[0, :, at] = d_in[length - 8 :]
+        for row in range(halo):
+            halo_ref[0, row : row + 1, at] = sum(
+                weight[tap] * d_conv[row - tap : row - tap + 1] for tap in range(row + 1)
+            )
+    sums_ref[0, taps + 1 :, :] = jnp.zeros((8 - taps - 1, width), F32)
+
+
+def conv_back(d_act, d_coeffs, x_proj, conv_in, before, conv_weight, conv_bias):
+    segs, length, inner = conv_in.shape
+    width = widest(inner, 1536)
+    taps, halo = conv_weight.shape[0], before.shape[1]
+    tokens = pl.BlockSpec((1, length, width), lambda s, e: (s, 0, e))
+
+    def rows(count):
+        return pl.BlockSpec((1, count, width), lambda s, e: (s, 0, e))
+
+    return pl.pallas_call(
+        conv_back_kernel,
+        grid=(segs, inner // width),
+        in_specs=[
+            tokens,
+            pl.BlockSpec((1, length, d_coeffs.shape[2]), lambda s, e: (s, 0, 0)),
+            pl.BlockSpec((width, x_proj.shape[1]), lambda s, e: (e, 0)),
+            tokens,
+            rows(halo),
+            pl.BlockSpec((taps, width), lambda s, e: (0, e)),
+            pl.BlockSpec((1, width), lambda s, e: (0, e)),
+        ],
+        out_specs=[tokens, rows(8), rows(halo), rows(8)],
+        out_shape=[
+            jax.ShapeDtypeStruct((segs, length, inner), BF16),
+            jax.ShapeDtypeStruct((segs, 8, inner), F32),
+            jax.ShapeDtypeStruct((segs, halo, inner), F32),
+            jax.ShapeDtypeStruct((segs, 8, inner), F32),
+        ],
+        scratch_shapes=[pltpu.VMEM((length + 8, width), F32), pltpu.VMEM((length + 8, width), F32)],
+        compiler_params=pltpu.CompilerParams(vmem_limit_bytes=VMEM_BYTES),
+        cost_estimate=pl.CostEstimate(
+            flops=50 * conv_in.size, bytes_accessed=8 * conv_in.size, transcendentals=conv_in.size
+        ),
+        name="conv_back",
+    )(d_act, d_coeffs, x_proj, conv_in, before, conv_weight, conv_bias[None])
+
+
 def norm_kernel(token_ref, gain_ref, normed_ref, turned_ref):
     token = token_ref[...].astype(F32)
     inverse = lax.rsqrt(jnp.mean(token * token, axis=-1, keepdims=True) + EPS)
@@ -1129,13 +1198,13 @@
     ends, entry_mu = block_ends(delta, activated, gate_in, d_gated, b_wide, c_wide, a_mat)
     total = jnp.sum(delta, axis=1, keepdims=True)
     start, end, first = carry(ends, entry_mu, total, entry_state, a_mat)
-    start, normed_all = lax.optimization_barrier((start, normed_all))
     ones_diag = diagonal_blocks(jnp.ones((1, CHUNK, states), F32))[0, 0]
     gated, d_gate, d_pre_low, d_act, d_b, d_c, d_amat, sums, gated_all, gate_columns, d_entry = scan_both(
         delta, activated, gate_in, d_gated, b_wide, c_wide,
         diagonal_blocks(c_in), diagonal_blocks(b_in), ones_diag, a_mat, d_skip, start, end, first,
     )
     gated, d_gate, d_pre_low, d_act = flat(gated), flat(d_gate), flat(d_pre_low), flat(d_act)
+    gated_all, normed_all = lax.optimization_barrier((gated_all, normed_all))
     gated_all = gated_all.reshape(-1, inner)
     gate_columns = gate_columns.reshape(n_seq * count, -1)
     if (inner // n_seq) % LANES:
@@ -1152,21 +1221,15 @@
     d_coeffs = jnp.concatenate([d_dt_low, flat(d_b), flat(d_c)], axis=-1).astype(BF16)
     d_x_proj = matmul_tn(d_coeffs, flat(activated))
     d_a_log = jnp.sum(d_amat, axis=0) * a_mat
-    d_act = split(d_act + matmul_nt(d_coeffs, x_proj))
-    conv_sigmoid = jax.nn.sigmoid(conv_out)
-    d_conv_out = d_act * (conv_sigmoid * (1.0 + conv_out * (1.0 - conv_sigmoid)))
-    d_conv_bias = jnp.sum(d_conv_out, axis=(0, 1))
-    d_conv_weight = jnp.stack(
-        [jnp.sum(d_conv_out * padded[:, tap : tap + length], axis=(0, 1)) for tap in range(taps)]
+    d_conv_in, last, halo_grad, conv_sums = conv_back(
+        split(d_act), split(d_coeffs), x_proj, conv_in, before, conv_weight, conv_bias
     )
-    halo_grad = sum(
-        conv_weight[tap] * jnp.pad(d_conv_out[:, : halo - tap], ((0, 0), (tap, 0), (0, 0))) for tap in range(halo)
-    )
+    conv_sums = jnp.sum(conv_sums, axis=0)
+    d_conv_weight, d_conv_bias = conv_sums[:taps], conv_sums[taps]
     returned = shifted(halo_grad, "seq", -1)
-    tail = jnp.pad(d_conv_out, ((0, 0), (0, halo), (0, 0)))
-    d_conv_in = sum(conv_weight[tap] * tail[:, halo - tap : halo - tap + length] for tap in range(taps))
-    d_conv_in = d_conv_in + jnp.pad(returned, ((0, 0), (length - halo, 0), (0, 0)))
-    d_conv_in = flat(d_conv_in).astype(BF16)
+    last = last + jnp.pad(returned, ((0, 0), (last.shape[1] - halo, 0), (0, 0)))
+    d_conv_in = lax.dynamic_update_slice_in_dim(d_conv_in, last.astype(BF16), length - last.shape[1], 1)
+    d_conv_in = flat(d_conv_in)
     if fast:
         small = jnp.concatenate(
             [

time: 565 us -> 544 us (0.963)
  other arithmetic: 39.4 us -> 19 us
  Pallas kernels: 355 us -> 370 us
  local copies, waits for them, and re-layouts: 55.4 us -> 44.9 us
  matrix products: 73.1 us -> 65.6 us
    pallas_call x0 -> x1, Pallas kernels: none -> 19.5 us  [conv_back(): pl.pallas_call(conv_back_kernel, grid=(segs, inner // width), in_specs=[t...]
    convert_element_type x1 -> x0, other arithmetic: 11.8 us -> none  [body(): d_conv_in = flat(d_conv_in).astype(BF16)]
    reduce_sum x1, other arithmetic: 6.77 us -> 0.02 us  [body(): conv_sums = jnp.sum(conv_sums, axis=0)]
    pallas_call x1, Pallas kernels: 150 us -> 144 us  [scan_both(): pl.pallas_call(functools.partial(scan_kernel, hosted, inner // width, seg...]
    unnamed x64 -> x68, local copies, waits for them, and re-layouts: 27.8 us -> 22.9 us
    dot_general x3 -> x2, matrix products: 18.1 us -> 14.1 us  [matmul_nt(): lax.dot_general(left, right, (((1,), (1,)), ((), ())), preferred_element_...]
  transfers between devices with their start and end apart: 8 -> 8, of which waited for: 0 -> 0; matrix products, arithmetic and copies ran while one was open for 22% -> 18% of each run, Pallas kernels for 36% -> 69%
where the time goes in v5:
time: 544 us; the launch traced here: 535 us
  Pallas kernels  370 us (68%)
  matrix products  65.6 us (12%)
  local copies, waits for them, and re-layouts  44.9 us (8%)
  starting transfers between devices  21.2 us (4%)
  other arithmetic  19 us (3%)
  between operations  14.6 us (3%)
    pallas_call x1, Pallas kernels, scan_both(): pl.pallas_call(functools.partial(scan_kernel, hosted, inner // width, seg...  144 us
    pallas_call x1, Pallas kernels, finish(): pl.pallas_call(finish_kernel, in_specs=[anywhere] * 9 + [inside], out_spe...  133 us
    dot_general x9, matrix products, matmul(): lax.dot_general(left, right, (((1,), (0,)), ((), ())), preferred_element_...  48.2 us
    pallas_call x1, Pallas kernels, block_ends(): pl.pallas_call(ends_kernel, grid=(segs, inner // width), in_specs=[tokens...  40.4 us
    pallas_call x1, Pallas kernels, carry(): pl.pallas_call(functools.partial(carry_kernel, pieces), in_specs=[vmem] *...  30.3 us
    unnamed x68, local copies, waits for them, and re-layouts  22.9 us
    pallas_call x1, Pallas kernels, conv_back(): pl.pallas_call(conv_back_kernel, grid=(segs, inner // width), in_specs=[t...  19.5 us
    ppermute x2, starting transfers between devices, shifted(): return lax.ppermute(block, axis, route)  18.4 us
  transfers between devices with their start and end apart: 8, of which 0 were waited for; matrix products, arithmetic and copies ran while one was open for 18% of the time, Pallas kernels for 69%

profile of v5, /device:TPU:1, one launch (start us, length us, event | category | flops | bytes accessed | tf_op | source)
XLA Modules:
  0.0 535.3 jit_solution(11910423217028024581)
XLA Ops:
  8.0 1.4 copy-done.1
  9.4 2.4 norm.1
  11.9 8.9 %fusion.10 = bf16[512,3072]{1,0:T(8,128)(2,1)S(1)} fusion(bf16[512,1536]{1,0:T(8,128)(2,1)S(1)} %get-tuple-element.42, bf16[1536,6144]{1,0:T(8,128)(2,1)} %proj_hbm.1), kind=kOutput, calls=%fused_computation.16 | convolution fusion | flops 4833411072 | bytes 14155776 | tf_op jit(solution)/shard_map/dot_general | solution.py:27
  20.9 1.6 copy-done.13
  22.6 4.6 collective-permute-start
  27.2 2.3 dynamic-slice_bitcast_fusion
  34.2 10.7 %fusion.2 = f32[512,3072]{1,0:T(8,128)} fusion(bf16[512,1536]{1,0:T(8,128)(2,1)S(1)} %get-tuple-element.42, bf16[1536,6144]{1,0:T(8,128)(2,1)} %proj_hbm.1), kind=kOutput, calls=%fused_computation.3 | convolution fusion | flops 4831838208 | bytes 17301504 | tf_op jit(solution)/shard_map/dot_general | solution.py:27
  44.9 11.1 %fusion.dg_ref = f32[4,128,3072]{2,1,0:T(8,128)} fusion(bf16[4,128,1536]{2,1,0:T(8,128)(2,1)S(1)} %copy-done.16, bf16[3072,1536]{1,0:T(8,128)(2,1)} %param.26), kind=kOutput, calls=%fused_computation.1 | convolution fusion | flops 4831838208 | bytes 17301504 | tf_op jit(solution)/shard_map/dot_general | solution.py:31
  57.4 4.3 multiply_convert_fusion.act_ref
  61.7 1.6 copy-done.11
  65.6 6.6 %bitcast_reduce_fusion = (f32[4,3072]{1,0:T(4,128)S(1)}, f32[512,3072]{1,0:T(8,128)}) fusion(f32[3072]{0:T(1024)S(1)} %copy-done.29, bf16[96,3072]{1,0:T(8,128)(2,1)S(1)} %copy-done, f32[512,128]{0,1:T(8,128)S(1)} %fusion.32), kind=kOutput, calls=%fused_computation.63 | convolution fusion | flops 314560512 | bytes 7041024 | tf_op jit(solution)/shard_map/dot_general | solution.py:27
  73.5 2.6 broadcast_in_dim.43.b_ref
  76.1 2.7 broadcast_in_dim.45.c_ref
  78.8 40.4 %block_ends.1 = (f32[4,16,3072]{2,1,0:T(8,128)}, f32[4,16,3072]{2,1,0:T(8,128)}) custom-call(f32[4,128,3072]{2,1,0:T(8,128)} %bitcast.113, bf16[4,128,3072]{2,1,0:T(8,128)(2,1)} %copy-done.11, f32[4,128,3072]{2,1,0:T(8,128)} %bitcast.111, f32[4,128,3072]{2,1,0:T(8,128)} %fusion.dg_ref, f32[4,128,16,128]{3,2,1,0:T(8,128)} %broadcast_in_dim.43.b_ref, ...), custom_call_target="tpu_custom_call" | custom-call | flops 226492416 | bytes 18874368 | tf_op jit(solution)/shard_map/block_ends/pallas_call | solution.py:299
  121.4 30.3 %carry.1 = (f32[4,16,3072]{2,1,0:T(8,128)S(1)}, f32[4,16,3072]{2,1,0:T(8,128)S(1)}, f32[4,16,3072]{2,1,0:T(8,128)S(1)}) custom-call(f32[4,16,3072]{2,1,0:T(8,128)S(1)} %copy-done.5, f32[4,16,3072]{2,1,0:T(8,128)S(1)} %copy-done.6, f32[4,1,3072]{2,1,0:T(1,128)S(1)} %broadcast_in_dim.48.total_ref, f32[4,16,3072]{2,1,0:T(8,128)S(1)} %copy-done.4, ...), custom_call_target="tpu_custom_call" | custom-call | tf_op jit(solution)/shard_map/carry/pallas_call | solution.py:228
  154.4 144.3 %scan_both.1 = (bf16[4,128,3072]{2,1,0:T(8,128)(2,1)}, bf16[4,128,3072]{2,1,0:T(8,128)(2,1)}, bf16[4,128,3072]{2,1,0:T(8,128)(2,1)}, f32[4,128,3072]{2,1,0:T(8,1...) custom-call(f32[4,128,3072]{2,1,0:T(8,128)} %bitcast.114, ...), custom_call_target="tpu_custom_call" | custom-call | flops 503316480 | bytes 37748736 | tf_op jit(solution)/shard_map/scan_both/pallas_call | solution.py:632
  303.2 8.5 %convolution_convert_fusion = bf16[384,3072]{1,0:T(8,128)(2,1)S(1)} fusion(bf16[384,2048]{0,1:T(8,128)(2,1)} %copy-done.17, bf16[2048,3072]{1,0:T(8,128)(2,1)} %bitcast.110), kind=kOutput, calls=%fused_computation.17 | convolution fusion | flops 4833017856 | bytes 16515072 | tf_op jit(solution)/shard_map/dot_general | solution.py:27
  311.7 2.4 copy.55
  315.4 3.0 convolution_convert_fusion.3
  319.3 19.5 %conv_back.1 = (bf16[4,128,3072]{2,1,0:T(8,128)(2,1)}, f32[4,8,3072]{2,1,0:T(8,128)}, f32[4,3,3072]{2,1,0:T(4,128)}, f32[4,8,3072]{2,1,0:T(8,128)}) custom-call(f32[4,128,3072]{2,1,0:T(8,128)} %get-tuple-element.49.d_act_ref, bf16[4,128,128]{2,1,0:T(8,128)(2,1)} %pad_maximum_fusion.coeff_ref, bf16[3072,128]{1,0:T(8,128)(2,1)} %proj_ref.1, ...), custom_call_target="tpu_custom_call" | custom-call | flops 78643200 | bytes 12582912 | tf_op jit(solution)/shard_map/conv_back/pallas_call | solution.py:1100
  338.8 13.8 %collective-permute-start.1 = (f32[4,3,3072]{2,1,0:T(4,128)}, f32[4,3,3072]{2,1,0:T(4,128)}, u32[]{:S(2)}, u32[]{:S(2)}) collective-permute-start(f32[4,3,3072]{2,1,0:T(4,128)} %get-tuple-element.55.halo_hbm), channel_id=1, source_target_pairs={{1,0},{2,1},{3,2},{4,3},{5,4},{6,5},{7,6},{9,8},{10,9},{11,10},{12... | collective-permute-start | bytes 442376 | tf_op jit(solution)/shard_map/ppermute | solution.py:107
  353.9 2.7 convolution_convert_fusion.2
  356.6 1.6 multiply_convert_fusion.1
  358.2 9.7 %convolution_add_fusion = f32[512,1536]{1,0:T(8,128)} fusion(bf16[512,3072]{1,0:T(8,128)(2,1)S(1)} %bitcast.118, bf16[3072,1536]{1,0:T(8,128)(2,1)} %param.26, bf16[512,1536]{1,0:T(8,128)(2,1)S(1)} %bitcast.73), kind=kOutput, calls=%fused_computation.21 | convolution fusion | flops 4833411072 | bytes 17301504 | tf_op jit(solution)/shard_map/dot_general | solution.py:27
  369.0 1.7 concatenate.20
  372.1 1.7 fusion.16
  373.7 1.8 copy.56
  375.6 133.0 %finish.1 = (f32[512,1536]{1,0:T(8,128)}, bf16[1536,768]{1,0:T(8,128)(2,1)}, bf16[4,80,384]{2,1,0:T(8,128)(2,1)}, f32[4,3,3072]{2,1,0:T(4,128)}) custom-call(bf16[512,3072]{1,0:T(8,128)(2,1)} %bitcast.108, bf16[512,3072]{1,0:T(8,128)(2,1)} %bitcast.115, bf16[8,512,384]{2,1,0:T(8,128)(2,1)} %bitcast.116, bf16[8,1536,512]{2,1,0:T(8,128)(2,1)} %bitcast.107, ...), custom_call_target="tpu_custom_call" | custom-call | flops 28991029248 | bytes 31457280 | tf_op jit(solution)/shard_map/finish/pallas_call | solution.py:1011
  513.4 4.2 convert_element_type.108
  520.4 1.4 convert_bitcast_fusion
  521.9 2.0 copy.49
  523.8 3.8 copy.65
  (130 shorter events, 33.9 us)
Async XLA Ops:
  7.2 58.4 %copy-start = (bf16[96,3072]{1,0:T(8,128)(2,1)S(1)}, bf16[96,3072]{1,0:T(8,128)(2,1)}, u32[]{:S(2)}) copy-start(bf16[96,3072]{1,0:T(8,128)(2,1)} %param.22) | copy-start | bytes 1769476
  7.2 294.9 %all-gather.6.cloned.1.call-start = ((), (), s32[]{:S(2)}) async-start(), calls=%async_computation.2 | async-start | bytes 14155776 | tf_op jit(solution)/shard_map/all_gather | solution.py:1175
  8.0 12.9 %copy-start.7 = (f32[1,1536]{1,0:T(1,128)}, f32[1,1536]{1,0:T(1,128)S(1)}, u32[]{:S(2)}) copy-start(f32[1,1536]{1,0:T(1,128)S(1)} %broadcast_in_dim.41.gain_ref) | copy-start | bytes 18436
  8.0 1.4 copy-start.1
  11.9 361.9 %reduce-scatter.4.cloned.1.call-start = ((), (), s32[]{:S(2)}) async-start(), calls=%async_computation.3 | async-start | bytes 2654208
  20.9 1.7 copy-start.13
  20.9 12.6 %copy-start.25 = (f32[4,3072]{1,0:T(4,128)S(1)}, f32[4,3072]{1,0:T(4,128)}, u32[]{:S(2)}) copy-start(f32[4,3072]{1,0:T(4,128)} %weight_ref.1) | copy-start | bytes 147460
  20.9 12.6 %copy-start.20 = (f32[16,3072]{1,0:T(8,128)S(1)}, f32[16,3072]{1,0:T(8,128)}, u32[]{:S(2)}) copy-start(f32[16,3072]{1,0:T(8,128)} %param.24) | copy-start | bytes 589828
  22.6 33.7 %collective-permute-start = (bf16[4,3,3072]{2,1,0:T(4,128)(2,1)S(1)}, bf16[4,3,3072]{2,1,0:T(4,128)(2,1)S(1)}, u32[]{:S(2)}, u32[]{:S(2)}) collective-permute-start(bf16[4,3,3072]{2,1,0:T(4,128)(2,1)S(1)} %slice.123), channel_id=1, source_target_pairs={{0,1},{1,2},{2,3},{3,4},{4,5},{5,6},{6,7},{8,9},{9,10},{10,11},{11... | collective-permute-start | bytes 221192 | tf_op jit(solution)/shard_map/ppermute | solution.py:107
  29.5 269.3 %collective-permute-start.2 = (bf16[384,512]{0,1:T(8,128)(2,1)}, bf16[384,512]{0,1:T(8,128)(2,1)}, u32[]{:S(2)}, u32[]{:S(2)}) collective-permute-start(bf16[384,512]{0,1:T(8,128)(2,1)} %get-tuple-element.103), channel_id=1, source_target_pairs={{0,8},{8,0},{16,24},{24,16},{1,9},{9,1},{17,25},{25,17},{2,10},{10... | collective-permute-start | bytes 1179656 | tf_op jit(solution)/shard_map/ppermute | solution.py:73
  30.7 269.1 %collective-permute-start.3 = (bf16[384,512]{0,1:T(8,128)(2,1)}, bf16[384,512]{0,1:T(8,128)(2,1)}, u32[]{:S(2)}, u32[]{:S(2)}) collective-permute-start(bf16[384,512]{0,1:T(8,128)(2,1)} %get-tuple-element.102), channel_id=1, source_target_pairs={{0,16},{8,24},{16,0},{24,8},{1,17},{9,25},{17,1},{25,9},{2,18},{10... | collective-permute-start | bytes 1179656 | tf_op jit(solution)/shard_map/ppermute | solution.py:73
  32.0 269.0 %collective-permute-start.4 = (bf16[384,512]{0,1:T(8,128)(2,1)}, bf16[384,512]{0,1:T(8,128)(2,1)}, u32[]{:S(2)}, u32[]{:S(2)}) collective-permute-start(bf16[384,512]{0,1:T(8,128)(2,1)} %get-tuple-element.101), channel_id=1, source_target_pairs={{0,24},{8,16},{16,8},{24,0},{1,25},{9,17},{17,9},{25,1},{2,26},{10... | collective-permute-start | bytes 1179656 | tf_op jit(solution)/shard_map/ppermute | solution.py:73
  34.2 10.8 %copy-start.16 = (bf16[4,128,1536]{2,1,0:T(8,128)(2,1)S(1)}, bf16[4,128,1536]{2,1,0:T(8,128)(2,1)}, u32[]{:S(2)}) copy-start(bf16[4,128,1536]{2,1,0:T(8,128)(2,1)} %param.27) | copy-start | bytes 4718596
  44.9 11.3 %copy-start.27 = (bf16[4,3,3072]{2,0,1:T(4,128)(2,1)S(1)}, bf16[4,3,3072]{2,0,1:T(4,128)(2,1)}, u32[]{:S(2)}) copy-start(bf16[4,3,3072]{2,0,1:T(4,128)(2,1)} %param.15) | copy-start | bytes 221188
  44.9 11.4 %copy-start.14 = (bf16[512,3072]{1,0:T(8,128)(2,1)S(1)}, bf16[512,3072]{1,0:T(8,128)(2,1)}, u32[]{:S(2)}) copy-start(bf16[512,3072]{1,0:T(8,128)(2,1)} %copy-done.13) | copy-start | bytes 9437188
  57.4 5.9 %copy-start.15 = (bf16[3072,128]{1,0:T(8,128)(2,1)S(1)}, bf16[3072,128]{1,0:T(8,128)(2,1)}, u32[]{:S(2)}) copy-start(bf16[3072,128]{1,0:T(8,128)(2,1)} %proj_ref.1) | copy-start | bytes 2359300
  61.7 1.6 copy-start.11
  61.7 4.0 copy-start.29
  78.8 40.4 %copy-start.3 = (f32[16,3072]{1,0:T(8,128)S(1)}, f32[16,3072]{1,0:T(8,128)}, u32[]{:S(2)}) copy-start(f32[16,3072]{1,0:T(8,128)} %exponential_negate_fusion.a_ref) | copy-start | bytes 589828
  78.8 40.4 %copy-start.4 = (f32[4,16,3072]{2,1,0:T(8,128)S(1)}, f32[4,16,3072]{2,1,0:T(8,128)}, u32[]{:S(2)}) copy-start(f32[4,16,3072]{2,1,0:T(8,128)} %entry_ref.1) | copy-start | bytes 2359300
  119.1 1.1 copy-start.5
  120.3 1.1 copy-start.6
  302.0 1.1 copy-start.17
  311.7 3.6 copy-start.24
  314.2 206.3 %all-gather.4.cloned.1.call-start = ((), (), s32[]{:S(2)}) async-start(), calls=%async_computation.1 | async-start | bytes 1474560 | tf_op jit(solution)/shard_map/all_gather | solution.py:1215
  338.8 19.4 %copy-start.2 = (bf16[4,128,1536]{2,1,0:T(8,128)(2,1)S(1)}, bf16[4,128,1536]{2,1,0:T(8,128)(2,1)}, u32[]{:S(2)}) copy-start(bf16[4,128,1536]{2,1,0:T(8,128)(2,1)} %param.14) | copy-start | bytes 4718596
  338.8 33.2 %collective-permute-start.1 = (f32[4,3,3072]{2,1,0:T(4,128)}, f32[4,3,3072]{2,1,0:T(4,128)}, u32[]{:S(2)}, u32[]{:S(2)}) collective-permute-start(f32[4,3,3072]{2,1,0:T(4,128)} %get-tuple-element.55.halo_hbm), channel_id=1, source_target_pairs={{1,0},{2,1},{3,2},{4,3},{5,4},{6,5},{7,6},{9,8},{10,9},{11,10},{12... | collective-permute-start | bytes 442376 | tf_op jit(solution)/shard_map/ppermute | solution.py:107
  353.9 4.3 copy-start.30
  358.2 9.7 %copy-start.12 = (bf16[4,128,3072]{2,1,0:T(8,128)(2,1)S(1)}, bf16[4,128,3072]{2,1,0:T(8,128)(2,1)}, u32[]{:S(2)}) copy-start(bf16[4,128,3072]{2,1,0:T(8,128)(2,1)} %copy-done.11) | copy-start | bytes 9437188
  370.8 1.3 copy-start.21
  513.3 5.2 copy-start.26
  523.8 3.8 copy-start.19
  (7 other events, 6.9 us)
Sparse Core Ops, SparseCore 0:
  12.0 119.2 all-gather.5
  314.3 43.2 reduce-scatter.3
  375.7 43.5 all-gather.3

commit v6 on v5

--- a/solution.py
+++ b/solution.py
@@ -122,8 +122,8 @@
 
 
 def carry_kernel(
-    pieces, end_ref, mu_ref, total_ref, entry_ref, a_ref, start_ref, lam_ref, back,
-    ahead, from_left, from_right, sent_right, sent_left, got_left, got_right,
+    pieces, end_ref, mu_ref, total_ref, entry_ref, a_ref, start_ref, lam_ref, first_ref,
+    ahead, back, from_left, from_right, sent_right, sent_left, got_left, got_right,
 ):
     count, mine = lax.axis_size("seq"), lax.axis_index("seq")
     width = end_ref.shape[2] // pieces
@@ -170,7 +170,7 @@
             @pl.when(has_left)
             def _():
                 to_right(piece).wait_recv()
-                start_ref[:, :, at(piece)] = from_left[:, :, at(piece)]
+                start_ref[:, :, at(piece)] = from_left[:, :, at(piece)].astype(F32)
 
             @pl.when(jnp.logical_not(has_left))
             def _():
@@ -178,7 +178,8 @@
 
             @pl.when(has_right)
             def _():
-                ahead[:, :, at(piece)] = end_ref[:, :, at(piece)] + decay(piece) * start_ref[:, :, at(piece)]
+                end = end_ref[:, :, at(piece)] + decay(piece) * start_ref[:, :, at(piece)]
+                ahead[:, :, at(piece)] = end.astype(BF16)
                 to_right(piece).start()
 
         other = tick - (count - 1 - mine)
@@ -188,13 +189,15 @@
             @pl.when(has_right)
             def _():
                 to_left(other).wait_recv()
-                lam_ref[:, :, at(other)] = from_right[:, :, at(other)]
+                lam_ref[:, :, at(other)] = from_right[:, :, at(other)].astype(F32)
 
             @pl.when(jnp.logical_not(has_right))
             def _():
                 lam_ref[:, :, at(other)] = jnp.zeros(lam_ref.shape[:2] + (width,), F32)
 
-            back[:, :, at(other)] = mu_ref[:, :, at(other)] + decay(other) * lam_ref[:, :, at(other)]
+            first = mu_ref[:, :, at(other)] + decay(other) * lam_ref[:, :, at(other)]
+            first_ref[:, :, at(other)] = first
+            back[:, :, at(other)] = first.astype(BF16)
 
             @pl.when(has_left)
             def _():
@@ -223,14 +226,14 @@
     while ends.shape[2] % (pieces * LANES):
         pieces -= 1
     shape = jax.ShapeDtypeStruct(ends.shape, F32)
-    held = pltpu.VMEM(ends.shape, F32)
+    held = pltpu.VMEM(ends.shape, BF16)
     vmem = pl.BlockSpec(memory_space=pltpu.VMEM)
     return pl.pallas_call(
         functools.partial(carry_kernel, pieces),
         in_specs=[vmem] * 5,
         out_specs=[vmem] * 3,
         out_shape=[shape, shape, shape],
-        scratch_shapes=[held] * 3 + [pltpu.SemaphoreType.DMA((pieces,))] * 4,
+        scratch_shapes=[held] * 4 + [pltpu.SemaphoreType.DMA((pieces,))] * 4,
         compiler_params=pltpu.CompilerParams(
             collective_id=1, has_side_effects=True, vmem_limit_bytes=32 * 2**20
         ),

time: 544 us -> 538 us (0.989)
  Pallas kernels: 370 us -> 364 us
    pallas_call x1, Pallas kernels: 30.3 us -> 24.8 us  [carry(): pl.pallas_call(functools.partial(carry_kernel, pieces), in_specs=[vmem] *...]
  transfers between devices with their start and end apart: 8 -> 8, of which waited for: 0 -> 0; matrix products, arithmetic and copies ran while one was open for 18% -> 18% of each run, Pallas kernels for 69% -> 68%
where the time goes in v6:
time: 538 us; the launch traced here: 529 us
  Pallas kernels  364 us (68%)
  matrix products  65.6 us (12%)
  local copies, waits for them, and re-layouts  44.9 us (8%)
  starting transfers between devices  21.2 us (4%)
  other arithmetic  19 us (4%)
  between operations  14.6 us (3%)
    pallas_call x1, Pallas kernels, scan_both(): pl.pallas_call(functools.partial(scan_kernel, hosted, inner // width, seg...  144 us
    pallas_call x1, Pallas kernels, finish(): pl.pallas_call(finish_kernel, in_specs=[anywhere] * 9 + [inside], out_spe...  133 us
    dot_general x9, matrix products, matmul(): lax.dot_general(left, right, (((1,), (0,)), ((), ())), preferred_element_...  48.2 us
    pallas_call x1, Pallas kernels, block_ends(): pl.pallas_call(ends_kernel, grid=(segs, inner // width), in_specs=[tokens...  40.4 us
    pallas_call x1, Pallas kernels, carry(): pl.pallas_call(functools.partial(carry_kernel, pieces), in_specs=[vmem] *...  24.8 us
    unnamed x68, local copies, waits for them, and re-layouts  22.9 us
    pallas_call x1, Pallas kernels, conv_back(): pl.pallas_call(conv_back_kernel, grid=(segs, inner // width), in_specs=[t...  19.5 us
    ppermute x2, starting transfers between devices, shifted(): return lax.ppermute(block, axis, route)  18.4 us
  transfers between devices with their start and end apart: 8, of which 0 were waited for; matrix products, arithmetic and copies ran while one was open for 18% of the time, Pallas kernels for 68%

profile of v6, /device:TPU:1, one launch (start us, length us, event | category | flops | bytes accessed | tf_op | source)
XLA Modules:
  0.0 529.5 jit_solution(5143642868752537695)
XLA Ops:
  8.0 1.4 copy-done.1
  9.4 2.4 norm.1
  11.9 8.9 %fusion.10 = bf16[512,3072]{1,0:T(8,128)(2,1)S(1)} fusion(bf16[512,1536]{1,0:T(8,128)(2,1)S(1)} %get-tuple-element.42, bf16[1536,6144]{1,0:T(8,128)(2,1)} %proj_hbm.1), kind=kOutput, calls=%fused_computation.16 | convolution fusion | flops 4833411072 | bytes 14155776 | tf_op jit(solution)/shard_map/dot_general | solution.py:27
  20.9 1.6 copy-done.13
  22.6 4.6 collective-permute-start
  27.2 2.3 dynamic-slice_bitcast_fusion
  34.2 10.7 %fusion.2 = f32[512,3072]{1,0:T(8,128)} fusion(bf16[512,1536]{1,0:T(8,128)(2,1)S(1)} %get-tuple-element.42, bf16[1536,6144]{1,0:T(8,128)(2,1)} %proj_hbm.1), kind=kOutput, calls=%fused_computation.3 | convolution fusion | flops 4831838208 | bytes 17301504 | tf_op jit(solution)/shard_map/dot_general | solution.py:27
  44.9 11.1 %fusion.dg_ref = f32[4,128,3072]{2,1,0:T(8,128)} fusion(bf16[4,128,1536]{2,1,0:T(8,128)(2,1)S(1)} %copy-done.16, bf16[3072,1536]{1,0:T(8,128)(2,1)} %param.26), kind=kOutput, calls=%fused_computation.1 | convolution fusion | flops 4831838208 | bytes 17301504 | tf_op jit(solution)/shard_map/dot_general | solution.py:31
  57.4 4.3 multiply_convert_fusion.act_ref
  61.7 1.6 copy-done.11
  65.6 6.6 %bitcast_reduce_fusion = (f32[4,3072]{1,0:T(4,128)S(1)}, f32[512,3072]{1,0:T(8,128)}) fusion(f32[3072]{0:T(1024)S(1)} %copy-done.29, bf16[96,3072]{1,0:T(8,128)(2,1)S(1)} %copy-done, f32[512,128]{0,1:T(8,128)S(1)} %fusion.32), kind=kOutput, calls=%fused_computation.63 | convolution fusion | flops 314560512 | bytes 7041024 | tf_op jit(solution)/shard_map/dot_general | solution.py:27
  73.5 2.6 broadcast_in_dim.43.b_ref
  76.1 2.7 broadcast_in_dim.45.c_ref
  78.8 40.4 %block_ends.1 = (f32[4,16,3072]{2,1,0:T(8,128)}, f32[4,16,3072]{2,1,0:T(8,128)}) custom-call(f32[4,128,3072]{2,1,0:T(8,128)} %bitcast.113, bf16[4,128,3072]{2,1,0:T(8,128)(2,1)} %copy-done.11, f32[4,128,3072]{2,1,0:T(8,128)} %bitcast.111, f32[4,128,3072]{2,1,0:T(8,128)} %fusion.dg_ref, f32[4,128,16,128]{3,2,1,0:T(8,128)} %broadcast_in_dim.43.b_ref, ...), custom_call_target="tpu_custom_call" | custom-call | flops 226492416 | bytes 18874368 | tf_op jit(solution)/shard_map/block_ends/pallas_call | solution.py:302
  121.4 24.8 %carry.1 = (f32[4,16,3072]{2,1,0:T(8,128)S(1)}, f32[4,16,3072]{2,1,0:T(8,128)S(1)}, f32[4,16,3072]{2,1,0:T(8,128)S(1)}) custom-call(f32[4,16,3072]{2,1,0:T(8,128)S(1)} %copy-done.5, f32[4,16,3072]{2,1,0:T(8,128)S(1)} %copy-done.6, f32[4,1,3072]{2,1,0:T(1,128)S(1)} %broadcast_in_dim.48.total_ref, f32[4,16,3072]{2,1,0:T(8,128)S(1)} %copy-done.4, ...), custom_call_target="tpu_custom_call" | custom-call | tf_op jit(solution)/shard_map/carry/pallas_call | solution.py:231
  148.9 144.3 %scan_both.1 = (bf16[4,128,3072]{2,1,0:T(8,128)(2,1)}, bf16[4,128,3072]{2,1,0:T(8,128)(2,1)}, bf16[4,128,3072]{2,1,0:T(8,128)(2,1)}, f32[4,128,3072]{2,1,0:T(8,1...) custom-call(f32[4,128,3072]{2,1,0:T(8,128)} %bitcast.114, ...), custom_call_target="tpu_custom_call" | custom-call | flops 503316480 | bytes 37748736 | tf_op jit(solution)/shard_map/scan_both/pallas_call | solution.py:635
  297.6 8.5 %convolution_convert_fusion = bf16[384,3072]{1,0:T(8,128)(2,1)S(1)} fusion(bf16[384,2048]{0,1:T(8,128)(2,1)} %copy-done.17, bf16[2048,3072]{1,0:T(8,128)(2,1)} %bitcast.110), kind=kOutput, calls=%fused_computation.17 | convolution fusion | flops 4833017856 | bytes 16515072 | tf_op jit(solution)/shard_map/dot_general | solution.py:27
  306.1 2.4 copy.55
  309.8 3.0 convolution_convert_fusion.3
  313.7 19.5 %conv_back.1 = (bf16[4,128,3072]{2,1,0:T(8,128)(2,1)}, f32[4,8,3072]{2,1,0:T(8,128)}, f32[4,3,3072]{2,1,0:T(4,128)}, f32[4,8,3072]{2,1,0:T(8,128)}) custom-call(f32[4,128,3072]{2,1,0:T(8,128)} %get-tuple-element.49.d_act_ref, bf16[4,128,128]{2,1,0:T(8,128)(2,1)} %pad_maximum_fusion.coeff_ref, bf16[3072,128]{1,0:T(8,128)(2,1)} %proj_ref.1, ...), custom_call_target="tpu_custom_call" | custom-call | flops 78643200 | bytes 12582912 | tf_op jit(solution)/shard_map/conv_back/pallas_call | solution.py:1103
  333.2 13.8 %collective-permute-start.1 = (f32[4,3,3072]{2,1,0:T(4,128)}, f32[4,3,3072]{2,1,0:T(4,128)}, u32[]{:S(2)}, u32[]{:S(2)}) collective-permute-start(f32[4,3,3072]{2,1,0:T(4,128)} %get-tuple-element.55.halo_hbm), channel_id=1, source_target_pairs={{1,0},{2,1},{3,2},{4,3},{5,4},{6,5},{7,6},{9,8},{10,9},{11,10},{12... | collective-permute-start | bytes 442376 | tf_op jit(solution)/shard_map/ppermute | solution.py:107
  348.3 2.7 convolution_convert_fusion.2
  351.0 1.6 multiply_convert_fusion.1
  352.6 9.7 %convolution_add_fusion = f32[512,1536]{1,0:T(8,128)} fusion(bf16[512,3072]{1,0:T(8,128)(2,1)S(1)} %bitcast.118, bf16[3072,1536]{1,0:T(8,128)(2,1)} %param.26, bf16[512,1536]{1,0:T(8,128)(2,1)S(1)} %bitcast.73), kind=kOutput, calls=%fused_computation.21 | convolution fusion | flops 4833411072 | bytes 17301504 | tf_op jit(solution)/shard_map/dot_general | solution.py:27
  363.5 1.7 concatenate.20
  366.5 1.7 fusion.16
  368.2 1.8 copy.56
  370.0 132.7 %finish.1 = (f32[512,1536]{1,0:T(8,128)}, bf16[1536,768]{1,0:T(8,128)(2,1)}, bf16[4,80,384]{2,1,0:T(8,128)(2,1)}, f32[4,3,3072]{2,1,0:T(4,128)}) custom-call(bf16[512,3072]{1,0:T(8,128)(2,1)} %bitcast.108, bf16[512,3072]{1,0:T(8,128)(2,1)} %bitcast.115, bf16[8,512,384]{2,1,0:T(8,128)(2,1)} %bitcast.116, bf16[8,1536,512]{2,1,0:T(8,128)(2,1)} %bitcast.107, ...), custom_call_target="tpu_custom_call" | custom-call | flops 28991029248 | bytes 31457280 | tf_op jit(solution)/shard_map/finish/pallas_call | solution.py:1014
  507.5 4.2 convert_element_type.108
  514.6 1.4 convert_bitcast_fusion
  516.0 2.0 copy.49
  518.0 3.8 copy.65
  (130 shorter events, 33.9 us)
Async XLA Ops:
  7.2 58.4 %copy-start = (bf16[96,3072]{1,0:T(8,128)(2,1)S(1)}, bf16[96,3072]{1,0:T(8,128)(2,1)}, u32[]{:S(2)}) copy-start(bf16[96,3072]{1,0:T(8,128)(2,1)} %param.22) | copy-start | bytes 1769476
  7.2 289.3 %all-gather.6.cloned.1.call-start = ((), (), s32[]{:S(2)}) async-start(), calls=%async_computation.2 | async-start | bytes 14155776 | tf_op jit(solution)/shard_map/all_gather | solution.py:1178
  8.0 12.9 %copy-start.7 = (f32[1,1536]{1,0:T(1,128)}, f32[1,1536]{1,0:T(1,128)S(1)}, u32[]{:S(2)}) copy-start(f32[1,1536]{1,0:T(1,128)S(1)} %broadcast_in_dim.41.gain_ref) | copy-start | bytes 18436
  8.0 1.4 copy-start.1
  11.9 356.3 %reduce-scatter.4.cloned.1.call-start = ((), (), s32[]{:S(2)}) async-start(), calls=%async_computation.3 | async-start | bytes 2654208
  20.9 1.7 copy-start.13
  20.9 12.6 %copy-start.25 = (f32[4,3072]{1,0:T(4,128)S(1)}, f32[4,3072]{1,0:T(4,128)}, u32[]{:S(2)}) copy-start(f32[4,3072]{1,0:T(4,128)} %weight_ref.1) | copy-start | bytes 147460
  20.9 12.6 %copy-start.20 = (f32[16,3072]{1,0:T(8,128)S(1)}, f32[16,3072]{1,0:T(8,128)}, u32[]{:S(2)}) copy-start(f32[16,3072]{1,0:T(8,128)} %param.24) | copy-start | bytes 589828
  22.6 33.7 %collective-permute-start = (bf16[4,3,3072]{2,1,0:T(4,128)(2,1)S(1)}, bf16[4,3,3072]{2,1,0:T(4,128)(2,1)S(1)}, u32[]{:S(2)}, u32[]{:S(2)}) collective-permute-start(bf16[4,3,3072]{2,1,0:T(4,128)(2,1)S(1)} %slice.123), channel_id=1, source_target_pairs={{0,1},{1,2},{2,3},{3,4},{4,5},{5,6},{6,7},{8,9},{9,10},{10,11},{11... | collective-permute-start | bytes 221192 | tf_op jit(solution)/shard_map/ppermute | solution.py:107
  29.5 263.7 %collective-permute-start.2 = (bf16[384,512]{0,1:T(8,128)(2,1)}, bf16[384,512]{0,1:T(8,128)(2,1)}, u32[]{:S(2)}, u32[]{:S(2)}) collective-permute-start(bf16[384,512]{0,1:T(8,128)(2,1)} %get-tuple-element.103), channel_id=1, source_target_pairs={{0,8},{8,0},{16,24},{24,16},{1,9},{9,1},{17,25},{25,17},{2,10},{10... | collective-permute-start | bytes 1179656 | tf_op jit(solution)/shard_map/ppermute | solution.py:73
  30.7 263.6 %collective-permute-start.3 = (bf16[384,512]{0,1:T(8,128)(2,1)}, bf16[384,512]{0,1:T(8,128)(2,1)}, u32[]{:S(2)}, u32[]{:S(2)}) collective-permute-start(bf16[384,512]{0,1:T(8,128)(2,1)} %get-tuple-element.102), channel_id=1, source_target_pairs={{0,16},{8,24},{16,0},{24,8},{1,17},{9,25},{17,1},{25,9},{2,18},{10... | collective-permute-start | bytes 1179656 | tf_op jit(solution)/shard_map/ppermute | solution.py:73
  32.0 263.4 %collective-permute-start.4 = (bf16[384,512]{0,1:T(8,128)(2,1)}, bf16[384,512]{0,1:T(8,128)(2,1)}, u32[]{:S(2)}, u32[]{:S(2)}) collective-permute-start(bf16[384,512]{0,1:T(8,128)(2,1)} %get-tuple-element.101), channel_id=1, source_target_pairs={{0,24},{8,16},{16,8},{24,0},{1,25},{9,17},{17,9},{25,1},{2,26},{10... | collective-permute-start | bytes 1179656 | tf_op jit(solution)/shard_map/ppermute | solution.py:73
  34.2 10.8 %copy-start.16 = (bf16[4,128,1536]{2,1,0:T(8,128)(2,1)S(1)}, bf16[4,128,1536]{2,1,0:T(8,128)(2,1)}, u32[]{:S(2)}) copy-start(bf16[4,128,1536]{2,1,0:T(8,128)(2,1)} %param.27) | copy-start | bytes 4718596
  44.9 11.3 %copy-start.27 = (bf16[4,3,3072]{2,0,1:T(4,128)(2,1)S(1)}, bf16[4,3,3072]{2,0,1:T(4,128)(2,1)}, u32[]{:S(2)}) copy-start(bf16[4,3,3072]{2,0,1:T(4,128)(2,1)} %param.15) | copy-start | bytes 221188
  44.9 11.4 %copy-start.14 = (bf16[512,3072]{1,0:T(8,128)(2,1)S(1)}, bf16[512,3072]{1,0:T(8,128)(2,1)}, u32[]{:S(2)}) copy-start(bf16[512,3072]{1,0:T(8,128)(2,1)} %copy-done.13) | copy-start | bytes 9437188
  57.4 5.9 %copy-start.15 = (bf16[3072,128]{1,0:T(8,128)(2,1)S(1)}, bf16[3072,128]{1,0:T(8,128)(2,1)}, u32[]{:S(2)}) copy-start(bf16[3072,128]{1,0:T(8,128)(2,1)} %proj_ref.1) | copy-start | bytes 2359300
  61.7 1.6 copy-start.11
  61.7 4.0 copy-start.29
  78.8 40.4 %copy-start.3 = (f32[16,3072]{1,0:T(8,128)S(1)}, f32[16,3072]{1,0:T(8,128)}, u32[]{:S(2)}) copy-start(f32[16,3072]{1,0:T(8,128)} %exponential_negate_fusion.a_ref) | copy-start | bytes 589828
  78.8 40.4 %copy-start.4 = (f32[4,16,3072]{2,1,0:T(8,128)S(1)}, f32[4,16,3072]{2,1,0:T(8,128)}, u32[]{:S(2)}) copy-start(f32[4,16,3072]{2,1,0:T(8,128)} %entry_ref.1) | copy-start | bytes 2359300
  119.1 1.1 copy-start.5
  120.3 1.1 copy-start.6
  296.4 1.1 copy-start.17
  306.1 3.6 copy-start.24
  308.6 206.0 %all-gather.4.cloned.1.call-start = ((), (), s32[]{:S(2)}) async-start(), calls=%async_computation.1 | async-start | bytes 1474560 | tf_op jit(solution)/shard_map/all_gather | solution.py:1218
  333.2 19.4 %copy-start.2 = (bf16[4,128,1536]{2,1,0:T(8,128)(2,1)S(1)}, bf16[4,128,1536]{2,1,0:T(8,128)(2,1)}, u32[]{:S(2)}) copy-start(bf16[4,128,1536]{2,1,0:T(8,128)(2,1)} %param.14) | copy-start | bytes 4718596
  333.2 33.2 %collective-permute-start.1 = (f32[4,3,3072]{2,1,0:T(4,128)}, f32[4,3,3072]{2,1,0:T(4,128)}, u32[]{:S(2)}, u32[]{:S(2)}) collective-permute-start(f32[4,3,3072]{2,1,0:T(4,128)} %get-tuple-element.55.halo_hbm), channel_id=1, source_target_pairs={{1,0},{2,1},{3,2},{4,3},{5,4},{6,5},{7,6},{9,8},{10,9},{11,10},{12... | collective-permute-start | bytes 442376 | tf_op jit(solution)/shard_map/ppermute | solution.py:107
  348.3 4.3 copy-start.30
  352.6 9.7 %copy-start.12 = (bf16[4,128,3072]{2,1,0:T(8,128)(2,1)S(1)}, bf16[4,128,3072]{2,1,0:T(8,128)(2,1)}, u32[]{:S(2)}) copy-start(bf16[4,128,3072]{2,1,0:T(8,128)(2,1)} %copy-done.11) | copy-start | bytes 9437188
  365.2 1.3 copy-start.21
  507.5 5.2 copy-start.26
  518.0 3.8 copy-start.19
  (7 other events, 6.9 us)
Sparse Core Ops, SparseCore 0:
  12.0 119.2 all-gather.5
  308.7 43.2 reduce-scatter.3
  370.2 43.5 all-gather.3
